TPU v7x, 32 devices: a whole 2x2x4 slice. The times are simulated.
32 devices in a mesh: row: 8 (over y, x, core), col: 4 (over z).
Axes of the slice: x: 2, y: 2, z: 4, core: 2. Of those that a mesh axis runs over, the one named last changes fastest.
Arguments:
- parent_inverse: float32 [24576, 24576], P('row', 'col'), may hold values from -6 to 6
- panel: float32 [24576, 1024], P(('col', 'row')), may hold values from -0.0390625 to 0.0390625
- saved_diag: float32 [1024, 1024], P('row', 'col'), may hold values from -6 to 6
Outputs:
- offdiag_block: float32 [24576, 1024], P(('row', 'col'))
- diag_block: float32 [1024, 1024], P('row', 'col')
All inputs are finite; a program needn't handle non-finite values.
Results may differ from a plain program's by a relative error of at most 0.00007.
Values sent between devices are 32-bit elements; how exact they have to be, the bound alone decides.
No kernel may reach another device: no remote copies, remote signals or barrier semaphores. Data moves between devices by JAX's collectives and lax.ppermute only.
A program may use at most 192 MiB of HBM per device.

v0:
```python
import jax
import jax.numpy as jnp
from jax import lax
from jax.sharding import PartitionSpec as P


def spread(block, axis, holder):
    block = jnp.where(lax.axis_index(axis) == holder, block, jnp.zeros_like(block))
    return lax.psum(block, axis)


def shards(parent_inverse, panel, saved_diag):
    block_rows = parent_inverse.shape[0]
    column_count = lax.axis_size("col")
    keep_rows = block_rows // column_count
    column_panel = lax.all_gather(panel, "row", axis=0, tiled=True)
    row_index = lax.axis_index("row")
    column_index = lax.axis_index("col")
    local_half = lax.dynamic_slice_in_dim(column_panel, row_index % 2 * block_rows, block_rows, 0)
    product = lax.psum_scatter(
        jnp.dot(
            parent_inverse,
            column_panel,
            precision=lax.Precision.HIGHEST,
            preferred_element_type=jnp.float32,
        ),
        "col",
        scatter_dimension=0,
        tiled=True,
    )
    panel_half = spread(local_half, "col", row_index // 2)
    own_rows = lax.dynamic_slice_in_dim(panel_half, column_index * keep_rows, keep_rows, 0)
    offdiag_block = -product
    partial_value = lax.dot_general(
        own_rows,
        product,
        (((0,), (0,)), ((), ())),
        precision=lax.Precision.HIGHEST,
        preferred_element_type=jnp.float32,
    )
    by_columns = lax.psum_scatter(partial_value, "col", scatter_dimension=1, tiled=True)
    summed = lax.psum_scatter(by_columns, "row", scatter_dimension=0, tiled=True)
    diag_block = saved_diag + summed
    return (offdiag_block, diag_block)


def solution(mesh):
    in_specs = (P("row", "col"), P(("col", "row"), None), P("row", "col"))
    out_specs = (P(("row", "col"), None), P("row", "col"))
    return jax.shard_map(shards, mesh=mesh, in_specs=in_specs, out_specs=out_specs, check_vma=False)
```

profile of v0, /device:TPU:0, one launch (start us, length us, event | category | flops | bytes accessed | tf_op | source)
XLA Modules:
  0.0 929.5 jit_solution(15885233374946585713)
XLA Ops:
  7.2 0.0 all-gather.2.cloned.1.call-start
  7.2 0.7 all-gather.2.cloned.1.call-update
  7.9 0.0 all-reduce.2.cloned.1.call-start
  8.0 130.0 %all-gather.2.cloned.1.call-done = f32[6144,1024]{1,0:T(8,128)} async-done(((f32[768,1024]{1,0:T(8,128)}), f32[6144,1024]{1,0:T(8,128)}) %all-gather.2.cloned.1.call-update) | async-done | bytes 25165840 | tf_op jit(solution)/shard_map/all_gather | solution.py:16
  137.9 12.0 %dynamic-slice_select_fusion = f32[3072,1024]{1,0:T(8,128)} fusion(f32[6144,1024]{1,0:T(8,128)} %all-gather.2.cloned.1.call-done, s32[]{:T(128)S(6)} %select_n.28, pred[]{:T(512)S(6)} %eq.5), kind=kLoop, calls=%fused_computation | loop fusion | flops 3145728 | bytes 25165828 | tf_op jit(solution)/shard_map/jit(_where)/select_n | solution.py:8
  150.0 0.0 all-reduce.2.cloned.1.call-update
  150.0 0.0 reduce-scatter.4.cloned.1.call-start
  150.0 252.7 %fusion.3 = f32[3072,1024]{1,0:T(8,128)} fusion(f32[3072,6144]{1,0:T(8,128)} %param.3, f32[6144,1024]{1,0:T(8,128)} %all-gather.2.cloned.1.call-done), kind=kOutput, calls=%fused_computation.4 | convolution fusion | flops 231928233984 | bytes 113246208 | tf_op jit(solution)/shard_map/dot_general | solution.py:21
  402.8 0.0 reduce-scatter.4.cloned.1.call-update
  402.8 0.2 reduce-scatter.6.cloned.1.call-start
  403.0 0.0 copy-start.1
  403.0 173.2 %all-reduce.2.cloned.1.call-done = f32[3072,1024]{1,0:T(8,128)} async-done(((f32[3072,1024]{1,0:T(8,128)}), f32[3072,1024]{1,0:T(8,128)}) %all-reduce.2.cloned.1.call-update) | async-done | bytes 12582928 | tf_op jit(solution)/shard_map/psum | solution.py:9
  576.2 213.2 %reduce-scatter.4.cloned.1.call-done = f32[768,1024]{1,0:T(8,128)} async-done(((f32[3072,1024]{1,0:T(8,128)}), f32[768,1024]{1,0:T(8,128)}) %reduce-scatter.4.cloned.1.call-update) | async-done | bytes 3145744 | tf_op jit(solution)/shard_map/reduce_scatter | solution.py:20
  789.4 0.0 copy-start
  789.4 14.0 %fusion = f32[1024,1024]{1,0:T(8,128)} fusion(f32[768,1024]{1,0:T(8,128)} %reduce-scatter.4.cloned.1.call-done, f32[3072,1024]{1,0:T(8,128)} %all-reduce.2.cloned.1.call-done, s32[]{:T(128)S(6)} %select_n.30), kind=kOutput, calls=%fused_computation.1 | convolution fusion | flops 9663676416 | bytes 10485764 | tf_op jit(solution)/shard_map/dot_general | solution.py:34
  803.5 0.0 reduce-scatter.6.cloned.1.call-update
  803.5 0.0 reduce-scatter.8.cloned.1.call-start
  803.5 77.9 %reduce-scatter.6.cloned.1.call-done = f32[1024,256]{1,0:T(8,128)} async-done(((f32[1024,1024]{1,0:T(8,128)}), f32[1024,256]{1,0:T(8,128)}) %reduce-scatter.6.cloned.1.call-update) | async-done | bytes 1048592 | tf_op jit(solution)/shard_map/reduce_scatter | solution.py:41
  881.5 0.0 reduce-scatter.8.cloned.1.call-update
  881.5 0.0 copy-done
  881.5 2.0 neg.3
  883.5 37.9 %reduce-scatter.8.cloned.1.call-done = f32[128,256]{1,0:T(8,128)} async-done(((f32[1024,256]{1,0:T(8,128)}), f32[128,256]{1,0:T(8,128)}) %reduce-scatter.8.cloned.1.call-update) | async-done | bytes 131088 | tf_op jit(solution)/shard_map/reduce_scatter | solution.py:42
  921.4 0.0 copy-done.1
  921.4 1.6 add.25
Async XLA Ops:
  7.2 130.8 %all-gather.2.cloned.1.call-start = ((), (), s32[]{:S(2)}) async-start(), calls=%async_computation.3 | async-start | bytes 28311552 | tf_op jit(solution)/shard_map/all_gather | solution.py:16
  7.9 568.3 %all-reduce.2.cloned.1.call-start = ((), (), s32[]{:S(2)}) async-start(), calls=%async_computation.5 | async-start | bytes 25165824 | tf_op jit(solution)/shard_map/psum | solution.py:9
  150.0 639.5 %reduce-scatter.4.cloned.1.call-start = ((), (), s32[]{:S(2)}) async-start(), calls=%async_computation.4 | async-start | bytes 15728640 | tf_op jit(solution)/shard_map/reduce_scatter | solution.py:20
  402.8 478.7 %reduce-scatter.6.cloned.1.call-start = ((), (), s32[]{:S(2)}) async-start(), calls=%async_computation.6 | async-start | bytes 5242880 | tf_op jit(solution)/shard_map/reduce_scatter | solution.py:41
  403.0 518.4 %copy-start.1 = (f32[128,256]{1,0:T(8,128)S(1)}, f32[128,256]{1,0:T(8,128)}, u32[]{:S(2)}) copy-start(f32[128,256]{1,0:T(8,128)} %param.5) | copy-start | bytes 393220
  789.4 92.0 %copy-start = (f32[768,1024]{1,0:T(8,128)S(1)}, f32[768,1024]{1,0:T(8,128)}, u32[]{:S(2)}) copy-start(f32[768,1024]{1,0:T(8,128)} %reduce-scatter.4.cloned.1.call-done) | copy-start | bytes 9437188
  803.5 117.9 %reduce-scatter.8.cloned.1.call-start = ((), (), s32[]{:S(2)}) async-start(), calls=%async_computation.7 | async-start | bytes 1179648 | tf_op jit(solution)/shard_map/reduce_scatter | solution.py:42
Sparse Core Ops, SparseCore 0:
  9.9 128.0 all-gather.1
  150.1 426.0 all-reduce.1
  578.6 210.7 reduce-scatter.3
  803.6 77.7 reduce-scatter.5
  884.8 36.5 reduce-scatter.7
where the time goes:
time: 930 us
  waiting for transfers between devices  633 us (68%)
  matrix products  267 us (29%)
  other arithmetic  15.6 us (2%)
  between operations  13.8 us (1%)
    dot_general x1, matrix products, shards(): jnp.dot(parent_inverse, column_panel, precision=lax.Precision.HIGHEST, pr...  253 us
    reduce_scatter x1, waiting for transfers between devices, shards(): lax.psum_scatter(jnp.dot(parent_inverse, column_panel, precision=lax.Prec...  213 us
    psum x1, waiting for transfers between devices, spread(): return lax.psum(block, axis)  173 us
    all_gather x1, waiting for transfers between devices, shards(): column_panel = lax.all_gather(panel, 'row', axis=0, tiled=True)  130 us
    reduce_scatter x1, waiting for transfers between devices, shards(): lax.psum_scatter(partial_value, 'col', scatter_dimension=1, tiled=True)  77.9 us
    reduce_scatter x1, waiting for transfers between devices, shards(): lax.psum_scatter(by_columns, 'row', scatter_dimension=0, tiled=True)  37.9 us
  transfers between devices with their start and end apart: 5, of which 5 were waited for; matrix products, arithmetic and copies ran while one was open for 27% of the time, Pallas kernels for 0%

commit v1 on v0

v1 whole, which is shorter than its diff:
```python
import functools

import jax
import jax.numpy as jnp
import numpy as np
from jax import lax
from jax.experimental import pallas as pl
from jax.experimental.pallas import tpu as pltpu
from jax.sharding import PartitionSpec as P

CHUNKS = 4
PARTS = 2
MIB = 1 << 20


def split(value):
    high = value.astype(jnp.bfloat16)
    low = (value - high.astype(jnp.float32)).astype(jnp.bfloat16)
    return high, low


def largest_divisor(extent, unit, limit):
    return max(d for d in range(unit, min(extent, limit) + 1, unit) if extent % d == 0)


def product_kernel(depth, block, place_ref, a_ref, *refs):
    pieces, (out_ref, high_ref, low_ref) = refs[:-3], refs[-3:]

    @pl.when(pl.program_id(0) == 0)
    def _():
        slot = 0
        for piece in pieces:
            for part in range(piece.shape[0] // block):
                high, low = split(piece[pl.ds(part * block, block), :])
                rows = pl.ds(pl.multiple_of(place_ref[slot] * block, block), block)
                high_ref[rows, :] = high
                low_ref[rows, :] = low
                slot += 1

    dot = functools.partial(jnp.dot, preferred_element_type=jnp.float32)

    def term(index):
        span = pl.ds(pl.multiple_of(index * depth, depth), depth)
        a_high, a_low = split(-a_ref[:, span])
        b_high, b_low = high_ref[span, :], low_ref[span, :]
        return dot(a_high, b_high) + (dot(a_low, b_high) + dot(a_high, b_low))

    def body(index, carry):
        out_ref[...] += term(index)
        return carry

    out_ref[...] = term(0)
    lax.fori_loop(1, a_ref.shape[1] // depth, body, 0)


def negative_product(a, pieces, place, tile, part):
    rows, inner = a.shape
    columns = pieces[0].shape[1]
    block = inner // place.shape[0]
    depth = largest_divisor(inner, 256, 1024)
    whole = [pl.BlockSpec(piece.shape, lambda i, _: (0, 0), pipeline_mode=pl.Buffered(1)) for piece in pieces]
    rows //= PARTS
    return pl.pallas_call(
        functools.partial(product_kernel, depth, block),
        grid_spec=pltpu.PrefetchScalarGridSpec(
            num_scalar_prefetch=1,
            grid=(rows // tile,),
            in_specs=[pl.BlockSpec((tile, inner), lambda i, _: (i * PARTS + part, 0))] + whole,
            out_specs=pl.BlockSpec((tile, columns), lambda i, _: (i, 0)),
            scratch_shapes=[pltpu.VMEM((inner, columns), jnp.bfloat16)] * 2,
        ),
        out_shape=jax.ShapeDtypeStruct((rows, columns), jnp.float32),
        compiler_params=pltpu.CompilerParams(vmem_limit_bytes=40 * MIB, dimension_semantics=("arbitrary",)),
        cost_estimate=pl.CostEstimate(
            flops=6 * rows * inner * columns,
            bytes_accessed=4 * (rows * inner + inner * columns + rows * columns),
            transcendentals=0,
        ),
    )(place, a, *pieces)


def gather_orders(count):
    masks = [1 << b for b in range(1, count.bit_length() - 1)]
    return masks, masks[::-1]


def gather_places(count):
    orders = gather_orders(count)
    held = [[i] for i in range(count)]
    for step in range(len(orders[0])):
        held = [held[i] + held[i ^ orders[i & 1][step]] for i in range(count)]
    return np.array([held[i] + held[i ^ 1] for i in range(count)], np.int32)


def after(value, *others):
    return lax.optimization_barrier((value, *others))[0]


def cross(pieces, masks, count):
    pairs = [(i, i ^ masks[i & 1]) for i in range(count)]
    return [lax.ppermute(piece, "row", pairs) for piece in pieces]


def sum_over_row(value, count):
    rows, columns = value.shape
    me = lax.axis_index("row")
    value = value.reshape((2,) * (count.bit_length() - 1) + (rows // count, columns))
    for bit in range(count.bit_length() - 1):
        axis = value.ndim - 3
        mine = (me >> bit) & 1
        keep = lax.dynamic_index_in_dim(value, mine, axis, keepdims=False)
        send = lax.dynamic_index_in_dim(value, 1 - mine, axis, keepdims=False)
        value = keep + lax.ppermute(send, "row", [(i, i ^ (1 << bit)) for i in range(count)])
    return value


def sum_over_col(value, count):
    me = lax.axis_index("col")
    width = value.shape[1] // count
    total = lax.dynamic_slice_in_dim(value, me * width, width, 1)
    for shift in range(1, count):
        send = lax.dynamic_slice_in_dim(value, (me + shift) % count * width, width, 1)
        total = total + lax.ppermute(send, "col", [(i, (i + shift) % count) for i in range(count)])
    return total


def shards(parent_inverse, panel, saved_diag):
    row_count, column_count = lax.axis_size("row"), lax.axis_size("col")
    width = panel.shape[1] // CHUNKS
    tile = parent_inverse.shape[0] // column_count // PARTS
    place = jnp.asarray(gather_places(row_count))[lax.axis_index("row")]
    steps = list(zip(*gather_orders(row_count))) + [(1, 1)]
    pairs = [
        (r * column_count + c, c * row_count + r) for r in range(row_count) for c in range(column_count)
    ]

    def gather_step(pieces, step, last):
        return pieces + cross([after(pieces[0], last)] + pieces[1:], steps[step], row_count)

    pieces = [lax.slice_in_dim(panel, 0, width, axis=1)]
    for step in range(len(steps)):
        pieces = pieces + cross(pieces, steps[step], row_count)
    own_rows = lax.ppermute(after(panel, pieces[-1]), ("row", "col"), pairs)
    partials = []
    for chunk in range(CHUNKS):
        following = [lax.slice_in_dim(panel, (chunk + 1) * width, (chunk + 2) * width, axis=1)] if chunk + 1 < CHUNKS else []
        last = pieces[-1]
        for part in range(PARTS):
            if chunk + 1 < CHUNKS:
                for step in range(part * (len(steps) - 1) // PARTS, (part + 1) * (len(steps) - 1) // PARTS):
                    following = gather_step(following, step, last)
            last = negative_product(after(parent_inverse, last), pieces, place, tile, part)
            partials.append(last)
        if chunk + 1 < CHUNKS:
            following = gather_step(following, len(steps) - 1, last)
        pieces = following
    blocks, grams = [], []
    for chunk in range(CHUNKS):
        halves = [
            lax.psum_scatter(partials[chunk * PARTS + part], "col", scatter_dimension=0, tiled=True)
            for part in range(PARTS)
        ]
        block = jnp.concatenate(halves, axis=0)
        gram = lax.dot_general(
            own_rows,
            after(block, partials[min(PARTS * CHUNKS, (chunk + 3) * PARTS) - 1]),
            (((0,), (0,)), ((), ())),
            precision=lax.Precision.HIGH,
            preferred_element_type=jnp.float32,
        )
        blocks.append(block)
        grams.append(sum_over_row(gram, row_count))
    offdiag_block = jnp.concatenate(blocks, axis=1)
    diag_block = saved_diag - sum_over_col(jnp.concatenate(grams, axis=1), column_count)
    return offdiag_block, diag_block


def solution(mesh):
    in_specs = (P("row", "col"), P(("col", "row"), None), P("row", "col"))
    out_specs = (P(("row", "col"), None), P("row", "col"))
    return jax.shard_map(shards, mesh=mesh, in_specs=in_specs, out_specs=out_specs, check_vma=False)
```

time: 930 us -> 591 us (0.64)
  waiting for transfers between devices: 633 us -> 119 us
  matrix products: 267 us -> 18.6 us
  Pallas kernels: 0 us -> 199 us
  starting transfers between devices: 0.38 us -> 182 us
  local copies, waits for them, and re-layouts: 0.01 us -> 49.7 us
  other arithmetic: 15.6 us -> 5.66 us
    reduce_scatter x3 -> x8, waiting for transfers between devices: 329 us -> 5.74 us  [shards(): lax.psum_scatter(partials[chunk * PARTS + part], 'col', scatter_dimension...]
    dot_general x2 -> x4, matrix products: 267 us -> 18.6 us  [shards(): lax.dot_general(own_rows, after(block, partials[min(PARTS * CHUNKS, (chun...]
    pallas_call x0 -> x8, Pallas kernels: none -> 199 us  [negative_product(): pl.pallas_call(functools.partial(product_kernel, depth, block), grid_spec...]
    ppermute x0 -> x44, starting transfers between devices: none -> 181 us  [the longest x12 133 us: sum_over_row(): lax.ppermute(send, 'row', [(i, i ^ 1 << bit) for i in range(count)])]
    psum x1 -> x0, waiting for transfers between devices: 173 us -> none  [spread(): return lax.psum(block, axis)]
    all_gather x1 -> x0, waiting for transfers between devices: 130 us -> none  [shards(): column_panel = lax.all_gather(panel, 'row', axis=0, tiled=True)]
    ppermute x0 -> x44, waiting for transfers between devices: none -> 113 us  [the longest x28 90.2 us: cross(): return [lax.ppermute(piece, 'row', pairs) for piece in pieces]]
    unnamed x4 -> x86, local copies, waits for them, and re-layouts: 0.01 us -> 39.4 us
  transfers between devices with their start and end apart: 5 -> 52, of which waited for: 5 -> 21; matrix products, arithmetic and copies ran while one was open for 27% -> 6% of each run, Pallas kernels for 0% -> 29%
where the time goes in v1:
time: 591 us; the launch traced here: 588 us
  Pallas kernels  199 us (34%)
  starting transfers between devices  182 us (31%)
  waiting for transfers between devices  119 us (20%)
  local copies, waits for them, and re-layouts  49.7 us (8%)
  matrix products  18.6 us (3%)
  between operations  14.7 us (2%)
    pallas_call x8, Pallas kernels, negative_product(): pl.pallas_call(functools.partial(product_kernel, depth, block), grid_spec...  199 us
    ppermute x12, starting transfers between devices, sum_over_row(): lax.ppermute(send, 'row', [(i, i ^ 1 << bit) for i in range(count)])  133 us
    ppermute x28, waiting for transfers between devices, cross(): return [lax.ppermute(piece, 'row', pairs) for piece in pieces]  90.2 us
    unnamed x86, local copies, waits for them, and re-layouts  39.4 us
    ppermute x1, starting transfers between devices, shards(): own_rows = lax.ppermute(after(panel, pieces[-1]), ('row', 'col'), pairs)  25 us
    ppermute x28, starting transfers between devices, cross(): return [lax.ppermute(piece, 'row', pairs) for piece in pieces]  19 us
    dot_general x4, matrix products, shards(): lax.dot_general(own_rows, after(block, partials[min(PARTS * CHUNKS, (chun...  18.6 us
    ppermute x12, waiting for transfers between devices, sum_over_row(): lax.ppermute(send, 'row', [(i, i ^ 1 << bit) for i in range(count)])  17.5 us
  transfers between devices with their start and end apart: 52, of which 21 were waited for; matrix products, arithmetic and copies ran while one was open for 6% of the time, Pallas kernels for 29%

profile of v1, /device:TPU:0, one launch (start us, length us, event | category | flops | bytes accessed | tf_op | source)
XLA Modules:
  0.0 588.1 jit_solution(12582253438699403185)
XLA Ops:
  12.3 10.1 %collective-permute-done.refs_1_ = f32[768,256]{1,0:T(8,128)} collective-permute-done((f32[768,256]{1,0:T(8,128)S(1)}, f32[768,256]{1,0:T(8,128)}, u32[]{:S(2)}, u32[]{:S(2)}) %collective-permute-start) | collective-permute-done | bytes 786464 | tf_op jit(solution)/shard_map/ppermute | solution.py:101
  24.4 10.2 %collective-permute-done.1.refs_3_ = f32[768,256]{1,0:T(8,128)} collective-permute-done((f32[768,256]{1,0:T(8,128)}, f32[768,256]{1,0:T(8,128)}, u32[]{:S(2)}, u32[]{:S(2)}) %collective-permute-start.1) | collective-permute-done | bytes 786464 | tf_op jit(solution)/shard_map/ppermute | solution.py:101
  35.2 7.9 %collective-permute-done.3.refs_2_ = f32[768,256]{1,0:T(8,128)} collective-permute-done((f32[768,256]{1,0:T(8,128)S(1)}, f32[768,256]{1,0:T(8,128)}, u32[]{:S(2)}, u32[]{:S(2)}) %collective-permute-start.3) | collective-permute-done | bytes 786464 | tf_op jit(solution)/shard_map/ppermute | solution.py:101
  45.7 25.5 %shard_map.59 = f32[1536,256]{1,0:T(8,128)S(1)} custom-call(s32[8]{0:T(128)S(1)} %fusion.place_ref, f32[3072,6144]{1,0:T(8,128)} %a_ref.7, f32[768,256]{1,0:T(8,128)S(1)} %get-tuple-element.46.refs_0_, f32[768,256]{1,0:T(8,128)} %collective-permute-done.refs_1_, f32[768,256]{1,0:T(8,128)} %collective-permute-done.3.refs_2_, ...), custom_call_target="tpu_custom_call" | custom-call | flops 14495514624 | bytes 45613056 | tf_op jit(solution)/shard_map/pallas_call | solution.py:63
  74.6 25.6 %shard_map.60 = f32[1536,256]{1,0:T(8,128)S(1)} custom-call(s32[8]{0:T(128)S(1)} %fusion.place_ref, f32[3072,6144]{1,0:T(8,128)} %a_ref.7, f32[768,256]{1,0:T(8,128)S(1)} %get-tuple-element.46.refs_0_, f32[768,256]{1,0:T(8,128)} %collective-permute-done.refs_1_, f32[768,256]{1,0:T(8,128)} %collective-permute-done.3.refs_2_, ...), custom_call_target="tpu_custom_call" | custom-call | flops 14495514624 | bytes 45613056 | tf_op jit(solution)/shard_map/pallas_call | solution.py:63
  103.5 10.2 %collective-permute-done.8.refs_3_ = f32[768,256]{1,0:T(8,128)S(1)} collective-permute-done((f32[768,256]{1,0:T(8,128)}, f32[768,256]{1,0:T(8,128)S(1)}, u32[]{:S(2)}, u32[]{:S(2)}) %collective-permute-start.8) | collective-permute-done | bytes 786464 | tf_op jit(solution)/shard_map/ppermute | solution.py:101
  114.2 7.9 %collective-permute-done.10.refs_2_ = f32[768,256]{1,0:T(8,128)S(1)} collective-permute-done((f32[768,256]{1,0:T(8,128)S(1)}, f32[768,256]{1,0:T(8,128)S(1)}, u32[]{:S(2)}, u32[]{:S(2)}) %collective-permute-start.10) | collective-permute-done | bytes 786464 | tf_op jit(solution)/shard_map/ppermute | solution.py:101
  125.7 24.2 %shard_map.61 = f32[1536,256]{1,0:T(8,128)S(1)} custom-call(s32[8]{0:T(128)S(1)} %fusion.place_ref, f32[3072,6144]{1,0:T(8,128)} %a_ref.7, f32[768,256]{1,0:T(8,128)S(1)} %get-tuple-element.29.refs_0_, f32[768,256]{1,0:T(8,128)} %collective-permute-done.7.refs_1_, f32[768,256]{1,0:T(8,128)S(1)} %collective-permute-done.10.refs_2_, ...), custom_call_target="tpu_custom_call" | custom-call | flops 14495514624 | bytes 45613056 | tf_op jit(solution)/shard_map/pallas_call | solution.py:63
  163.7 24.1 %shard_map.62 = f32[1536,256]{1,0:T(8,128)S(1)} custom-call(s32[8]{0:T(128)S(1)} %fusion.place_ref, f32[3072,6144]{1,0:T(8,128)} %a_ref.7, f32[768,256]{1,0:T(8,128)S(1)} %get-tuple-element.29.refs_0_, f32[768,256]{1,0:T(8,128)} %collective-permute-done.7.refs_1_, f32[768,256]{1,0:T(8,128)S(1)} %copy-done.19, f32[768,256]{1,0:T(8,128)S(1)} %copy-done.15, ...), custom_call_target="tpu_custom_call" | custom-call | flops 14495514624 | bytes 45613056 | tf_op jit(solution)/shard_map/pallas_call | solution.py:63
  191.4 10.0 %collective-permute-done.15.refs_3_ = f32[768,256]{1,0:T(8,128)S(1)} collective-permute-done((f32[768,256]{1,0:T(8,128)S(1)}, f32[768,256]{1,0:T(8,128)S(1)}, u32[]{:S(2)}, u32[]{:S(2)}) %collective-permute-start.15) | collective-permute-done | bytes 786464 | tf_op jit(solution)/shard_map/ppermute | solution.py:101
  201.9 7.9 %collective-permute-done.17.refs_2_ = f32[768,256]{1,0:T(8,128)S(1)} collective-permute-done((f32[768,256]{1,0:T(8,128)S(1)}, f32[768,256]{1,0:T(8,128)S(1)}, u32[]{:S(2)}, u32[]{:S(2)}) %collective-permute-start.17) | collective-permute-done | bytes 786464 | tf_op jit(solution)/shard_map/ppermute | solution.py:101
  213.3 24.9 %shard_map.63 = f32[1536,256]{1,0:T(8,128)} custom-call(s32[8]{0:T(128)S(1)} %fusion.place_ref, f32[3072,6144]{1,0:T(8,128)} %a_ref.7, f32[768,256]{1,0:T(8,128)S(1)} %get-tuple-element.34.refs_0_, f32[768,256]{1,0:T(8,128)S(1)} %collective-permute-done.14.refs_1_, f32[768,256]{1,0:T(8,128)S(1)} %collective-permute-done.17.refs_2_, ...), custom_call_target="tpu_custom_call" | custom-call | flops 14495514624 | bytes 45613056 | tf_op jit(solution)/shard_map/pallas_call | solution.py:63
  252.2 24.8 %shard_map.64 = f32[1536,256]{1,0:T(8,128)} custom-call(s32[8]{0:T(128)S(1)} %fusion.place_ref, f32[3072,6144]{1,0:T(8,128)} %a_ref.7, f32[768,256]{1,0:T(8,128)S(1)} %get-tuple-element.34.refs_0_, f32[768,256]{1,0:T(8,128)S(1)} %collective-permute-done.14.refs_1_, f32[768,256]{1,0:T(8,128)S(1)} %copy-done.17, f32[768,256]{1,0:T(8,128)S(1)} %copy-done.13, ...), custom_call_target="tpu_custom_call" | custom-call | flops 14495514624 | bytes 45613056 | tf_op jit(solution)/shard_map/pallas_call | solution.py:63
  279.2 10.0 %collective-permute-done.22.refs_3_ = f32[768,256]{1,0:T(8,128)S(1)} collective-permute-done((f32[768,256]{1,0:T(8,128)S(1)}, f32[768,256]{1,0:T(8,128)S(1)}, u32[]{:S(2)}, u32[]{:S(2)}) %collective-permute-start.22) | collective-permute-done | bytes 786464 | tf_op jit(solution)/shard_map/ppermute | solution.py:101
  289.6 7.9 %collective-permute-done.24.refs_2_ = f32[768,256]{1,0:T(8,128)S(1)} collective-permute-done((f32[768,256]{1,0:T(8,128)S(1)}, f32[768,256]{1,0:T(8,128)S(1)}, u32[]{:S(2)}, u32[]{:S(2)}) %collective-permute-start.24) | collective-permute-done | bytes 786464 | tf_op jit(solution)/shard_map/ppermute | solution.py:101
  298.1 25.0 %collective-permute-start.28 = (f32[768,1024]{1,0:T(8,128)}, f32[768,1024]{1,0:T(8,128)}, u32[]{:S(2)}, u32[]{:S(2)}) collective-permute-start(f32[768,1024]{1,0:T(8,128)} %param.5), channel_id=1, source_target_pairs={{0,0},{1,8},{2,16},{3,24},{4,1},{5,9},{6,17},{7,25},{8,2},{9,10},{... | collective-permute-start | bytes 9437192 | tf_op jit(solution)/shard_map/ppermute | solution.py:143
  323.1 24.8 %shard_map.65 = f32[1536,256]{1,0:T(8,128)} custom-call(s32[8]{0:T(128)S(1)} %fusion.place_ref, f32[3072,6144]{1,0:T(8,128)} %a_ref.7, f32[768,256]{1,0:T(8,128)S(1)} %get-tuple-element.39.refs_0_, f32[768,256]{1,0:T(8,128)S(1)} %collective-permute-done.21.refs_1_, f32[768,256]{1,0:T(8,128)S(1)} %collective-permute-done.24.refs_2_, ...), custom_call_target="tpu_custom_call" | custom-call | flops 14495514624 | bytes 45613056 | tf_op jit(solution)/shard_map/pallas_call | solution.py:63
  355.2 4.9 fusion.2
  361.9 25.0 %shard_map.66 = f32[1536,256]{1,0:T(8,128)} custom-call(s32[8]{0:T(128)S(1)} %fusion.place_ref, f32[3072,6144]{1,0:T(8,128)} %a_ref.7, f32[768,256]{1,0:T(8,128)S(1)} %get-tuple-element.39.refs_0_, f32[768,256]{1,0:T(8,128)S(1)} %collective-permute-done.21.refs_1_, f32[768,256]{1,0:T(8,128)S(1)} %collective-permute-done.24.refs_2_, ...), custom_call_target="tpu_custom_call" | custom-call | flops 14495514624 | bytes 45613056 | tf_op jit(solution)/shard_map/pallas_call | solution.py:63
  388.2 30.5 %collective-permute-start.30 = (f32[2,128,256]{2,1,0:T(8,128)S(1)}, f32[2,128,256]{2,1,0:T(8,128)S(1)}, u32[]{:S(2)}, u32[]{:S(2)}) collective-permute-start(f32[2,128,256]{2,1,0:T(8,128)S(1)} %dynamic-slice_bitcast_fusion.7), channel_id=1, source_target_pairs={{0,8},{4,12},{8,0},{12,4},{16,24},{20,28},{24,16},{28,20},{1,9},{5... | collective-permute-start | bytes 786440 | tf_op jit(solution)/shard_map/ppermute | solution.py:113
  426.2 93.1 %collective-permute-start.31 = (f32[128,256]{1,0:T(8,128)S(1)}, f32[128,256]{1,0:T(8,128)S(1)}, u32[]{:S(2)}, u32[]{:S(2)}) collective-permute-start(f32[128,256]{1,0:T(8,128)S(1)} %dynamic-slice_bitcast_fusion.11), channel_id=1, source_target_pairs={{0,16},{4,20},{8,24},{12,28},{16,0},{20,4},{24,8},{28,12},{1,17},{... | collective-permute-start | bytes 393224 | tf_op jit(solution)/shard_map/ppermute | solution.py:113
  536.2 5.7 reduce-scatter.23.cloned.1.call-done
  542.9 4.6 fusion.5
  551.3 6.8 %collective-permute-done.36 = f32[2,128,256]{2,1,0:T(8,128)S(1)} collective-permute-done((f32[2,128,256]{2,1,0:T(8,128)S(1)}, f32[2,128,256]{2,1,0:T(8,128)S(1)}, u32[]{:S(2)}, u32[]{:S(2)}) %collective-permute-start.36) | collective-permute-done | bytes 262176 | tf_op jit(solution)/shard_map/ppermute | solution.py:113
  (220 shorter events, 121.8 us)
Async XLA Ops:
  7.2 344.4 %reduce-scatter.9.cloned.1.call-start = ((), (), s32[]{:S(2)}) async-start(), calls=%async_computation.8 | async-start | bytes 1966080 | tf_op jit(solution)/shard_map/reduce_scatter | solution.py:160
  24.4 18.7 %collective-permute-start.3 = (f32[768,256]{1,0:T(8,128)S(1)}, f32[768,256]{1,0:T(8,128)}, u32[]{:S(2)}, u32[]{:S(2)}) collective-permute-start(f32[768,256]{1,0:T(8,128)S(1)} %get-tuple-element.46.refs_0_), channel_id=1, source_target_pairs={{0,16},{4,12},{8,24},{12,4},{16,0},{20,28},{24,8},{28,20},{1,17},{... | collective-permute-start | bytes 2359304 | tf_op jit(solution)/shard_map/ppermute | solution.py:101
  72.5 280.9 %reduce-scatter.11.cloned.1.call-start = ((), (), s32[]{:S(2)}) async-start(), calls=%async_computation.9 | async-start | bytes 1966080 | tf_op jit(solution)/shard_map/reduce_scatter | solution.py:160
  72.5 28.9 %collective-permute-start.7 = (f32[768,256]{1,0:T(8,128)S(1)}, f32[768,256]{1,0:T(8,128)}, u32[]{:S(2)}, u32[]{:S(2)}) collective-permute-start(f32[768,256]{1,0:T(8,128)S(1)} %get-tuple-element.29.refs_0_), channel_id=1, source_target_pairs={{0,8},{4,20},{8,0},{12,28},{16,24},{20,4},{24,16},{28,12},{1,9},{5... | collective-permute-start | bytes 2359304 | tf_op jit(solution)/shard_map/ppermute | solution.py:101
  101.3 317.3 %reduce-scatter.13.cloned.1.call-start = ((), (), s32[]{:S(2)}) async-start(), calls=%async_computation.10 | async-start | bytes 1966080 | tf_op jit(solution)/shard_map/reduce_scatter | solution.py:160
  103.0 19.1 %collective-permute-start.10 = (f32[768,256]{1,0:T(8,128)S(1)}, f32[768,256]{1,0:T(8,128)S(1)}, u32[]{:S(2)}, u32[]{:S(2)}) collective-permute-start(f32[768,256]{1,0:T(8,128)S(1)} %get-tuple-element.29.refs_0_), channel_id=1, source_target_pairs={{0,16},{4,12},{8,24},{12,4},{16,0},{20,28},{24,8},{28,20},{1,17},{... | collective-permute-start | bytes 2359304 | tf_op jit(solution)/shard_map/ppermute | solution.py:101
  156.5 263.2 %reduce-scatter.15.cloned.1.call-start = ((), (), s32[]{:S(2)}) async-start(), calls=%async_computation.11 | async-start | bytes 1966080 | tf_op jit(solution)/shard_map/reduce_scatter | solution.py:160
  156.6 32.7 %collective-permute-start.14 = (f32[768,256]{1,0:T(8,128)S(1)}, f32[768,256]{1,0:T(8,128)S(1)}, u32[]{:S(2)}, u32[]{:S(2)}) collective-permute-start(f32[768,256]{1,0:T(8,128)S(1)} %get-tuple-element.34.refs_0_), channel_id=1, source_target_pairs={{0,8},{4,20},{8,0},{12,28},{16,24},{20,4},{24,16},{28,12},{1,9},{5... | collective-permute-start | bytes 2359304 | tf_op jit(solution)/shard_map/ppermute | solution.py:101
  189.1 335.8 %reduce-scatter.17.cloned.1.call-start = ((), (), s32[]{:S(2)}) async-start(), calls=%async_computation.12 | async-start | bytes 1966080 | tf_op jit(solution)/shard_map/reduce_scatter | solution.py:160
  191.2 18.6 %collective-permute-start.17 = (f32[768,256]{1,0:T(8,128)S(1)}, f32[768,256]{1,0:T(8,128)S(1)}, u32[]{:S(2)}, u32[]{:S(2)}) collective-permute-start(f32[768,256]{1,0:T(8,128)S(1)} %get-tuple-element.34.refs_0_), channel_id=1, source_target_pairs={{0,16},{4,12},{8,24},{12,4},{16,0},{20,28},{24,8},{28,20},{1,17},{... | collective-permute-start | bytes 2359304 | tf_op jit(solution)/shard_map/ppermute | solution.py:101
  243.6 282.3 %reduce-scatter.19.cloned.1.call-start = ((), (), s32[]{:S(2)}) async-start(), calls=%async_computation.13 | async-start | bytes 1966080 | tf_op jit(solution)/shard_map/reduce_scatter | solution.py:160
  243.7 33.4 %collective-permute-start.21 = (f32[768,256]{1,0:T(8,128)S(1)}, f32[768,256]{1,0:T(8,128)S(1)}, u32[]{:S(2)}, u32[]{:S(2)}) collective-permute-start(f32[768,256]{1,0:T(8,128)S(1)} %get-tuple-element.39.refs_0_), channel_id=1, source_target_pairs={{0,8},{4,20},{8,0},{12,28},{16,24},{20,4},{24,16},{28,12},{1,9},{5... | collective-permute-start | bytes 2359304 | tf_op jit(solution)/shard_map/ppermute | solution.py:101
  277.0 258.2 %reduce-scatter.21.cloned.1.call-start = ((), (), s32[]{:S(2)}) async-start(), calls=%async_computation.14 | async-start | bytes 1966080 | tf_op jit(solution)/shard_map/reduce_scatter | solution.py:160
  278.7 18.9 %collective-permute-start.24 = (f32[768,256]{1,0:T(8,128)S(1)}, f32[768,256]{1,0:T(8,128)S(1)}, u32[]{:S(2)}, u32[]{:S(2)}) collective-permute-start(f32[768,256]{1,0:T(8,128)S(1)} %get-tuple-element.39.refs_0_), channel_id=1, source_target_pairs={{0,16},{4,12},{8,24},{12,4},{16,0},{20,28},{24,8},{28,20},{1,17},{... | collective-permute-start | bytes 2359304 | tf_op jit(solution)/shard_map/ppermute | solution.py:101
  289.1 34.0 %collective-permute-start.23 = (f32[768,256]{1,0:T(8,128)S(1)}, f32[768,256]{1,0:T(8,128)S(1)}, u32[]{:S(2)}, u32[]{:S(2)}) collective-permute-start(f32[768,256]{1,0:T(8,128)S(1)} %collective-permute-done.22.refs_3_), channel_id=1, source_target_pairs={{0,4},{4,0},{8,12},{12,8},{16,20},{20,16},{24,28},{28,24},{1,5},{5... | collective-permute-start | bytes 2359304 | tf_op jit(solution)/shard_map/ppermute | solution.py:101
  289.1 34.0 %collective-permute-start.25 = (f32[768,256]{1,0:T(8,128)S(1)}, f32[768,256]{1,0:T(8,128)S(1)}, u32[]{:S(2)}, u32[]{:S(2)}) collective-permute-start(f32[768,256]{1,0:T(8,128)S(1)} %get-tuple-element.39.refs_0_), channel_id=1, source_target_pairs={{0,4},{4,0},{8,12},{12,8},{16,20},{20,16},{24,28},{28,24},{1,5},{5... | collective-permute-start | bytes 2359304 | tf_op jit(solution)/shard_map/ppermute | solution.py:101
  297.5 25.6 %collective-permute-start.27 = (f32[768,256]{1,0:T(8,128)S(1)}, f32[768,256]{1,0:T(8,128)S(1)}, u32[]{:S(2)}, u32[]{:S(2)}) collective-permute-start(f32[768,256]{1,0:T(8,128)S(1)} %collective-permute-done.24.refs_2_), channel_id=1, source_target_pairs={{0,4},{4,0},{8,12},{12,8},{16,20},{20,16},{24,28},{28,24},{1,5},{5... | collective-permute-start | bytes 2359304 | tf_op jit(solution)/shard_map/ppermute | solution.py:101
  297.5 25.6 %collective-permute-start.26 = (f32[768,256]{1,0:T(8,128)S(1)}, f32[768,256]{1,0:T(8,128)S(1)}, u32[]{:S(2)}, u32[]{:S(2)}) collective-permute-start(f32[768,256]{1,0:T(8,128)S(1)} %collective-permute-done.21.refs_1_), channel_id=1, source_target_pairs={{0,4},{4,0},{8,12},{12,8},{16,20},{20,16},{24,28},{28,24},{1,5},{5... | collective-permute-start | bytes 2359304 | tf_op jit(solution)/shard_map/ppermute | solution.py:101
  298.1 57.1 %collective-permute-start.28 = (f32[768,1024]{1,0:T(8,128)}, f32[768,1024]{1,0:T(8,128)}, u32[]{:S(2)}, u32[]{:S(2)}) collective-permute-start(f32[768,1024]{1,0:T(8,128)} %param.5), channel_id=1, source_target_pairs={{0,0},{1,8},{2,16},{3,24},{4,1},{5,9},{6,17},{7,25},{8,2},{9,10},{... | collective-permute-start | bytes 9437192 | tf_op jit(solution)/shard_map/ppermute | solution.py:143
  351.5 190.4 %reduce-scatter.23.cloned.1.call-start = ((), (), s32[]{:S(2)}) async-start(), calls=%async_computation.15 | async-start | bytes 1966080 | tf_op jit(solution)/shard_map/reduce_scatter | solution.py:160
  361.9 25.1 %collective-permute-start.29 = (f32[2,2,128,256]{3,2,1,0:T(8,128)}, f32[2,2,128,256]{3,2,1,0:T(8,128)}, u32[]{:S(2)}, u32[]{:S(2)}) collective-permute-start(f32[2,2,128,256]{3,2,1,0:T(8,128)} %dynamic-slice_bitcast_fusion.3), channel_id=1, source_target_pairs={{0,4},{4,0},{8,12},{12,8},{16,20},{20,16},{24,28},{28,24},{1,5},{5... | collective-permute-start | bytes 1572872 | tf_op jit(solution)/shard_map/ppermute | solution.py:113
  388.2 37.9 %collective-permute-start.30 = (f32[2,128,256]{2,1,0:T(8,128)S(1)}, f32[2,128,256]{2,1,0:T(8,128)S(1)}, u32[]{:S(2)}, u32[]{:S(2)}) collective-permute-start(f32[2,128,256]{2,1,0:T(8,128)S(1)} %dynamic-slice_bitcast_fusion.7), channel_id=1, source_target_pairs={{0,8},{4,12},{8,0},{12,4},{16,24},{20,28},{24,16},{28,20},{1,9},{5... | collective-permute-start | bytes 786440 | tf_op jit(solution)/shard_map/ppermute | solution.py:113
  426.2 96.6 %collective-permute-start.32 = (f32[2,2,128,256]{3,2,1,0:T(8,128)}, f32[2,2,128,256]{3,2,1,0:T(8,128)S(1)}, u32[]{:S(2)}, u32[]{:S(2)}) collective-permute-start(f32[2,2,128,256]{3,2,1,0:T(8,128)} %dynamic-slice_bitcast_fusion.2), channel_id=1, source_target_pairs={{0,4},{4,0},{8,12},{12,8},{16,20},{20,16},{24,28},{28,24},{1,5},{5... | collective-permute-start | bytes 1572872 | tf_op jit(solution)/shard_map/ppermute | solution.py:113
  426.2 96.5 %collective-permute-start.31 = (f32[128,256]{1,0:T(8,128)S(1)}, f32[128,256]{1,0:T(8,128)S(1)}, u32[]{:S(2)}, u32[]{:S(2)}) collective-permute-start(f32[128,256]{1,0:T(8,128)S(1)} %dynamic-slice_bitcast_fusion.11), channel_id=1, source_target_pairs={{0,16},{4,20},{8,24},{12,28},{16,0},{20,4},{24,8},{28,12},{1,17},{... | collective-permute-start | bytes 393224 | tf_op jit(solution)/shard_map/ppermute | solution.py:113
  (69 other events, 344.9 us)
Sparse Core Ops, SparseCore 0:
  72.6 37.0 reduce-scatter.8
  112.0 34.2 reduce-scatter.10
  156.6 35.5 reduce-scatter.12
  194.4 34.2 reduce-scatter.14
  243.7 36.7 reduce-scatter.16
  282.6 43.8 reduce-scatter.18
  351.6 81.4 reduce-scatter.20
  435.5 106.3 reduce-scatter.22

commit v2 on v1

v2 whole, which is shorter than its diff:
```python
import functools

import jax
import jax.numpy as jnp
import numpy as np
from jax import lax
from jax.experimental import pallas as pl
from jax.experimental.pallas import tpu as pltpu
from jax.sharding import PartitionSpec as P

CHUNKS = 4
LANES = 128
MIB = 1 << 20


def split(value):
    high = value.astype(jnp.bfloat16)
    low = (value - high.astype(jnp.float32)).astype(jnp.bfloat16)
    return high, low


def largest_divisor(extent, unit, limit):
    return max(d for d in range(unit, min(extent, limit) + 1, unit) if extent % d == 0)


def product_kernel(count, place_ref, a_ref, *refs):
    del place_ref
    pieces, sums, (out_ref, high_ref, low_ref) = refs[:count], refs[count:-3], refs[-3:]
    step = pl.program_id(1)

    for slot, piece in enumerate(pieces):

        @pl.when((pl.program_id(0) == 0) & (step == slot))
        def _():
            high_ref[slot], low_ref[slot] = split(-piece[...])

    @pl.when(step == 0)
    def _():
        out_ref[...] = sums[0][...] if sums else jnp.zeros_like(out_ref)

    dot = functools.partial(jnp.dot, preferred_element_type=jnp.float32)
    extent = largest_divisor(a_ref.shape[0], 16, 256)
    for first in range(0, a_ref.shape[0], extent):
        rows = pl.ds(first, extent)
        high, low = split(a_ref[rows, :])
        both = dot(jnp.concatenate([high, low], axis=0), high_ref[step])
        out_ref[rows, :] += both[:extent] + (both[extent:] + dot(high, low_ref[step]))


def negative_product(a, pieces, place, sums=None):
    rows = a.shape[0]
    depth, columns = pieces[0].shape
    tile = largest_divisor(rows, 16, 768)
    out_spec = pl.BlockSpec((tile, columns), lambda i, k, _: (i, 0))
    whole = [pl.BlockSpec(piece.shape, lambda i, k, _: (0, 0), pipeline_mode=pl.Buffered(1)) for piece in pieces]
    given = [] if sums is None else [sums]
    return pl.pallas_call(
        functools.partial(product_kernel, len(pieces)),
        grid_spec=pltpu.PrefetchScalarGridSpec(
            num_scalar_prefetch=1,
            grid=(rows // tile, len(pieces)),
            in_specs=[pl.BlockSpec((tile, depth), lambda i, k, place: (i, place[k]))] + whole + [out_spec] * len(given),
            out_specs=out_spec,
            scratch_shapes=[pltpu.VMEM((len(pieces), depth, columns), jnp.bfloat16)] * 2,
        ),
        out_shape=jax.ShapeDtypeStruct((rows, columns), jnp.float32),
        compiler_params=pltpu.CompilerParams(
            vmem_limit_bytes=40 * MIB, dimension_semantics=("arbitrary", "arbitrary")
        ),
        cost_estimate=pl.CostEstimate(
            flops=6 * rows * depth * len(pieces) * columns,
            bytes_accessed=4 * (rows * depth * len(pieces) + depth * len(pieces) * columns + 2 * rows * columns),
            transcendentals=0,
        ),
    )(place, a, *pieces, *given)


def gather_orders(count):
    masks = [1 << b for b in range(1, count.bit_length() - 1)]
    return list(zip(masks, masks[::-1]))


def gather_places(count):
    held = [[i] for i in range(count)]
    for masks in gather_orders(count):
        held = [held[i] + held[i ^ masks[i & 1]] for i in range(count)]
    half = count // 4
    both = [
        held[i][:half] + held[i ^ 1][:half] + held[i][half:] + held[i ^ 1][half:] for i in range(count)
    ]
    return np.array(both, np.int32)


def after(value, *others):
    return lax.optimization_barrier((value, *others))[0]


def cross(pieces, masks, count):
    pairs = [(i, i ^ masks[i & 1]) for i in range(count)]
    return [lax.ppermute(piece, "row", pairs) for piece in pieces]


def sum_over_row(value, count):
    rows, columns = value.shape
    me = lax.axis_index("row")
    value = value.reshape((2,) * (count.bit_length() - 1) + (rows // count, columns))
    for bit in range(count.bit_length() - 1):
        axis = value.ndim - 3
        mine = (me >> bit) & 1
        keep = lax.dynamic_index_in_dim(value, mine, axis, keepdims=False)
        send = lax.dynamic_index_in_dim(value, 1 - mine, axis, keepdims=False)
        value = keep + lax.ppermute(send, "row", [(i, i ^ (1 << bit)) for i in range(count)])
    return value


def sum_over_col(value, count):
    me = lax.axis_index("col")
    width = value.shape[1] // count
    total = lax.dynamic_slice_in_dim(value, me * width, width, 1)
    for shift in range(1, count):
        send = lax.dynamic_slice_in_dim(value, (me + shift) % count * width, width, 1)
        total = total + lax.ppermute(send, "col", [(i, (i + shift) % count) for i in range(count)])
    return total


def move(value, target):
    row_count, column_count = lax.axis_size("row"), lax.axis_size("col")
    pairs = []
    for r in range(row_count):
        for c in range(column_count):
            to_row, to_column = target(r, c)
            pairs.append((r * column_count + c, to_row * column_count + to_column))
    return lax.ppermute(value, ("row", "col"), pairs)


def shards(parent_inverse, panel, saved_diag):
    row_count, column_count = lax.axis_size("row"), lax.axis_size("col")
    row_index, column_index = lax.axis_index("row"), lax.axis_index("col")
    group = row_count // column_count
    block_rows = panel.shape[0]
    width = panel.shape[1] // CHUNKS
    stepwise = block_rows % LANES == 0
    orders = gather_orders(row_count)
    places = gather_places(row_count)
    place = jnp.asarray(places)[row_index]
    slots = jnp.asarray(np.argsort(places, axis=1).astype(np.int32))[row_index]

    def cut(chunk):
        return lax.slice_in_dim(panel, chunk * width, (chunk + 1) * width, axis=1)

    def partner(pieces):
        return cross(pieces, (1, 1), row_count)

    def early(chunk, last):
        pieces = [cut(chunk) if last is None else after(cut(chunk), last)]
        for masks in orders[:-1]:
            pieces = pieces + cross(pieces, masks, row_count)
        return pieces, pieces + partner(pieces)

    def spread(chunk, select):
        wanted = row_index % group * column_count + (column_index ^ (row_index // group) ^ (chunk % column_count))
        return move(select(wanted), lambda r, c: (r, c ^ (r // group) ^ (chunk % column_count)))

    def hop(value, chunk):
        return move(
            value, lambda r, c: (((r // group) ^ c ^ (chunk % column_count)) * group + r % group, c)
        )

    blocks, own_rows = [], []

    def held_back(chunk):
        return after(parent_inverse, blocks[chunk - 2]) if chunk >= 2 else parent_inverse

    def summed(partial_block):
        return lax.psum_scatter(partial_block, "col", scatter_dimension=0, tiled=True)

    waiting = None
    last = None
    if stepwise:
        half = row_count // 2
        following = early(0, None)
        for chunk in range(CHUNKS):
            mine, first = following
            others = cross([mine[0] if last is None else after(mine[0], last)] + mine[1:], orders[-1], row_count)
            last = negative_product(held_back(chunk), first, place[:half])
            second = others + partner(others)
            if chunk + 1 < CHUNKS:
                following = early(chunk + 1, last)
            if waiting is not None:
                own_rows.append(hop(waiting, chunk - 1))
                waiting = None
            waiting = spread(chunk, lambda wanted: lax.select_n(slots[wanted], *first, *second))
            last = negative_product(parent_inverse, second, place[half:], last)
            blocks.append(summed(last))
        own_rows.append(hop(waiting, CHUNKS - 1))
    else:
        for chunk in range(CHUNKS):
            whole = lax.all_gather(cut(chunk), "row", axis=0, tiled=True)
            waiting = spread(
                chunk, lambda wanted: lax.dynamic_slice_in_dim(whole, wanted * block_rows, block_rows, 0)
            )
            own_rows.append(hop(waiting, chunk))
            last = negative_product(held_back(chunk), [whole], jnp.zeros((1,), jnp.int32))
            blocks.append(summed(last))
    own_rows = jnp.concatenate(own_rows, axis=1)
    grams = []
    for block in blocks:
        gram = lax.dot_general(
            own_rows,
            after(block, last),
            (((0,), (0,)), ((), ())),
            precision=lax.Precision.HIGH,
            preferred_element_type=jnp.float32,
        )
        grams.append(sum_over_row(gram, row_count))
    offdiag_block = jnp.concatenate(blocks, axis=1)
    diag_block = saved_diag - sum_over_col(jnp.concatenate(grams, axis=1), column_count)
    return offdiag_block, diag_block


def solution(mesh):
    in_specs = (P("row", "col"), P(("col", "row"), None), P("row", "col"))
    out_specs = (P(("row", "col"), None), P("row", "col"))
    return jax.shard_map(shards, mesh=mesh, in_specs=in_specs, out_specs=out_specs, check_vma=False)
```

time: 591 us -> 621 us (1.051)
  waiting for transfers between devices: 119 us -> 222 us
  starting transfers between devices: 182 us -> 102 us
  local copies, waits for them, and re-layouts: 49.7 us -> 17.5 us
  between operations: 14.7 us -> 32.4 us
  other arithmetic: 5.66 us -> 18.9 us
  Pallas kernels: 199 us -> 210 us
    ppermute x12, starting transfers between devices: 133 us -> 9.44 us  [sum_over_row(): lax.ppermute(send, 'row', [(i, i ^ 1 << bit) for i in range(count)])]
    ppermute x1 -> x8, waiting for transfers between devices: 0.01 us -> 78.3 us  [move(): return lax.ppermute(value, ('row', 'col'), pairs)]
    ppermute x1 -> x8, starting transfers between devices: 25 us -> 68.3 us  [move(): return lax.ppermute(value, ('row', 'col'), pairs)]
    unnamed x86 -> x47, local copies, waits for them, and re-layouts: 39.4 us -> 10.2 us
    ppermute x28, waiting for transfers between devices: 90.2 us -> 113 us  [cross(): return [lax.ppermute(piece, 'row', pairs) for piece in pieces]]
    pallas_call x8, Pallas kernels: 199 us -> 210 us  [negative_product(): pl.pallas_call(functools.partial(product_kernel, len(pieces)), grid_spec=...]
    select_n x0 -> x4, other arithmetic: none -> 11.2 us  [shards(): lax.select_n(slots[wanted], *first, *second)]
    ppermute x12, waiting for transfers between devices: 17.5 us -> 24.6 us  [sum_over_row(): lax.ppermute(send, 'row', [(i, i ^ 1 << bit) for i in range(count)])]
  transfers between devices with their start and end apart: 52 -> 55, of which waited for: 21 -> 19; matrix products, arithmetic and copies ran while one was open for 6% -> 7% of each run, Pallas kernels for 29% -> 30%
where the time goes in v2:
time: 621 us; the launch traced here: 616 us
  waiting for transfers between devices  222 us (36%)
  Pallas kernels  210 us (34%)
  starting transfers between devices  102 us (16%)
  between operations  32.4 us (5%)
  other arithmetic  18.9 us (3%)
  local copies, waits for them, and re-layouts  17.5 us (3%)
  matrix products  13 us (2%)
    pallas_call x8, Pallas kernels, negative_product(): pl.pallas_call(functools.partial(product_kernel, len(pieces)), grid_spec=...  210 us
    ppermute x28, waiting for transfers between devices, cross(): return [lax.ppermute(piece, 'row', pairs) for piece in pieces]  113 us
    ppermute x8, waiting for transfers between devices, move(): return lax.ppermute(value, ('row', 'col'), pairs)  78.3 us
    ppermute x8, starting transfers between devices, move(): return lax.ppermute(value, ('row', 'col'), pairs)  68.3 us
    ppermute x12, waiting for transfers between devices, sum_over_row(): lax.ppermute(send, 'row', [(i, i ^ 1 << bit) for i in range(count)])  24.6 us
    ppermute x28, starting transfers between devices, cross(): return [lax.ppermute(piece, 'row', pairs) for piece in pieces]  17.9 us
    dot_general x4, matrix products, shards(): lax.dot_general(own_rows, after(block, last), (((0,), (0,)), ((), ())), p...  13 us
  transfers between devices with their start and end apart: 55, of which 19 were waited for; matrix products, arithmetic and copies ran while one was open for 7% of the time, Pallas kernels for 30%

profile of v2, /device:TPU:0, one launch (start us, length us, event | category | flops | bytes accessed | tf_op | source)
XLA Modules:
  0.0 616.1 jit_solution(12402726318987474869)
XLA Ops:
  12.9 16.3 %collective-permute-done.1.refs_1_ = f32[768,256]{1,0:T(8,128)S(1)} collective-permute-done((f32[768,256]{1,0:T(8,128)S(1)}, f32[768,256]{1,0:T(8,128)S(1)}, u32[]{:S(2)}, u32[]{:S(2)}) %collective-permute-start.1) | collective-permute-done | bytes 786464 | tf_op jit(solution)/shard_map/ppermute | solution.py:100
  32.1 9.1 %collective-permute-done.2.refs_1_ = f32[768,256]{1,0:T(8,128)S(1)} collective-permute-done((f32[768,256]{1,0:T(8,128)S(1)}, f32[768,256]{1,0:T(8,128)S(1)}, u32[]{:S(2)}, u32[]{:S(2)}) %collective-permute-start.2) | collective-permute-done | bytes 786464 | tf_op jit(solution)/shard_map/ppermute | solution.py:100
  41.2 25.4 %shard_map.68.refs_4_ = f32[3072,256]{1,0:T(8,128)S(1)} custom-call(s32[4]{0:T(128)S(1)} %get-tuple-element.37.place_ref, f32[3072,6144]{1,0:T(8,128)} %a_ref.13, f32[768,256]{1,0:T(8,128)S(1)} %slice.32.refs_0_, f32[768,256]{1,0:T(8,128)S(1)} %collective-permute-done.1.refs_1_, f32[768,256]{1,0:T(8,128)} %collective-permute-done.5.refs_2_, ...), custom_call_target="tpu_custom_call" | custom-call | flops 14495514624 | bytes 47185920 | tf_op jit(solution)/shard_map/pallas_call | solution.py:57
  66.7 26.5 %shard_map.69 = f32[3072,256]{1,0:T(8,128)} custom-call(s32[4]{0:T(128)S(1)} %get-tuple-element.38.place_ref, f32[3072,6144]{1,0:T(8,128)} %a_ref.13, f32[768,256]{1,0:T(8,128)S(1)} %collective-permute-done.refs_0_, f32[768,256]{1,0:T(8,128)S(1)} %collective-permute-done.2.refs_1_, f32[768,256]{1,0:T(8,128)S(1)} %collective-permute-done.3.refs_2_, ...), custom_call_target="tpu_custom_call" | custom-call | flops 14495514624 | bytes 47185920 | tf_op jit(solution)/shard_map/pallas_call | solution.py:57
  101.1 4.7 select_select_fusion.3
  108.9 17.4 %collective-permute-done.8.refs_1_ = f32[768,256]{1,0:T(8,128)S(1)} collective-permute-done((f32[768,256]{1,0:T(8,128)S(1)}, f32[768,256]{1,0:T(8,128)S(1)}, u32[]{:S(2)}, u32[]{:S(2)}) %collective-permute-start.8) | collective-permute-done | bytes 786464 | tf_op jit(solution)/shard_map/ppermute | solution.py:100
  128.0 10.3 %collective-permute-done.9.refs_1_ = f32[768,256]{1,0:T(8,128)S(1)} collective-permute-done((f32[768,256]{1,0:T(8,128)S(1)}, f32[768,256]{1,0:T(8,128)S(1)}, u32[]{:S(2)}, u32[]{:S(2)}) %collective-permute-start.9) | collective-permute-done | bytes 786464 | tf_op jit(solution)/shard_map/ppermute | solution.py:100
  138.4 25.3 %shard_map.70.refs_4_ = f32[3072,256]{1,0:T(8,128)S(1)} custom-call(s32[4]{0:T(128)S(1)} %get-tuple-element.37.place_ref, f32[3072,6144]{1,0:T(8,128)} %a_ref.13, f32[768,256]{1,0:T(8,128)S(1)} %get-tuple-element.15.refs_0_, f32[768,256]{1,0:T(8,128)S(1)} %collective-permute-done.8.refs_1_, f32[768,256]{1,0:T(8,128)S(1)} %collective-permute-done.12.refs_2_, ...), custom_call_target="tpu_custom_call" | custom-call | flops 14495514624 | bytes 47185920 | tf_op jit(solution)/shard_map/pallas_call | solution.py:57
  163.7 26.5 %shard_map.71 = f32[3072,256]{1,0:T(8,128)} custom-call(s32[4]{0:T(128)S(1)} %get-tuple-element.38.place_ref, f32[3072,6144]{1,0:T(8,128)} %a_ref.13, f32[768,256]{1,0:T(8,128)S(1)} %collective-permute-done.7.refs_0_, f32[768,256]{1,0:T(8,128)S(1)} %collective-permute-done.9.refs_1_, f32[768,256]{1,0:T(8,128)S(1)} %collective-permute-done.10.refs_2_, ...), custom_call_target="tpu_custom_call" | custom-call | flops 14495514624 | bytes 47185920 | tf_op jit(solution)/shard_map/pallas_call | solution.py:57
  195.0 17.9 %collective-permute-done.15.refs_1_ = f32[768,256]{1,0:T(8,128)} collective-permute-done((f32[768,256]{1,0:T(8,128)S(1)}, f32[768,256]{1,0:T(8,128)}, u32[]{:S(2)}, u32[]{:S(2)}) %collective-permute-start.15) | collective-permute-done | bytes 786464 | tf_op jit(solution)/shard_map/ppermute | solution.py:100
  214.1 11.1 %collective-permute-done.16.refs_1_ = f32[768,256]{1,0:T(8,128)} collective-permute-done((f32[768,256]{1,0:T(8,128)}, f32[768,256]{1,0:T(8,128)}, u32[]{:S(2)}, u32[]{:S(2)}) %collective-permute-start.16) | collective-permute-done | bytes 786464 | tf_op jit(solution)/shard_map/ppermute | solution.py:100
  225.2 25.8 %shard_map.72.refs_4_ = f32[3072,256]{1,0:T(8,128)S(1)} custom-call(s32[4]{0:T(128)S(1)} %get-tuple-element.37.place_ref, f32[3072,6144]{1,0:T(8,128)} %a_ref.13, f32[768,256]{1,0:T(8,128)S(1)} %get-tuple-element.17.refs_0_, f32[768,256]{1,0:T(8,128)} %collective-permute-done.15.refs_1_, f32[768,256]{1,0:T(8,128)} %collective-permute-done.19.refs_2_, ...), custom_call_target="tpu_custom_call" | custom-call | flops 14495514624 | bytes 47185920 | tf_op jit(solution)/shard_map/pallas_call | solution.py:57
  251.1 27.5 %shard_map.73 = f32[3072,256]{1,0:T(8,128)} custom-call(s32[4]{0:T(128)S(1)} %get-tuple-element.38.place_ref, f32[3072,6144]{1,0:T(8,128)} %a_ref.13, f32[768,256]{1,0:T(8,128)} %collective-permute-done.14.refs_0_, f32[768,256]{1,0:T(8,128)} %collective-permute-done.16.refs_1_, f32[768,256]{1,0:T(8,128)} %collective-permute-done.17.refs_2_, ...), custom_call_target="tpu_custom_call" | custom-call | flops 14495514624 | bytes 47185920 | tf_op jit(solution)/shard_map/pallas_call | solution.py:57
  280.7 18.5 %collective-permute-done.22.refs_1_ = f32[768,256]{1,0:T(8,128)} collective-permute-done((f32[768,256]{1,0:T(8,128)S(1)}, f32[768,256]{1,0:T(8,128)}, u32[]{:S(2)}, u32[]{:S(2)}) %collective-permute-start.22) | collective-permute-done | bytes 786464 | tf_op jit(solution)/shard_map/ppermute | solution.py:100
  299.7 11.8 %collective-permute-done.23.refs_1_ = f32[768,256]{1,0:T(8,128)} collective-permute-done((f32[768,256]{1,0:T(8,128)}, f32[768,256]{1,0:T(8,128)}, u32[]{:S(2)}, u32[]{:S(2)}) %collective-permute-start.23) | collective-permute-done | bytes 786464 | tf_op jit(solution)/shard_map/ppermute | solution.py:100
  311.5 25.8 %shard_map.74.refs_4_ = f32[3072,256]{1,0:T(8,128)S(1)} custom-call(s32[4]{0:T(128)S(1)} %get-tuple-element.37.place_ref, f32[3072,6144]{1,0:T(8,128)} %a_ref.13, f32[768,256]{1,0:T(8,128)S(1)} %get-tuple-element.20.refs_0_, f32[768,256]{1,0:T(8,128)} %collective-permute-done.22.refs_1_, f32[768,256]{1,0:T(8,128)} %collective-permute-done.26.refs_2_, ...), custom_call_target="tpu_custom_call" | custom-call | flops 14495514624 | bytes 47185920 | tf_op jit(solution)/shard_map/pallas_call | solution.py:57
  337.3 27.5 %shard_map.75 = f32[3072,256]{1,0:T(8,128)} custom-call(s32[4]{0:T(128)S(1)} %get-tuple-element.38.place_ref, f32[3072,6144]{1,0:T(8,128)} %a_ref.13, f32[768,256]{1,0:T(8,128)} %collective-permute-done.21.refs_0_, f32[768,256]{1,0:T(8,128)} %collective-permute-done.23.refs_1_, f32[768,256]{1,0:T(8,128)} %collective-permute-done.24.refs_2_, ...), custom_call_target="tpu_custom_call" | custom-call | flops 14495514624 | bytes 47185920 | tf_op jit(solution)/shard_map/pallas_call | solution.py:57
  378.0 7.4 %collective-permute-start.28 = (f32[768,256]{1,0:T(8,128)}, f32[768,256]{1,0:T(8,128)}, u32[]{:S(2)}, u32[]{:S(2)}) collective-permute-start(f32[768,256]{1,0:T(8,128)} %get-tuple-element.26), channel_id=1, source_target_pairs={{0,0},{1,1},{2,2},{3,3},{4,4},{5,5},{6,6},{7,7},{8,9},{9,8},{10,11... | collective-permute-start | bytes 2359304 | tf_op jit(solution)/shard_map/ppermute | solution.py:133
  402.0 7.4 %collective-permute-start.29 = (f32[768,256]{1,0:T(8,128)}, f32[768,256]{1,0:T(8,128)}, u32[]{:S(2)}, u32[]{:S(2)}) collective-permute-start(f32[768,256]{1,0:T(8,128)} %collective-permute-done.28), channel_id=1, source_target_pairs={{0,0},{1,9},{2,18},{3,27},{4,4},{5,13},{6,22},{7,31},{8,8},{9,1},{... | collective-permute-start | bytes 2359304 | tf_op jit(solution)/shard_map/ppermute | solution.py:133
  409.4 48.4 %collective-permute-done.30 = f32[768,256]{1,0:T(8,128)} collective-permute-done((f32[768,256]{1,0:T(8,128)S(1)}, f32[768,256]{1,0:T(8,128)}, u32[]{:S(2)}, u32[]{:S(2)}) %collective-permute-start.30) | collective-permute-done | bytes 786464 | tf_op jit(solution)/shard_map/ppermute | solution.py:133
  459.8 39.5 %collective-permute-start.33 = (f32[768,256]{1,0:T(8,128)}, f32[768,256]{1,0:T(8,128)}, u32[]{:S(2)}, u32[]{:S(2)}) collective-permute-start(f32[768,256]{1,0:T(8,128)} %collective-permute-done.32), channel_id=1, source_target_pairs={{0,16},{1,25},{2,2},{3,11},{4,20},{5,29},{6,6},{7,15},{8,24},{9,17... | collective-permute-start | bytes 2359304 | tf_op jit(solution)/shard_map/ppermute | solution.py:133
  504.0 29.8 %collective-permute-done.33 = f32[768,256]{1,0:T(8,128)} collective-permute-done((f32[768,256]{1,0:T(8,128)}, f32[768,256]{1,0:T(8,128)}, u32[]{:S(2)}, u32[]{:S(2)}) %collective-permute-start.33) | collective-permute-done | bytes 786464 | tf_op jit(solution)/shard_map/ppermute | solution.py:133
  550.1 5.8 collective-permute-done.37
  577.6 6.9 %collective-permute-done.43 = f32[2,128,256]{2,1,0:T(8,128)S(1)} collective-permute-done((f32[2,128,256]{2,1,0:T(8,128)S(1)}, f32[2,128,256]{2,1,0:T(8,128)S(1)}, u32[]{:S(2)}, u32[]{:S(2)}) %collective-permute-start.43) | collective-permute-done | bytes 262176 | tf_op jit(solution)/shard_map/ppermute | solution.py:112
  (186 shorter events, 110.9 us)
Async XLA Ops:
  7.2 218.0 %reduce-scatter.5.cloned.1.call-start = ((), (), s32[]{:S(2)}) async-start(), calls=%async_computation.4 | async-start | bytes 3932160 | tf_op jit(solution)/shard_map/reduce_scatter | solution.py:175
  8.4 20.8 %collective-permute-start.1 = (f32[768,256]{1,0:T(8,128)S(1)}, f32[768,256]{1,0:T(8,128)S(1)}, u32[]{:S(2)}, u32[]{:S(2)}) collective-permute-start(f32[768,256]{1,0:T(8,128)S(1)} %slice.32.refs_0_), channel_id=1, source_target_pairs={{0,8},{4,20},{8,0},{12,28},{16,24},{20,4},{24,16},{28,12},{1,9},{5... | collective-permute-start | bytes 2359304 | tf_op jit(solution)/shard_map/ppermute | solution.py:100
  11.4 20.7 %collective-permute-start = (f32[768,256]{1,0:T(8,128)S(1)}, f32[768,256]{1,0:T(8,128)S(1)}, u32[]{:S(2)}, u32[]{:S(2)}) collective-permute-start(f32[768,256]{1,0:T(8,128)S(1)} %slice.32.refs_0_), channel_id=1, source_target_pairs={{0,16},{4,12},{8,24},{12,4},{16,0},{20,28},{24,8},{28,20},{1,17},{... | collective-permute-start | bytes 2359304 | tf_op jit(solution)/shard_map/ppermute | solution.py:100
  32.1 34.6 %collective-permute-start.3 = (f32[768,256]{1,0:T(8,128)S(1)}, f32[768,256]{1,0:T(8,128)S(1)}, u32[]{:S(2)}, u32[]{:S(2)}) collective-permute-start(f32[768,256]{1,0:T(8,128)S(1)} %collective-permute-done.refs_0_), channel_id=1, source_target_pairs={{0,4},{4,0},{8,12},{12,8},{16,20},{20,16},{24,28},{28,24},{1,5},{5... | collective-permute-start | bytes 2359304 | tf_op jit(solution)/shard_map/ppermute | solution.py:100
  41.2 25.5 %collective-permute-start.4 = (f32[768,256]{1,0:T(8,128)S(1)}, f32[768,256]{1,0:T(8,128)S(1)}, u32[]{:S(2)}, u32[]{:S(2)}) collective-permute-start(f32[768,256]{1,0:T(8,128)S(1)} %collective-permute-done.2.refs_1_), channel_id=1, source_target_pairs={{0,4},{4,0},{8,12},{12,8},{16,20},{20,16},{24,28},{28,24},{1,5},{5... | collective-permute-start | bytes 2359304 | tf_op jit(solution)/shard_map/ppermute | solution.py:100
  95.0 216.4 %reduce-scatter.7.cloned.1.call-start = ((), (), s32[]{:S(2)}) async-start(), calls=%async_computation.5 | async-start | bytes 3932160 | tf_op jit(solution)/shard_map/reduce_scatter | solution.py:175
  105.8 20.6 %collective-permute-start.8 = (f32[768,256]{1,0:T(8,128)S(1)}, f32[768,256]{1,0:T(8,128)S(1)}, u32[]{:S(2)}, u32[]{:S(2)}) collective-permute-start(f32[768,256]{1,0:T(8,128)S(1)} %get-tuple-element.15.refs_0_), channel_id=1, source_target_pairs={{0,8},{4,20},{8,0},{12,28},{16,24},{20,4},{24,16},{28,12},{1,9},{5... | collective-permute-start | bytes 2359304 | tf_op jit(solution)/shard_map/ppermute | solution.py:100
  127.9 35.8 %collective-permute-start.10 = (f32[768,256]{1,0:T(8,128)S(1)}, f32[768,256]{1,0:T(8,128)S(1)}, u32[]{:S(2)}, u32[]{:S(2)}) collective-permute-start(f32[768,256]{1,0:T(8,128)S(1)} %collective-permute-done.7.refs_0_), channel_id=1, source_target_pairs={{0,4},{4,0},{8,12},{12,8},{16,20},{20,16},{24,28},{28,24},{1,5},{5... | collective-permute-start | bytes 2359304 | tf_op jit(solution)/shard_map/ppermute | solution.py:100
  138.3 25.4 %collective-permute-start.11 = (f32[768,256]{1,0:T(8,128)S(1)}, f32[768,256]{1,0:T(8,128)S(1)}, u32[]{:S(2)}, u32[]{:S(2)}) collective-permute-start(f32[768,256]{1,0:T(8,128)S(1)} %collective-permute-done.9.refs_1_), channel_id=1, source_target_pairs={{0,4},{4,0},{8,12},{12,8},{16,20},{20,16},{24,28},{28,24},{1,5},{5... | collective-permute-start | bytes 2359304 | tf_op jit(solution)/shard_map/ppermute | solution.py:100
  192.0 371.0 %reduce-scatter.9.cloned.1.call-start = ((), (), s32[]{:S(2)}) async-start(), calls=%async_computation.6 | async-start | bytes 3932160 | tf_op jit(solution)/shard_map/reduce_scatter | solution.py:175
  192.3 20.6 %collective-permute-start.15 = (f32[768,256]{1,0:T(8,128)S(1)}, f32[768,256]{1,0:T(8,128)}, u32[]{:S(2)}, u32[]{:S(2)}) collective-permute-start(f32[768,256]{1,0:T(8,128)S(1)} %get-tuple-element.17.refs_0_), channel_id=1, source_target_pairs={{0,8},{4,20},{8,0},{12,28},{16,24},{20,4},{24,16},{28,12},{1,9},{5... | collective-permute-start | bytes 2359304 | tf_op jit(solution)/shard_map/ppermute | solution.py:100
  214.0 37.0 %collective-permute-start.17 = (f32[768,256]{1,0:T(8,128)}, f32[768,256]{1,0:T(8,128)}, u32[]{:S(2)}, u32[]{:S(2)}) collective-permute-start(f32[768,256]{1,0:T(8,128)} %collective-permute-done.14.refs_0_), channel_id=1, source_target_pairs={{0,4},{4,0},{8,12},{12,8},{16,20},{20,16},{24,28},{28,24},{1,5},{5... | collective-permute-start | bytes 2359304 | tf_op jit(solution)/shard_map/ppermute | solution.py:100
  225.2 25.9 %collective-permute-start.18 = (f32[768,256]{1,0:T(8,128)}, f32[768,256]{1,0:T(8,128)}, u32[]{:S(2)}, u32[]{:S(2)}) collective-permute-start(f32[768,256]{1,0:T(8,128)} %collective-permute-done.16.refs_1_), channel_id=1, source_target_pairs={{0,4},{4,0},{8,12},{12,8},{16,20},{20,16},{24,28},{28,24},{1,5},{5... | collective-permute-start | bytes 2359304 | tf_op jit(solution)/shard_map/ppermute | solution.py:100
  278.6 290.0 %reduce-scatter.11.cloned.1.call-start = ((), (), s32[]{:S(2)}) async-start(), calls=%async_computation.7 | async-start | bytes 3932160 | tf_op jit(solution)/shard_map/reduce_scatter | solution.py:175
  299.7 37.6 %collective-permute-start.24 = (f32[768,256]{1,0:T(8,128)}, f32[768,256]{1,0:T(8,128)}, u32[]{:S(2)}, u32[]{:S(2)}) collective-permute-start(f32[768,256]{1,0:T(8,128)} %collective-permute-done.21.refs_0_), channel_id=1, source_target_pairs={{0,4},{4,0},{8,12},{12,8},{16,20},{20,16},{24,28},{28,24},{1,5},{5... | collective-permute-start | bytes 2359304 | tf_op jit(solution)/shard_map/ppermute | solution.py:100
  311.4 25.9 %collective-permute-start.25 = (f32[768,256]{1,0:T(8,128)}, f32[768,256]{1,0:T(8,128)}, u32[]{:S(2)}, u32[]{:S(2)}) collective-permute-start(f32[768,256]{1,0:T(8,128)} %collective-permute-done.23.refs_1_), channel_id=1, source_target_pairs={{0,4},{4,0},{8,12},{12,8},{16,20},{20,16},{24,28},{28,24},{1,5},{5... | collective-permute-start | bytes 2359304 | tf_op jit(solution)/shard_map/ppermute | solution.py:100
  378.0 24.0 %collective-permute-start.28 = (f32[768,256]{1,0:T(8,128)}, f32[768,256]{1,0:T(8,128)}, u32[]{:S(2)}, u32[]{:S(2)}) collective-permute-start(f32[768,256]{1,0:T(8,128)} %get-tuple-element.26), channel_id=1, source_target_pairs={{0,0},{1,1},{2,2},{3,3},{4,4},{5,5},{6,6},{7,7},{8,9},{9,8},{10,11... | collective-permute-start | bytes 2359304 | tf_op jit(solution)/shard_map/ppermute | solution.py:133
  387.5 70.4 %collective-permute-start.30 = (f32[768,256]{1,0:T(8,128)S(1)}, f32[768,256]{1,0:T(8,128)}, u32[]{:S(2)}, u32[]{:S(2)}) collective-permute-start(f32[768,256]{1,0:T(8,128)S(1)} %select_select_fusion.2), channel_id=1, source_target_pairs={{0,1},{1,0},{2,3},{3,2},{4,5},{5,4},{6,7},{7,6},{8,8},{9,9},{10,10... | collective-permute-start | bytes 2359304 | tf_op jit(solution)/shard_map/ppermute | solution.py:133
  393.2 66.5 %collective-permute-start.32 = (f32[768,256]{1,0:T(8,128)S(1)}, f32[768,256]{1,0:T(8,128)}, u32[]{:S(2)}, u32[]{:S(2)}) collective-permute-start(f32[768,256]{1,0:T(8,128)S(1)} %select_select_fusion.1), channel_id=1, source_target_pairs={{0,2},{1,3},{2,0},{3,1},{4,6},{5,7},{6,4},{7,5},{8,11},{9,10},{10,... | collective-permute-start | bytes 2359304 | tf_op jit(solution)/shard_map/ppermute | solution.py:133
  399.7 99.5 %collective-permute-start.34 = (f32[768,256]{1,0:T(8,128)S(1)}, f32[768,256]{1,0:T(8,128)}, u32[]{:S(2)}, u32[]{:S(2)}) collective-permute-start(f32[768,256]{1,0:T(8,128)S(1)} %select_select_fusion), channel_id=1, source_target_pairs={{0,3},{1,2},{2,1},{3,0},{4,7},{5,6},{6,5},{7,4},{8,10},{9,11},{10,... | collective-permute-start | bytes 2359304 | tf_op jit(solution)/shard_map/ppermute | solution.py:133
  402.0 99.5 %collective-permute-start.29 = (f32[768,256]{1,0:T(8,128)}, f32[768,256]{1,0:T(8,128)}, u32[]{:S(2)}, u32[]{:S(2)}) collective-permute-start(f32[768,256]{1,0:T(8,128)} %collective-permute-done.28), channel_id=1, source_target_pairs={{0,0},{1,9},{2,18},{3,27},{4,4},{5,13},{6,22},{7,31},{8,8},{9,1},{... | collective-permute-start | bytes 2359304 | tf_op jit(solution)/shard_map/ppermute | solution.py:133
  457.9 44.9 %collective-permute-start.31 = (f32[768,256]{1,0:T(8,128)}, f32[768,256]{1,0:T(8,128)}, u32[]{:S(2)}, u32[]{:S(2)}) collective-permute-start(f32[768,256]{1,0:T(8,128)} %collective-permute-done.30), channel_id=1, source_target_pairs={{0,8},{1,1},{2,26},{3,19},{4,12},{5,5},{6,30},{7,23},{8,0},{9,9},{... | collective-permute-start | bytes 2359304 | tf_op jit(solution)/shard_map/ppermute | solution.py:133
  459.8 74.1 %collective-permute-start.33 = (f32[768,256]{1,0:T(8,128)}, f32[768,256]{1,0:T(8,128)}, u32[]{:S(2)}, u32[]{:S(2)}) collective-permute-start(f32[768,256]{1,0:T(8,128)} %collective-permute-done.32), channel_id=1, source_target_pairs={{0,16},{1,25},{2,2},{3,11},{4,20},{5,29},{6,6},{7,15},{8,24},{9,17... | collective-permute-start | bytes 2359304 | tf_op jit(solution)/shard_map/ppermute | solution.py:133
  499.3 35.8 %collective-permute-start.35 = (f32[768,256]{1,0:T(8,128)}, f32[768,256]{1,0:T(8,128)}, u32[]{:S(2)}, u32[]{:S(2)}) collective-permute-start(f32[768,256]{1,0:T(8,128)} %collective-permute-done.34), channel_id=1, source_target_pairs={{0,24},{1,17},{2,10},{3,3},{4,28},{5,21},{6,14},{7,7},{8,16},{9,25... | collective-permute-start | bytes 2359304 | tf_op jit(solution)/shard_map/ppermute | solution.py:133
  (53 other events, 665.3 us)
Sparse Core Ops, SparseCore 0:
  95.1 61.8 reduce-scatter.4
  192.2 61.1 reduce-scatter.6
  278.7 60.9 reduce-scatter.8
  364.9 92.0 reduce-scatter.10

commit v3 on v2

--- a/solution.py
+++ b/solution.py
@@ -9,6 +9,7 @@
 from jax.sharding import PartitionSpec as P
 
 CHUNKS = 4
+SPLITS = 2
 LANES = 128
 MIB = 1 << 20
 
@@ -23,56 +24,103 @@
     return max(d for d in range(unit, min(extent, limit) + 1, unit) if extent % d == 0)
 
 
-def product_kernel(count, place_ref, a_ref, *refs):
+def split_kernel(place_ref, *refs):
     del place_ref
-    pieces, sums, (out_ref, high_ref, low_ref) = refs[:count], refs[count:-3], refs[-3:]
-    step = pl.program_id(1)
-
-    for slot, piece in enumerate(pieces):
-
-        @pl.when((pl.program_id(0) == 0) & (step == slot))
-        def _():
-            high_ref[slot], low_ref[slot] = split(-piece[...])
-
-    @pl.when(step == 0)
+    high_ref, low_ref = refs[-2:]
+    count = high_ref.shape[1] // refs[0].shape[1]
+    for slot, a_ref in enumerate(refs[:count]):
+        span = pl.ds(slot * a_ref.shape[1], a_ref.shape[1])
+        high_ref[:, span], low_ref[:, span] = split(a_ref[...])
+
+
+def split_part(a, place, depth, part, given):
+    rows = a.shape[0]
+    count = place.shape[0]
+    tile = largest_divisor(rows // SPLITS, 16, 256)
+    steps = rows // SPLITS // tile
+    a_specs = [
+        pl.BlockSpec((tile, depth), lambda i, place, slot=slot: (part * steps + i, place[slot])) for slot in range(count)
+    ]
+    return pl.pallas_call(
+        split_kernel,
+        grid_spec=pltpu.PrefetchScalarGridSpec(
+            num_scalar_prefetch=1,
+            grid=(steps,),
+            in_specs=a_specs + [pl.BlockSpec(memory_space=pl.ANY)] * len(given),
+            out_specs=[pl.BlockSpec((tile, count * depth), lambda i, _: (part * steps + i, 0))] * 2,
+        ),
+        out_shape=[jax.ShapeDtypeStruct((rows, count * depth), jnp.bfloat16)] * 2,
+        input_output_aliases={1 + count: 0, 2 + count: 1} if given else {},
+        compiler_params=pltpu.CompilerParams(vmem_limit_bytes=24 * MIB, dimension_semantics=("arbitrary",)),
+        cost_estimate=pl.CostEstimate(
+            flops=2 * rows * depth * count // SPLITS,
+            bytes_accessed=8 * rows * depth * count // SPLITS,
+            transcendentals=0,
+        ),
+    )(place, *[a] * count, *given)
+
+
+def product_kernel(count, ahead, place_ref, *refs):
+    del place_ref
+    a_count = 2 if ahead else count
+    a_refs, pieces, sums = refs[:a_count], refs[a_count : a_count + count], refs[a_count + count : -2]
+    out_ref, both_ref = refs[-2:]
+    columns = out_ref.shape[1]
+    depth = both_ref.shape[1]
+
+    @pl.when(pl.program_id(0) == 0)
     def _():
-        out_ref[...] = sums[0][...] if sums else jnp.zeros_like(out_ref)
+        for slot, piece in enumerate(pieces):
+            both_ref[slot, :, :columns], both_ref[slot, :, columns:] = split(-piece[...])
 
     dot = functools.partial(jnp.dot, preferred_element_type=jnp.float32)
-    extent = largest_divisor(a_ref.shape[0], 16, 256)
-    for first in range(0, a_ref.shape[0], extent):
+    extent = largest_divisor(out_ref.shape[0], 16, 256)
+    for first in range(0, out_ref.shape[0], extent):
         rows = pl.ds(first, extent)
-        high, low = split(a_ref[rows, :])
-        both = dot(jnp.concatenate([high, low], axis=0), high_ref[step])
-        out_ref[rows, :] += both[:extent] + (both[extent:] + dot(high, low_ref[step]))
-
-
-def negative_product(a, pieces, place, sums=None):
-    rows = a.shape[0]
+        wide = narrow = None
+        for slot in range(count):
+            if ahead:
+                high, low = (a_ref[rows, slot * depth : (slot + 1) * depth] for a_ref in a_refs)
+            else:
+                high, low = split(a_refs[slot][rows, :])
+            terms = dot(high, both_ref[slot]), dot(low, both_ref[slot, :, :columns])
+            wide, narrow = terms if wide is None else (wide + terms[0], narrow + terms[1])
+        total = wide[:, :columns] + (wide[:, columns:] + narrow)
+        out_ref[rows, :] = total + sums[0][rows, :] if sums else total
+
+
+def negative_product(a, pieces, place=None, sums=None):
+    ahead = place is None
+    rows = a[0].shape[0] if ahead else a.shape[0]
+    count = len(pieces)
     depth, columns = pieces[0].shape
-    tile = largest_divisor(rows, 16, 768)
-    out_spec = pl.BlockSpec((tile, columns), lambda i, k, _: (i, 0))
-    whole = [pl.BlockSpec(piece.shape, lambda i, k, _: (0, 0), pipeline_mode=pl.Buffered(1)) for piece in pieces]
+    tile = largest_divisor(rows, 16, 512)
+    out_spec = pl.BlockSpec((tile, columns), lambda i, _: (i, 0))
+    if ahead:
+        place = jnp.zeros((1,), jnp.int32)
+        a_specs = [pl.BlockSpec((tile, depth * count), lambda i, _: (i, 0))] * 2
+    else:
+        a = [a] * count
+        a_specs = [pl.BlockSpec((tile, depth), lambda i, place, slot=slot: (i, place[slot])) for slot in range(count)]
+    whole = [pl.BlockSpec(piece.shape, lambda i, _: (0, 0), pipeline_mode=pl.Buffered(1)) for piece in pieces]
     given = [] if sums is None else [sums]
     return pl.pallas_call(
-        functools.partial(product_kernel, len(pieces)),
+        functools.partial(product_kernel, count, ahead),
         grid_spec=pltpu.PrefetchScalarGridSpec(
             num_scalar_prefetch=1,
-            grid=(rows // tile, len(pieces)),
-            in_specs=[pl.BlockSpec((tile, depth), lambda i, k, place: (i, place[k]))] + whole + [out_spec] * len(given),
+            grid=(rows // tile,),
+            in_specs=a_specs + whole + [out_spec] * len(given),
             out_specs=out_spec,
-            scratch_shapes=[pltpu.VMEM((len(pieces), depth, columns), jnp.bfloat16)] * 2,
+            scratch_shapes=[pltpu.VMEM((count, depth, 2 * columns), jnp.bfloat16)],
         ),
         out_shape=jax.ShapeDtypeStruct((rows, columns), jnp.float32),
-        compiler_params=pltpu.CompilerParams(
-            vmem_limit_bytes=40 * MIB, dimension_semantics=("arbitrary", "arbitrary")
-        ),
+        compiler_params=pltpu.CompilerParams(vmem_limit_bytes=40 * MIB, dimension_semantics=("arbitrary",)),
         cost_estimate=pl.CostEstimate(
-            flops=6 * rows * depth * len(pieces) * columns,
-            bytes_accessed=4 * (rows * depth * len(pieces) + depth * len(pieces) * columns + 2 * rows * columns),
+            flops=6 * rows * depth * count * columns,
+            bytes_accessed=4 * (rows * depth * count + depth * count * columns + 2 * rows * columns),
             transcendentals=0,
         ),
-    )(place, a, *pieces, *given)
+    )(place, *a, *pieces, *given)
 
 
 def gather_orders(count):
@@ -166,31 +214,30 @@
             value, lambda r, c: (((r // group) ^ c ^ (chunk % column_count)) * group + r % group, c)
         )
 
-    blocks, own_rows = [], []
-
-    def held_back(chunk):
-        return after(parent_inverse, blocks[chunk - 2]) if chunk >= 2 else parent_inverse
-
     def summed(partial_block):
         return lax.psum_scatter(partial_block, "col", scatter_dimension=0, tiled=True)
 
+    products, blocks, own_rows = [], [], []
     waiting = None
     last = None
     if stepwise:
         half = row_count // 2
+        halves = ()
+        for part in range(SPLITS):
+            halves = split_part(parent_inverse, place[half:], block_rows, part, halves)
         following = early(0, None)
         for chunk in range(CHUNKS):
             mine, first = following
             others = cross([mine[0] if last is None else after(mine[0], last)] + mine[1:], orders[-1], row_count)
-            last = negative_product(held_back(chunk), first, place[:half])
+            last = negative_product(parent_inverse, first, place[:half])
             second = others + partner(others)
             if chunk + 1 < CHUNKS:
                 following = early(chunk + 1, last)
             if waiting is not None:
                 own_rows.append(hop(waiting, chunk - 1))
-                waiting = None
             waiting = spread(chunk, lambda wanted: lax.select_n(slots[wanted], *first, *second))
-            last = negative_product(parent_inverse, second, place[half:], last)
+            last = negative_product(halves, second, sums=last)
+            products.append(last)
             blocks.append(summed(last))
         own_rows.append(hop(waiting, CHUNKS - 1))
     else:
@@ -200,14 +247,14 @@
                 chunk, lambda wanted: lax.dynamic_slice_in_dim(whole, wanted * block_rows, block_rows, 0)
             )
             own_rows.append(hop(waiting, chunk))
-            last = negative_product(held_back(chunk), [whole], jnp.zeros((1,), jnp.int32))
-            blocks.append(summed(last))
+            products.append(negative_product(parent_inverse, [whole], jnp.zeros((1,), jnp.int32)))
+            blocks.append(summed(products[-1]))
     own_rows = jnp.concatenate(own_rows, axis=1)
     grams = []
-    for block in blocks:
+    for chunk, block in enumerate(blocks):
         gram = lax.dot_general(
             own_rows,
-            after(block, last),
+            after(block, products[min(chunk + 2, CHUNKS - 1)]),
             (((0,), (0,)), ((), ())),
             precision=lax.Precision.HIGH,
             preferred_element_type=jnp.float32,

time: 621 us -> 605 us (0.974)
  starting transfers between devices: 102 us -> 75.5 us
  Pallas kernels: 210 us -> 186 us
  local copies, waits for them, and re-layouts: 17.5 us -> 36.4 us
  waiting for transfers between devices: 222 us -> 231 us
    ppermute x8, starting transfers between devices: 68.3 us -> 33.4 us  [move(): return lax.ppermute(value, ('row', 'col'), pairs)]
    ppermute x8, waiting for transfers between devices: 78.3 us -> 111 us  [move(): return lax.ppermute(value, ('row', 'col'), pairs)]
    ppermute x28, waiting for transfers between devices: 113 us -> 88.1 us  [cross(): return [lax.ppermute(piece, 'row', pairs) for piece in pieces]]
    pallas_call x8 -> x10, Pallas kernels: 210 us -> 186 us  [the longest x8 163 us: negative_product(): pl.pallas_call(functools.partial(product_kernel, count, ahead), grid_spec...]
    unnamed x47 -> x95, local copies, waits for them, and re-layouts: 10.2 us -> 27.6 us
    ppermute x12, starting transfers between devices: 9.44 us -> 18 us  [sum_over_row(): lax.ppermute(send, 'row', [(i, i ^ 1 << bit) for i in range(count)])]
  transfers between devices with their start and end apart: 55 -> 55, of which waited for: 19 -> 17; matrix products, arithmetic and copies ran while one was open for 7% -> 8% of each run, Pallas kernels for 30% -> 28%
where the time goes in v3:
time: 605 us; the launch traced here: 598 us
  waiting for transfers between devices  231 us (38%)
  Pallas kernels  186 us (31%)
  starting transfers between devices  75.5 us (12%)
  local copies, waits for them, and re-layouts  36.4 us (6%)
  between operations  33.3 us (6%)
  other arithmetic  20.6 us (3%)
  matrix products  15.2 us (3%)
    pallas_call x8, Pallas kernels, negative_product(): pl.pallas_call(functools.partial(product_kernel, count, ahead), grid_spec...  163 us
    ppermute x8, waiting for transfers between devices, move(): return lax.ppermute(value, ('row', 'col'), pairs)  111 us
    ppermute x28, waiting for transfers between devices, cross(): return [lax.ppermute(piece, 'row', pairs) for piece in pieces]  88.1 us
    ppermute x8, starting transfers between devices, move(): return lax.ppermute(value, ('row', 'col'), pairs)  33.4 us
    unnamed x95, local copies, waits for them, and re-layouts  27.6 us
    ppermute x12, waiting for transfers between devices, sum_over_row(): lax.ppermute(send, 'row', [(i, i ^ 1 << bit) for i in range(count)])  24.2 us
    pallas_call x2, Pallas kernels, split_part(): pl.pallas_call(split_kernel, grid_spec=pltpu.PrefetchScalarGridSpec(num_s...  23.2 us
    ppermute x28, starting transfers between devices, cross(): return [lax.ppermute(piece, 'row', pairs) for piece in pieces]  21.4 us
  transfers between devices with their start and end apart: 55, of which 17 were waited for; matrix products, arithmetic and copies ran while one was open for 8% of the time, Pallas kernels for 28%

profile of v3, /device:TPU:0, one launch (start us, length us, event | category | flops | bytes accessed | tf_op | source)
XLA Modules:
  0.0 598.2 jit_solution(16288707348632025203)
XLA Ops:
  13.7 16.6 %collective-permute-done.1.refs_5_ = f32[768,256]{1,0:T(8,128)} collective-permute-done((f32[768,256]{1,0:T(8,128)}, f32[768,256]{1,0:T(8,128)}, u32[]{:S(2)}, u32[]{:S(2)}) %collective-permute-start.1) | collective-permute-done | bytes 786464 | tf_op jit(solution)/shard_map/ppermute | solution.py:148
  33.1 11.6 %shard_map.68 = (bf16[3072,3072]{1,0:T(8,128)(2,1)S(1)}, bf16[3072,3072]{1,0:T(8,128)(2,1)}) custom-call(s32[4]{0:T(128)S(1)} %get-tuple-element.42.place_ref, f32[3072,6144]{1,0:T(8,128)} %refs_3_.11, f32[3072,6144]{1,0:T(8,128)} %refs_3_.11, f32[3072,6144]{1,0:T(8,128)} %refs_3_.11, f32[3072,6144]{1,0:T(8,128)} %refs_3_.11), custom_call_target="tpu_custom_call" | custom-call | flops 9437184 | bytes 37748736 | tf_op jit(solution)/shard_map/pallas_call | solution.py:44
  44.8 11.6 %shard_map.69 = (bf16[3072,3072]{1,0:T(8,128)(2,1)S(1)}, bf16[3072,3072]{1,0:T(8,128)(2,1)}) custom-call(s32[4]{0:T(128)S(1)} %get-tuple-element.42.place_ref, f32[3072,6144]{1,0:T(8,128)} %refs_3_.11, f32[3072,6144]{1,0:T(8,128)} %refs_3_.11, f32[3072,6144]{1,0:T(8,128)} %refs_3_.11, ...), custom_call_target="tpu_custom_call", output_to_operand_aliasing={{0}: (5, {}), {1}: (6, {})} | custom-call | flops 9437184 | bytes 37748736 | tf_op jit(solution)/shard_map/pallas_call | solution.py:44
  56.4 6.4 %copy-done = bf16[3072,3072]{1,0:T(8,128)(2,1)} copy-done((bf16[3072,3072]{1,0:T(8,128)(2,1)}, bf16[3072,3072]{1,0:T(8,128)(2,1)S(1)}, u32[]{:S(2)}) %copy-start) | copy-done | bytes 18874392
  63.3 21.6 %shard_map.70.refs_6_ = f32[3072,256]{1,0:T(8,128)S(1)} custom-call(s32[4]{0:T(128)S(1)} %get-tuple-element.41.place_ref, f32[3072,6144]{1,0:T(8,128)} %refs_3_.11, f32[3072,6144]{1,0:T(8,128)} %refs_3_.11, f32[3072,6144]{1,0:T(8,128)} %refs_3_.11, f32[3072,6144]{1,0:T(8,128)} %refs_3_.11, f32[768,256]{1,0:T(8,128)} %slice.30.refs_4_, ...), custom_call_target="tpu_custom_call" | custom-call | flops 14495514624 | bytes 47185920 | tf_op jit(solution)/shard_map/pallas_call | solution.py:107
  84.9 21.2 %shard_map.71 = f32[3072,256]{1,0:T(8,128)} custom-call(s32[1]{0:T(128)} %constant.197.clone.1.place_ref, bf16[3072,3072]{1,0:T(8,128)(2,1)} %copy-done, bf16[3072,3072]{1,0:T(8,128)(2,1)} %get-tuple-element.19.refs_1_, f32[768,256]{1,0:T(8,128)} %collective-permute-done.refs_2_, f32[768,256]{1,0:T(8,128)} %collective-permute-done.2.refs_3_, ...), custom_call_target="tpu_custom_call" | custom-call | flops 14495514624 | bytes 47185920 | tf_op jit(solution)/shard_map/pallas_call | solution.py:107
  119.8 17.1 %collective-permute-done.8.refs_5_ = f32[768,256]{1,0:T(8,128)S(1)} collective-permute-done((f32[768,256]{1,0:T(8,128)S(1)}, f32[768,256]{1,0:T(8,128)S(1)}, u32[]{:S(2)}, u32[]{:S(2)}) %collective-permute-start.8) | collective-permute-done | bytes 786464 | tf_op jit(solution)/shard_map/ppermute | solution.py:148
  138.6 10.3 %collective-permute-done.9.refs_3_ = f32[768,256]{1,0:T(8,128)S(1)} collective-permute-done((f32[768,256]{1,0:T(8,128)S(1)}, f32[768,256]{1,0:T(8,128)S(1)}, u32[]{:S(2)}, u32[]{:S(2)}) %collective-permute-start.9) | collective-permute-done | bytes 786464 | tf_op jit(solution)/shard_map/ppermute | solution.py:148
  148.9 20.4 %shard_map.72.refs_6_ = f32[3072,256]{1,0:T(8,128)S(1)} custom-call(s32[4]{0:T(128)S(1)} %get-tuple-element.41.place_ref, f32[3072,6144]{1,0:T(8,128)} %refs_3_.11, f32[3072,6144]{1,0:T(8,128)} %refs_3_.11, f32[3072,6144]{1,0:T(8,128)} %refs_3_.11, f32[3072,6144]{1,0:T(8,128)} %refs_3_.11, f32[768,256]{1,0:T(8,128)S(1)} %get-tuple-element.21.refs_4_, ...), custom_call_target="tpu_custom_call" | custom-call | flops 14495514624 | bytes 47185920 | tf_op jit(solution)/shard_map/pallas_call | solution.py:107
  169.4 19.6 %shard_map.73 = f32[3072,256]{1,0:T(8,128)S(1)} custom-call(s32[1]{0:T(128)} %constant.197.clone.1.place_ref, bf16[3072,3072]{1,0:T(8,128)(2,1)} %copy-done, bf16[3072,3072]{1,0:T(8,128)(2,1)} %get-tuple-element.19.refs_1_, f32[768,256]{1,0:T(8,128)S(1)} %collective-permute-done.7.refs_2_, f32[768,256]{1,0:T(8,128)S(1)} %collective-permute-done.9.refs_3_, ...), custom_call_target="tpu_custom_call" | custom-call | flops 14495514624 | bytes 47185920 | tf_op jit(solution)/shard_map/pallas_call | solution.py:107
  195.5 17.4 %collective-permute-done.15.refs_5_ = f32[768,256]{1,0:T(8,128)S(1)} collective-permute-done((f32[768,256]{1,0:T(8,128)S(1)}, f32[768,256]{1,0:T(8,128)S(1)}, u32[]{:S(2)}, u32[]{:S(2)}) %collective-permute-start.15) | collective-permute-done | bytes 786464 | tf_op jit(solution)/shard_map/ppermute | solution.py:148
  214.7 10.1 %collective-permute-done.16.refs_3_ = f32[768,256]{1,0:T(8,128)S(1)} collective-permute-done((f32[768,256]{1,0:T(8,128)S(1)}, f32[768,256]{1,0:T(8,128)S(1)}, u32[]{:S(2)}, u32[]{:S(2)}) %collective-permute-start.16) | collective-permute-done | bytes 786464 | tf_op jit(solution)/shard_map/ppermute | solution.py:148
  224.9 20.5 %shard_map.74.refs_6_ = f32[3072,256]{1,0:T(8,128)S(1)} custom-call(s32[4]{0:T(128)S(1)} %get-tuple-element.41.place_ref, f32[3072,6144]{1,0:T(8,128)} %refs_3_.11, f32[3072,6144]{1,0:T(8,128)} %refs_3_.11, f32[3072,6144]{1,0:T(8,128)} %refs_3_.11, f32[3072,6144]{1,0:T(8,128)} %refs_3_.11, f32[768,256]{1,0:T(8,128)S(1)} %get-tuple-element.23.refs_4_, ...), custom_call_target="tpu_custom_call" | custom-call | flops 14495514624 | bytes 47185920 | tf_op jit(solution)/shard_map/pallas_call | solution.py:107
  245.5 19.6 %shard_map.75 = f32[3072,256]{1,0:T(8,128)S(1)} custom-call(s32[1]{0:T(128)} %constant.197.clone.1.place_ref, bf16[3072,3072]{1,0:T(8,128)(2,1)} %copy-done, bf16[3072,3072]{1,0:T(8,128)(2,1)} %get-tuple-element.19.refs_1_, f32[768,256]{1,0:T(8,128)S(1)} %collective-permute-done.14.refs_2_, f32[768,256]{1,0:T(8,128)S(1)} %collective-permute-done.16.refs_3_, ...), custom_call_target="tpu_custom_call" | custom-call | flops 14495514624 | bytes 47185920 | tf_op jit(solution)/shard_map/pallas_call | solution.py:107
  272.7 16.6 %collective-permute-done.22.refs_5_ = f32[768,256]{1,0:T(8,128)S(1)} collective-permute-done((f32[768,256]{1,0:T(8,128)S(1)}, f32[768,256]{1,0:T(8,128)S(1)}, u32[]{:S(2)}, u32[]{:S(2)}) %collective-permute-start.22) | collective-permute-done | bytes 786464 | tf_op jit(solution)/shard_map/ppermute | solution.py:148
  304.1 7.4 %collective-permute-start.28 = (f32[768,256]{1,0:T(8,128)}, f32[768,256]{1,0:T(8,128)}, u32[]{:S(2)}, u32[]{:S(2)}) collective-permute-start(f32[768,256]{1,0:T(8,128)} %get-tuple-element.30), channel_id=1, source_target_pairs={{0,0},{1,1},{2,2},{3,3},{4,4},{5,5},{6,6},{7,7},{8,9},{9,8},{10,11... | collective-permute-start | bytes 2359304 | tf_op jit(solution)/shard_map/ppermute | solution.py:181
  318.4 20.2 %shard_map.76.refs_6_ = f32[3072,256]{1,0:T(8,128)S(1)} custom-call(s32[4]{0:T(128)S(1)} %get-tuple-element.41.place_ref, f32[3072,6144]{1,0:T(8,128)} %refs_3_.11, f32[3072,6144]{1,0:T(8,128)} %refs_3_.11, f32[3072,6144]{1,0:T(8,128)} %refs_3_.11, f32[3072,6144]{1,0:T(8,128)} %refs_3_.11, f32[768,256]{1,0:T(8,128)S(1)} %copy-done.1, ...), custom_call_target="tpu_custom_call" | custom-call | flops 14495514624 | bytes 47185920 | tf_op jit(solution)/shard_map/pallas_call | solution.py:107
  338.7 19.6 %shard_map.77 = f32[3072,256]{1,0:T(8,128)S(1)} custom-call(s32[1]{0:T(128)} %constant.197.clone.1.place_ref, bf16[3072,3072]{1,0:T(8,128)(2,1)} %copy-done, bf16[3072,3072]{1,0:T(8,128)(2,1)} %get-tuple-element.19.refs_1_, f32[768,256]{1,0:T(8,128)S(1)} %collective-permute-done.21.refs_2_, f32[768,256]{1,0:T(8,128)S(1)} %collective-permute-done.23.refs_3_, ...), custom_call_target="tpu_custom_call" | custom-call | flops 14495514624 | bytes 47185920 | tf_op jit(solution)/shard_map/pallas_call | solution.py:107
  372.8 7.4 %collective-permute-start.29 = (f32[768,256]{1,0:T(8,128)}, f32[768,256]{1,0:T(8,128)}, u32[]{:S(2)}, u32[]{:S(2)}) collective-permute-start(f32[768,256]{1,0:T(8,128)} %collective-permute-done.28), channel_id=1, source_target_pairs={{0,0},{1,9},{2,18},{3,27},{4,4},{5,13},{6,22},{7,31},{8,8},{9,1},{... | collective-permute-start | bytes 2359304 | tf_op jit(solution)/shard_map/ppermute | solution.py:181
  384.3 79.6 %collective-permute-done.32 = f32[768,256]{1,0:T(8,128)} collective-permute-done((f32[768,256]{1,0:T(8,128)S(1)}, f32[768,256]{1,0:T(8,128)}, u32[]{:S(2)}, u32[]{:S(2)}) %collective-permute-start.32) | collective-permute-done | bytes 786464 | tf_op jit(solution)/shard_map/ppermute | solution.py:181
  470.5 31.9 %collective-permute-done.33 = f32[768,256]{1,0:T(8,128)} collective-permute-done((f32[768,256]{1,0:T(8,128)}, f32[768,256]{1,0:T(8,128)}, u32[]{:S(2)}, u32[]{:S(2)}) %collective-permute-start.33) | collective-permute-done | bytes 786464 | tf_op jit(solution)/shard_map/ppermute | solution.py:181
  514.9 10.5 %collective-permute-start.37 = (f32[2,128,256]{2,1,0:T(8,128)S(1)}, f32[2,128,256]{2,1,0:T(8,128)}, u32[]{:S(2)}, u32[]{:S(2)}) collective-permute-start(f32[2,128,256]{2,1,0:T(8,128)S(1)} %dynamic-slice_bitcast_fusion.7), channel_id=1, source_target_pairs={{0,8},{4,12},{8,0},{12,4},{16,24},{20,28},{24,16},{28,20},{1,9},{5... | collective-permute-start | bytes 786440 | tf_op jit(solution)/shard_map/ppermute | solution.py:160
  539.3 5.4 collective-permute-done.40
  562.2 6.9 %collective-permute-done.43 = f32[2,128,256]{2,1,0:T(8,128)S(1)} collective-permute-done((f32[2,128,256]{2,1,0:T(8,128)S(1)}, f32[2,128,256]{2,1,0:T(8,128)S(1)}, u32[]{:S(2)}, u32[]{:S(2)}) %collective-permute-start.43) | collective-permute-done | bytes 262176 | tf_op jit(solution)/shard_map/ppermute | solution.py:160
  (236 shorter events, 135.4 us)
Async XLA Ops:
  7.2 496.5 %reduce-scatter.5.cloned.1.call-start = ((), (), s32[]{:S(2)}) async-start(), calls=%async_computation.4 | async-start | bytes 3932160 | tf_op jit(solution)/shard_map/reduce_scatter | solution.py:218
  12.2 50.5 %collective-permute-start = (f32[768,256]{1,0:T(8,128)}, f32[768,256]{1,0:T(8,128)}, u32[]{:S(2)}, u32[]{:S(2)}) collective-permute-start(f32[768,256]{1,0:T(8,128)} %slice.30.refs_4_), channel_id=1, source_target_pairs={{0,16},{4,12},{8,24},{12,4},{16,0},{20,28},{24,8},{28,20},{1,17},{... | collective-permute-start | bytes 2359304 | tf_op jit(solution)/shard_map/ppermute | solution.py:148
  30.4 32.4 %collective-permute-start.2 = (f32[768,256]{1,0:T(8,128)}, f32[768,256]{1,0:T(8,128)}, u32[]{:S(2)}, u32[]{:S(2)}) collective-permute-start(f32[768,256]{1,0:T(8,128)} %collective-permute-done.1.refs_5_), channel_id=1, source_target_pairs={{0,16},{4,12},{8,24},{12,4},{16,0},{20,28},{24,8},{28,20},{1,17},{... | collective-permute-start | bytes 2359304 | tf_op jit(solution)/shard_map/ppermute | solution.py:148
  31.8 31.4 %collective-permute-start.5 = (f32[768,256]{1,0:T(8,128)}, f32[768,256]{1,0:T(8,128)}, u32[]{:S(2)}, u32[]{:S(2)}) collective-permute-start(f32[768,256]{1,0:T(8,128)} %slice.30.refs_4_), channel_id=1, source_target_pairs={{0,4},{4,0},{8,12},{12,8},{16,20},{20,16},{24,28},{28,24},{1,5},{5... | collective-permute-start | bytes 2359304 | tf_op jit(solution)/shard_map/ppermute | solution.py:148
  31.9 31.4 %collective-permute-start.6 = (f32[768,256]{1,0:T(8,128)}, f32[768,256]{1,0:T(8,128)}, u32[]{:S(2)}, u32[]{:S(2)}) collective-permute-start(f32[768,256]{1,0:T(8,128)} %collective-permute-done.1.refs_5_), channel_id=1, source_target_pairs={{0,4},{4,0},{8,12},{12,8},{16,20},{20,16},{24,28},{28,24},{1,5},{5... | collective-permute-start | bytes 2359304 | tf_op jit(solution)/shard_map/ppermute | solution.py:148
  62.7 22.1 %collective-permute-start.3 = (f32[768,256]{1,0:T(8,128)}, f32[768,256]{1,0:T(8,128)S(1)}, u32[]{:S(2)}, u32[]{:S(2)}) collective-permute-start(f32[768,256]{1,0:T(8,128)} %collective-permute-done.refs_2_), channel_id=1, source_target_pairs={{0,4},{4,0},{8,12},{12,8},{16,20},{20,16},{24,28},{28,24},{1,5},{5... | collective-permute-start | bytes 2359304 | tf_op jit(solution)/shard_map/ppermute | solution.py:148
  62.8 22.1 %collective-permute-start.4 = (f32[768,256]{1,0:T(8,128)}, f32[768,256]{1,0:T(8,128)S(1)}, u32[]{:S(2)}, u32[]{:S(2)}) collective-permute-start(f32[768,256]{1,0:T(8,128)} %collective-permute-done.2.refs_3_), channel_id=1, source_target_pairs={{0,4},{4,0},{8,12},{12,8},{16,20},{20,16},{24,28},{28,24},{1,5},{5... | collective-permute-start | bytes 2359304 | tf_op jit(solution)/shard_map/ppermute | solution.py:148
  106.1 419.2 %reduce-scatter.7.cloned.1.call-start = ((), (), s32[]{:S(2)}) async-start(), calls=%async_computation.5 | async-start | bytes 3932160 | tf_op jit(solution)/shard_map/reduce_scatter | solution.py:218
  138.5 30.8 %collective-permute-start.10 = (f32[768,256]{1,0:T(8,128)S(1)}, f32[768,256]{1,0:T(8,128)S(1)}, u32[]{:S(2)}, u32[]{:S(2)}) collective-permute-start(f32[768,256]{1,0:T(8,128)S(1)} %collective-permute-done.7.refs_2_), channel_id=1, source_target_pairs={{0,4},{4,0},{8,12},{12,8},{16,20},{20,16},{24,28},{28,24},{1,5},{5... | collective-permute-start | bytes 2359304 | tf_op jit(solution)/shard_map/ppermute | solution.py:148
  192.5 355.2 %reduce-scatter.9.cloned.1.call-start = ((), (), s32[]{:S(2)}) async-start(), calls=%async_computation.6 | async-start | bytes 3932160 | tf_op jit(solution)/shard_map/reduce_scatter | solution.py:218
  214.6 30.8 %collective-permute-start.17 = (f32[768,256]{1,0:T(8,128)S(1)}, f32[768,256]{1,0:T(8,128)S(1)}, u32[]{:S(2)}, u32[]{:S(2)}) collective-permute-start(f32[768,256]{1,0:T(8,128)S(1)} %collective-permute-done.14.refs_2_), channel_id=1, source_target_pairs={{0,4},{4,0},{8,12},{12,8},{16,20},{20,16},{24,28},{28,24},{1,5},{5... | collective-permute-start | bytes 2359304 | tf_op jit(solution)/shard_map/ppermute | solution.py:148
  268.5 284.7 %reduce-scatter.11.cloned.1.call-start = ((), (), s32[]{:S(2)}) async-start(), calls=%async_computation.7 | async-start | bytes 3932160 | tf_op jit(solution)/shard_map/reduce_scatter | solution.py:218
  271.5 43.0 %collective-permute-start.26 = (f32[768,256]{1,0:T(8,128)S(1)}, f32[768,256]{1,0:T(8,128)S(1)}, u32[]{:S(2)}, u32[]{:S(2)}) collective-permute-start(f32[768,256]{1,0:T(8,128)S(1)} %copy-done.1), channel_id=1, source_target_pairs={{0,4},{4,0},{8,12},{12,8},{16,20},{20,16},{24,28},{28,24},{1,5},{5... | collective-permute-start | bytes 2359304 | tf_op jit(solution)/shard_map/ppermute | solution.py:148
  271.5 46.3 %collective-permute-start.21 = (f32[768,256]{1,0:T(8,128)S(1)}, f32[768,256]{1,0:T(8,128)S(1)}, u32[]{:S(2)}, u32[]{:S(2)}) collective-permute-start(f32[768,256]{1,0:T(8,128)S(1)} %copy-done.1), channel_id=1, source_target_pairs={{0,16},{4,12},{8,24},{12,4},{16,0},{20,28},{24,8},{28,20},{1,17},{... | collective-permute-start | bytes 2359304 | tf_op jit(solution)/shard_map/ppermute | solution.py:148
  289.3 28.9 %collective-permute-start.23 = (f32[768,256]{1,0:T(8,128)S(1)}, f32[768,256]{1,0:T(8,128)S(1)}, u32[]{:S(2)}, u32[]{:S(2)}) collective-permute-start(f32[768,256]{1,0:T(8,128)S(1)} %collective-permute-done.22.refs_5_), channel_id=1, source_target_pairs={{0,16},{4,12},{8,24},{12,4},{16,0},{20,28},{24,8},{28,20},{1,17},{... | collective-permute-start | bytes 2359304 | tf_op jit(solution)/shard_map/ppermute | solution.py:148
  290.5 28.0 %collective-permute-start.27 = (f32[768,256]{1,0:T(8,128)S(1)}, f32[768,256]{1,0:T(8,128)S(1)}, u32[]{:S(2)}, u32[]{:S(2)}) collective-permute-start(f32[768,256]{1,0:T(8,128)S(1)} %collective-permute-done.22.refs_5_), channel_id=1, source_target_pairs={{0,4},{4,0},{8,12},{12,8},{16,20},{20,16},{24,28},{28,24},{1,5},{5... | collective-permute-start | bytes 2359304 | tf_op jit(solution)/shard_map/ppermute | solution.py:148
  304.1 68.6 %collective-permute-start.28 = (f32[768,256]{1,0:T(8,128)}, f32[768,256]{1,0:T(8,128)}, u32[]{:S(2)}, u32[]{:S(2)}) collective-permute-start(f32[768,256]{1,0:T(8,128)} %get-tuple-element.30), channel_id=1, source_target_pairs={{0,0},{1,1},{2,2},{3,3},{4,4},{5,5},{6,6},{7,7},{8,9},{9,8},{10,11... | collective-permute-start | bytes 2359304 | tf_op jit(solution)/shard_map/ppermute | solution.py:181
  314.5 65.7 %collective-permute-start.30 = (f32[768,256]{1,0:T(8,128)}, f32[768,256]{1,0:T(8,128)}, u32[]{:S(2)}, u32[]{:S(2)}) collective-permute-start(f32[768,256]{1,0:T(8,128)} %select_select_fusion.2), channel_id=1, source_target_pairs={{0,1},{1,0},{2,3},{3,2},{4,5},{5,4},{6,7},{7,6},{8,8},{9,9},{10,10... | collective-permute-start | bytes 2359304 | tf_op jit(solution)/shard_map/ppermute | solution.py:181
  365.1 98.7 %collective-permute-start.32 = (f32[768,256]{1,0:T(8,128)S(1)}, f32[768,256]{1,0:T(8,128)}, u32[]{:S(2)}, u32[]{:S(2)}) collective-permute-start(f32[768,256]{1,0:T(8,128)S(1)} %select_select_fusion.1), channel_id=1, source_target_pairs={{0,2},{1,3},{2,0},{3,1},{4,6},{5,7},{6,4},{7,5},{8,11},{9,10},{10,... | collective-permute-start | bytes 2359304 | tf_op jit(solution)/shard_map/ppermute | solution.py:181
  370.5 95.3 %collective-permute-start.34 = (f32[768,256]{1,0:T(8,128)S(1)}, f32[768,256]{1,0:T(8,128)}, u32[]{:S(2)}, u32[]{:S(2)}) collective-permute-start(f32[768,256]{1,0:T(8,128)S(1)} %select_select_fusion), channel_id=1, source_target_pairs={{0,3},{1,2},{2,1},{3,0},{4,7},{5,6},{6,5},{7,4},{8,10},{9,11},{10,... | collective-permute-start | bytes 2359304 | tf_op jit(solution)/shard_map/ppermute | solution.py:181
  372.8 95.2 %collective-permute-start.29 = (f32[768,256]{1,0:T(8,128)}, f32[768,256]{1,0:T(8,128)}, u32[]{:S(2)}, u32[]{:S(2)}) collective-permute-start(f32[768,256]{1,0:T(8,128)} %collective-permute-done.28), channel_id=1, source_target_pairs={{0,0},{1,9},{2,18},{3,27},{4,4},{5,13},{6,22},{7,31},{8,8},{9,1},{... | collective-permute-start | bytes 2359304 | tf_op jit(solution)/shard_map/ppermute | solution.py:181
  380.2 89.1 %collective-permute-start.31 = (f32[768,256]{1,0:T(8,128)}, f32[768,256]{1,0:T(8,128)}, u32[]{:S(2)}, u32[]{:S(2)}) collective-permute-start(f32[768,256]{1,0:T(8,128)} %collective-permute-done.30), channel_id=1, source_target_pairs={{0,8},{1,1},{2,26},{3,19},{4,12},{5,5},{6,30},{7,23},{8,0},{9,9},{... | collective-permute-start | bytes 2359304 | tf_op jit(solution)/shard_map/ppermute | solution.py:181
  463.9 38.5 %collective-permute-start.33 = (f32[768,256]{1,0:T(8,128)}, f32[768,256]{1,0:T(8,128)}, u32[]{:S(2)}, u32[]{:S(2)}) collective-permute-start(f32[768,256]{1,0:T(8,128)} %collective-permute-done.32), channel_id=1, source_target_pairs={{0,16},{1,25},{2,2},{3,11},{4,20},{5,29},{6,6},{7,15},{8,24},{9,17... | collective-permute-start | bytes 2359304 | tf_op jit(solution)/shard_map/ppermute | solution.py:181
  465.8 37.9 %collective-permute-start.35 = (f32[768,256]{1,0:T(8,128)}, f32[768,256]{1,0:T(8,128)}, u32[]{:S(2)}, u32[]{:S(2)}) collective-permute-start(f32[768,256]{1,0:T(8,128)} %collective-permute-done.34), channel_id=1, source_target_pairs={{0,24},{1,17},{2,10},{3,3},{4,28},{5,21},{6,14},{7,7},{8,16},{9,25... | collective-permute-start | bytes 2359304 | tf_op jit(solution)/shard_map/ppermute | solution.py:181
  (77 other events, 897.0 us)
Sparse Core Ops, SparseCore 0:
  106.2 61.4 reduce-scatter.4
  192.6 61.3 reduce-scatter.6
  268.7 68.0 reduce-scatter.8
  361.9 107.7 reduce-scatter.10

commit v4 on v2

v4 whole, which is shorter than its diff:
```python
import functools

import jax
import jax.numpy as jnp
import numpy as np
from jax import lax
from jax.experimental import pallas as pl
from jax.experimental.pallas import tpu as pltpu
from jax.sharding import PartitionSpec as P

CHUNKS = 4
LANES = 128
MIB = 1 << 20


def split(value):
    high = value.astype(jnp.bfloat16)
    low = (value - high.astype(jnp.float32)).astype(jnp.bfloat16)
    return high, low


def largest_divisor(extent, unit, limit):
    return max(d for d in range(unit, min(extent, limit) + 1, unit) if extent % d == 0)


def product_kernel(count, place_ref, *refs):
    del place_ref
    a_refs, pieces, sums, (out_ref, both_ref) = refs[:count], refs[count : 2 * count], refs[2 * count : -2], refs[-2:]
    columns = out_ref.shape[1]

    @pl.when(pl.program_id(0) == 0)
    def _():
        for slot, piece in enumerate(pieces):
            both_ref[slot, :, :columns], both_ref[slot, :, columns:] = split(-piece[...])

    dot = functools.partial(jnp.dot, preferred_element_type=jnp.float32)
    extent = largest_divisor(out_ref.shape[0], 16, 256)
    for first in range(0, out_ref.shape[0], extent):
        rows = pl.ds(first, extent)
        wide = narrow = None
        for slot in range(count):
            high, low = split(a_refs[slot][rows, :])
            terms = dot(high, both_ref[slot]), dot(low, both_ref[slot, :, :columns])
            wide, narrow = terms if wide is None else (wide + terms[0], narrow + terms[1])
        total = wide[:, :columns] + (wide[:, columns:] + narrow)
        out_ref[rows, :] = total + sums[0][rows, :] if sums else total


def negative_product(a, pieces, place, sums=None):
    rows = a.shape[0]
    count = len(pieces)
    depth, columns = pieces[0].shape
    tile = largest_divisor(rows, 16, 512)
    out_spec = pl.BlockSpec((tile, columns), lambda i, _: (i, 0))
    a_specs = [pl.BlockSpec((tile, depth), lambda i, place, slot=slot: (i, place[slot])) for slot in range(count)]
    whole = [pl.BlockSpec(piece.shape, lambda i, _: (0, 0), pipeline_mode=pl.Buffered(1)) for piece in pieces]
    given = [] if sums is None else [sums]
    return pl.pallas_call(
        functools.partial(product_kernel, count),
        grid_spec=pltpu.PrefetchScalarGridSpec(
            num_scalar_prefetch=1,
            grid=(rows // tile,),
            in_specs=a_specs + whole + [out_spec] * len(given),
            out_specs=out_spec,
            scratch_shapes=[pltpu.VMEM((count, depth, 2 * columns), jnp.bfloat16)],
        ),
        out_shape=jax.ShapeDtypeStruct((rows, columns), jnp.float32),
        compiler_params=pltpu.CompilerParams(vmem_limit_bytes=32 * MIB, dimension_semantics=("arbitrary",)),
        cost_estimate=pl.CostEstimate(
            flops=6 * rows * depth * count * columns,
            bytes_accessed=4 * (rows * depth * count + depth * count * columns + 2 * rows * columns),
            transcendentals=0,
        ),
    )(place, *[a] * count, *pieces, *given)


def gather_orders(count):
    masks = [1 << b for b in range(1, count.bit_length() - 1)]
    return list(zip(masks, masks[::-1]))


def gather_places(count):
    held = [[i] for i in range(count)]
    for masks in gather_orders(count):
        held = [held[i] + held[i ^ masks[i & 1]] for i in range(count)]
    half = count // 4
    both = [
        held[i][:half] + held[i ^ 1][:half] + held[i][half:] + held[i ^ 1][half:] for i in range(count)
    ]
    return np.array(both, np.int32)


def after(value, *others):
    return lax.optimization_barrier((value, *others))[0]


def cross(pieces, masks, count):
    pairs = [(i, i ^ masks[i & 1]) for i in range(count)]
    return [lax.ppermute(piece, "row", pairs) for piece in pieces]


def sum_over_row(value, count):
    rows, columns = value.shape
    me = lax.axis_index("row")
    value = value.reshape((2,) * (count.bit_length() - 1) + (rows // count, columns))
    for bit in range(count.bit_length() - 1):
        axis = value.ndim - 3
        mine = (me >> bit) & 1
        keep = lax.dynamic_index_in_dim(value, mine, axis, keepdims=False)
        send = lax.dynamic_index_in_dim(value, 1 - mine, axis, keepdims=False)
        value = keep + lax.ppermute(send, "row", [(i, i ^ (1 << bit)) for i in range(count)])
    return value


def sum_over_col(value, count):
    me = lax.axis_index("col")
    width = value.shape[1] // count
    total = lax.dynamic_slice_in_dim(value, me * width, width, 1)
    for shift in range(1, count):
        send = lax.dynamic_slice_in_dim(value, (me + shift) % count * width, width, 1)
        total = total + lax.ppermute(send, "col", [(i, (i + shift) % count) for i in range(count)])
    return total


def move(value, target):
    row_count, column_count = lax.axis_size("row"), lax.axis_size("col")
    pairs = []
    for r in range(row_count):
        for c in range(column_count):
            to_row, to_column = target(r, c)
            pairs.append((r * column_count + c, to_row * column_count + to_column))
    return lax.ppermute(value, ("row", "col"), pairs)


def shards(parent_inverse, panel, saved_diag):
    row_count, column_count = lax.axis_size("row"), lax.axis_size("col")
    row_index, column_index = lax.axis_index("row"), lax.axis_index("col")
    group = row_count // column_count
    block_rows = panel.shape[0]
    width = panel.shape[1] // CHUNKS
    stepwise = block_rows % LANES == 0
    orders = gather_orders(row_count)
    places = gather_places(row_count)
    place = jnp.asarray(places)[row_index]
    slots = jnp.asarray(np.argsort(places, axis=1).astype(np.int32))[row_index]

    def cut(chunk):
        return lax.slice_in_dim(panel, chunk * width, (chunk + 1) * width, axis=1)

    def partner(pieces):
        return cross(pieces, (1, 1), row_count)

    def all_after(pieces, *others):
        return [after(piece, *others) for piece in pieces]

    def turn(chunk):
        return chunk * 2 % column_count + chunk * 2 // column_count

    def spread(chunk, select):
        wanted = row_index % group * column_count + (column_index ^ (row_index // group) ^ turn(chunk))
        return move(select(wanted), lambda r, c: (r, c ^ (r // group) ^ turn(chunk)))

    def hop(value, chunk):
        return move(value, lambda r, c: (((r // group) ^ c ^ turn(chunk)) * group + r % group, c))

    def summed(partial_block, *others):
        return lax.psum_scatter(after(partial_block, *others), "col", scatter_dimension=0, tiled=True)

    products, blocks, moved = [], [], []
    if stepwise:
        half = row_count // 2

        def link(pieces, orders):
            for masks in orders:
                pieces = pieces + cross(pieces, masks, row_count)
            return pieces

        mine = [link([cut(0)], orders[:-1])] + [None] * (CHUNKS - 1)
        theirs = [partner(all_after(mine[0], mine[0][-1]))] + [None] * (CHUNKS - 1)
        late = [cross(all_after(mine[0], theirs[0][-1]), orders[-1], row_count)] + [None] * (CHUNKS - 1)
        mine[1] = link(all_after([cut(1)], late[0][-1]), orders[:-1])
        last = None
        for chunk in range(CHUNKS):
            if chunk == 1:
                theirs[1] = partner(all_after(mine[1], last))
                late[1] = cross(all_after(mine[1], theirs[1][-1]), orders[-1], row_count)
            if 1 <= chunk < CHUNKS - 1:
                mine[chunk + 1] = link(all_after([cut(chunk + 1)], last), orders[:-1])
            first = mine[chunk] + theirs[chunk]
            waits = moved[-1:]
            last = negative_product(after(parent_inverse, *waits) if waits else parent_inverse, first, place[:half])
            second = late[chunk] + partner(late[chunk])
            if 1 <= chunk < CHUNKS - 1:
                theirs[chunk + 1] = partner(all_after(mine[chunk + 1], last))
                late[chunk + 1] = cross(all_after(mine[chunk + 1], last), orders[-1], row_count)
            moved.append(spread(chunk, lambda wanted: lax.select_n(slots[wanted], *first, *second)))
            last = negative_product(parent_inverse, second, place[half:], last)
            products.append(last)
            if chunk == 0:
                waits = mine[1][-1:]
            elif chunk < CHUNKS - 1:
                waits = theirs[chunk + 1] + late[chunk + 1]
            else:
                waits = []
            blocks.append(summed(last, *waits))
        moved = [hop(after(value, products[-2]), chunk) for chunk, value in enumerate(moved)]
    else:
        for chunk in range(CHUNKS):
            whole = lax.all_gather(cut(chunk), "row", axis=0, tiled=True)
            part = spread(chunk, lambda wanted: lax.dynamic_slice_in_dim(whole, wanted * block_rows, block_rows, 0))
            moved.append(hop(part, chunk))
            products.append(negative_product(parent_inverse, [whole], jnp.zeros((1,), jnp.int32)))
            blocks.append(summed(products[-1]))
    own_rows = jnp.concatenate(moved, axis=1)
    grams = []
    for chunk, block in enumerate(blocks):
        waits = [products[-1]] if chunk < CHUNKS - 1 else grams
        gram = lax.dot_general(
            own_rows,
            after(block, *waits),
            (((0,), (0,)), ((), ())),
            precision=lax.Precision.HIGH,
            preferred_element_type=jnp.float32,
        )
        grams.append(sum_over_row(gram, row_count))
    offdiag_block = jnp.concatenate(blocks, axis=1)
    diag_block = saved_diag - sum_over_col(jnp.concatenate(grams, axis=1), column_count)
    return offdiag_block, diag_block


def solution(mesh):
    in_specs = (P("row", "col"), P(("col", "row"), None), P("row", "col"))
    out_specs = (P(("row", "col"), None), P("row", "col"))
    return jax.shard_map(shards, mesh=mesh, in_specs=in_specs, out_specs=out_specs, check_vma=False)
```

time: 621 us -> 639 us (1.029)
  Pallas kernels: 210 us -> 172 us
  starting transfers between devices: 102 us -> 133 us
  waiting for transfers between devices: 222 us -> 237 us
    ppermute x8, waiting for transfers between devices: 78.3 us -> 142 us  [move(): return lax.ppermute(value, ('row', 'col'), pairs)]
    ppermute x28, waiting for transfers between devices: 113 us -> 49.6 us  [cross(): return [lax.ppermute(piece, 'row', pairs) for piece in pieces]]
    ppermute x28, starting transfers between devices: 17.9 us -> 71.5 us  [cross(): return [lax.ppermute(piece, 'row', pairs) for piece in pieces]]
    pallas_call x8, Pallas kernels: 210 us -> 172 us  [negative_product(): pl.pallas_call(functools.partial(product_kernel, count), grid_spec=pltpu....]
    ppermute x8, starting transfers between devices: 68.3 us -> 47.3 us  [move(): return lax.ppermute(value, ('row', 'col'), pairs)]
    ppermute x12, waiting for transfers between devices: 24.6 us -> 39.7 us  [sum_over_row(): lax.ppermute(send, 'row', [(i, i ^ 1 << bit) for i in range(count)])]
    unnamed x47 -> x57, local copies, waits for them, and re-layouts: 10.2 us -> 13.5 us
  transfers between devices with their start and end apart: 55 -> 55, of which waited for: 19 -> 20; matrix products, arithmetic and copies ran while one was open for 7% -> 6% of each run, Pallas kernels for 30% -> 27%
where the time goes in v4:
time: 639 us; the launch traced here: 632 us
  waiting for transfers between devices  237 us (37%)
  Pallas kernels  172 us (27%)
  starting transfers between devices  133 us (21%)
  between operations  33.1 us (5%)
  local copies, waits for them, and re-layouts  20.8 us (3%)
  other arithmetic  20.8 us (3%)
  matrix products  15.2 us (2%)
    pallas_call x8, Pallas kernels, negative_product(): pl.pallas_call(functools.partial(product_kernel, count), grid_spec=pltpu....  172 us
    ppermute x8, waiting for transfers between devices, move(): return lax.ppermute(value, ('row', 'col'), pairs)  142 us
    ppermute x28, starting transfers between devices, cross(): return [lax.ppermute(piece, 'row', pairs) for piece in pieces]  71.5 us
    ppermute x28, waiting for transfers between devices, cross(): return [lax.ppermute(piece, 'row', pairs) for piece in pieces]  49.6 us
    ppermute x8, starting transfers between devices, move(): return lax.ppermute(value, ('row', 'col'), pairs)  47.3 us
    ppermute x12, waiting for transfers between devices, sum_over_row(): lax.ppermute(send, 'row', [(i, i ^ 1 << bit) for i in range(count)])  39.7 us
    dot_general x4, matrix products, shards(): lax.dot_general(own_rows, after(block, *waits), (((0,), (0,)), ((), ())),...  15.2 us
    unnamed x57, local copies, waits for them, and re-layouts  13.5 us
  transfers between devices with their start and end apart: 55, of which 20 were waited for; matrix products, arithmetic and copies ran while one was open for 6% of the time, Pallas kernels for 27%

profile of v4, /device:TPU:0, one launch (start us, length us, event | category | flops | bytes accessed | tf_op | source)
XLA Modules:
  0.0 632.3 jit_solution(6861875292562101201)
XLA Ops:
  11.4 10.0 %collective-permute-done.refs_5_ = f32[768,256]{1,0:T(8,128)S(1)} collective-permute-done((f32[768,256]{1,0:T(8,128)S(1)}, f32[768,256]{1,0:T(8,128)S(1)}, u32[]{:S(2)}, u32[]{:S(2)}) %collective-permute-start) | collective-permute-done | bytes 786464 | tf_op jit(solution)/shard_map/ppermute | solution.py:99
  36.6 8.4 %collective-permute-done.3.refs_5_ = f32[768,256]{1,0:T(8,128)S(1)} collective-permute-done((f32[768,256]{1,0:T(8,128)S(1)}, f32[768,256]{1,0:T(8,128)S(1)}, u32[]{:S(2)}, u32[]{:S(2)}) %collective-permute-start.3) | collective-permute-done | bytes 786464 | tf_op jit(solution)/shard_map/ppermute | solution.py:99
  46.4 21.1 %shard_map.68.refs_8_ = f32[3072,256]{1,0:T(8,128)S(1)} custom-call(s32[4]{0:T(128)S(1)} %get-tuple-element.71.place_ref, f32[3072,6144]{1,0:T(8,128)} %refs_3_.12, f32[3072,6144]{1,0:T(8,128)} %refs_3_.12, f32[3072,6144]{1,0:T(8,128)} %refs_3_.12, f32[3072,6144]{1,0:T(8,128)} %refs_3_.12, f32[768,256]{1,0:T(8,128)S(1)} %slice.32.refs_4_, ...), custom_call_target="tpu_custom_call" | custom-call | flops 14495514624 | bytes 47185920 | tf_op jit(solution)/shard_map/pallas_call | solution.py:58
  72.6 21.4 %shard_map.69 = f32[3072,256]{1,0:T(8,128)} custom-call(s32[4]{0:T(128)S(1)} %get-tuple-element.72.place_ref, f32[3072,6144]{1,0:T(8,128)} %refs_3_.12, f32[3072,6144]{1,0:T(8,128)} %refs_3_.12, f32[3072,6144]{1,0:T(8,128)} %refs_3_.12, f32[3072,6144]{1,0:T(8,128)} %refs_3_.12, f32[768,256]{1,0:T(8,128)S(1)} %collective-permute-done.2.refs_4_, ...), custom_call_target="tpu_custom_call" | custom-call | flops 14495514624 | bytes 47185920 | tf_op jit(solution)/shard_map/pallas_call | solution.py:58
  102.5 15.4 %collective-permute-done.9.refs_4_ = f32[768,256]{1,0:T(8,128)S(1)} collective-permute-done((f32[768,256]{1,0:T(8,128)S(1)}, f32[768,256]{1,0:T(8,128)S(1)}, u32[]{:S(2)}, u32[]{:S(2)}) %collective-permute-start.9) | collective-permute-done | bytes 786464 | tf_op jit(solution)/shard_map/ppermute | solution.py:99
  117.9 10.3 %collective-permute-done.10.refs_5_ = f32[768,256]{1,0:T(8,128)S(1)} collective-permute-done((f32[768,256]{1,0:T(8,128)}, f32[768,256]{1,0:T(8,128)S(1)}, u32[]{:S(2)}, u32[]{:S(2)}) %collective-permute-start.10) | collective-permute-done | bytes 786464 | tf_op jit(solution)/shard_map/ppermute | solution.py:99
  128.3 20.9 %shard_map.70.refs_8_ = f32[3072,256]{1,0:T(8,128)S(1)} custom-call(s32[4]{0:T(128)S(1)} %get-tuple-element.71.place_ref, f32[3072,6144]{1,0:T(8,128)} %refs_3_.12, f32[3072,6144]{1,0:T(8,128)} %refs_3_.12, f32[3072,6144]{1,0:T(8,128)} %refs_3_.12, f32[3072,6144]{1,0:T(8,128)} %refs_3_.12, f32[768,256]{1,0:T(8,128)S(1)} %get-tuple-element.41.refs_4_, ...), custom_call_target="tpu_custom_call" | custom-call | flops 14495514624 | bytes 47185920 | tf_op jit(solution)/shard_map/pallas_call | solution.py:58
  149.2 49.7 %collective-permute-start.18 = (f32[768,256]{1,0:T(8,128)S(1)}, f32[768,256]{1,0:T(8,128)S(1)}, u32[]{:S(2)}, u32[]{:S(2)}) collective-permute-start(f32[768,256]{1,0:T(8,128)S(1)} %get-tuple-element.43.refs_4_), channel_id=1, source_target_pairs={{0,16},{4,12},{8,24},{12,4},{16,0},{20,28},{24,8},{28,20},{1,17},{... | collective-permute-start | bytes 2359304 | tf_op jit(solution)/shard_map/ppermute | solution.py:99
  199.5 21.4 %shard_map.71 = f32[3072,256]{1,0:T(8,128)} custom-call(s32[4]{0:T(128)S(1)} %get-tuple-element.72.place_ref, f32[3072,6144]{1,0:T(8,128)} %refs_3_.12, f32[3072,6144]{1,0:T(8,128)} %refs_3_.12, f32[3072,6144]{1,0:T(8,128)} %refs_3_.12, f32[3072,6144]{1,0:T(8,128)} %refs_3_.12, f32[768,256]{1,0:T(8,128)S(1)} %collective-permute-done.9.refs_4_, ...), custom_call_target="tpu_custom_call" | custom-call | flops 14495514624 | bytes 47185920 | tf_op jit(solution)/shard_map/pallas_call | solution.py:58
  233.2 5.2 collective-permute-start.24
  238.4 71.8 %collective-permute-done.22 = f32[768,256]{1,0:T(8,128)} collective-permute-done((f32[768,256]{1,0:T(8,128)S(1)}, f32[768,256]{1,0:T(8,128)}, u32[]{:S(2)}, u32[]{:S(2)}) %collective-permute-start.22) | collective-permute-done | bytes 786464 | tf_op jit(solution)/shard_map/ppermute | solution.py:132
  310.2 21.1 %shard_map.72.refs_8_ = f32[3072,256]{1,0:T(8,128)S(1)} custom-call(s32[4]{0:T(128)S(1)} %get-tuple-element.71.place_ref, f32[3072,6144]{1,0:T(8,128)} %refs_3_.12, f32[3072,6144]{1,0:T(8,128)} %refs_3_.12, f32[3072,6144]{1,0:T(8,128)} %refs_3_.12, f32[3072,6144]{1,0:T(8,128)} %refs_3_.12, f32[768,256]{1,0:T(8,128)S(1)} %get-tuple-element.43.refs_4_, ...), custom_call_target="tpu_custom_call" | custom-call | flops 14495514624 | bytes 47185920 | tf_op jit(solution)/shard_map/pallas_call | solution.py:58
  333.4 22.1 %shard_map.73 = f32[3072,256]{1,0:T(8,128)} custom-call(s32[4]{0:T(128)S(1)} %get-tuple-element.72.place_ref, f32[3072,6144]{1,0:T(8,128)} %refs_3_.12, f32[3072,6144]{1,0:T(8,128)} %refs_3_.12, f32[3072,6144]{1,0:T(8,128)} %refs_3_.12, f32[3072,6144]{1,0:T(8,128)} %refs_3_.12, f32[768,256]{1,0:T(8,128)S(1)} %copy-done.2, ...), custom_call_target="tpu_custom_call" | custom-call | flops 14495514624 | bytes 47185920 | tf_op jit(solution)/shard_map/pallas_call | solution.py:58
  370.5 7.4 %collective-permute-start.31 = (f32[768,256]{1,0:T(8,128)}, f32[768,256]{1,0:T(8,128)}, u32[]{:S(2)}, u32[]{:S(2)}) collective-permute-start(f32[768,256]{1,0:T(8,128)} %collective-permute-done.13), channel_id=1, source_target_pairs={{0,0},{1,9},{2,18},{3,27},{4,4},{5,13},{6,22},{7,31},{8,8},{9,1},{... | collective-permute-start | bytes 2359304 | tf_op jit(solution)/shard_map/ppermute | solution.py:132
  377.9 42.0 %collective-permute-done.30 = f32[768,256]{1,0:T(8,128)} collective-permute-done((f32[768,256]{1,0:T(8,128)S(1)}, f32[768,256]{1,0:T(8,128)}, u32[]{:S(2)}, u32[]{:S(2)}) %collective-permute-start.30) | collective-permute-done | bytes 786464 | tf_op jit(solution)/shard_map/ppermute | solution.py:132
  420.4 21.3 %shard_map.74.refs_8_ = f32[3072,256]{1,0:T(8,128)S(1)} custom-call(s32[4]{0:T(128)S(1)} %get-tuple-element.71.place_ref, f32[3072,6144]{1,0:T(8,128)} %refs_3_.12, f32[3072,6144]{1,0:T(8,128)} %refs_3_.12, f32[3072,6144]{1,0:T(8,128)} %refs_3_.12, f32[3072,6144]{1,0:T(8,128)} %refs_3_.12, f32[768,256]{1,0:T(8,128)S(1)} %copy-done, ...), custom_call_target="tpu_custom_call" | custom-call | flops 14495514624 | bytes 47185920 | tf_op jit(solution)/shard_map/pallas_call | solution.py:58
  447.4 22.3 %shard_map.75 = f32[3072,256]{1,0:T(8,128)} custom-call(s32[4]{0:T(128)S(1)} %get-tuple-element.72.place_ref, f32[3072,6144]{1,0:T(8,128)} %refs_3_.12, f32[3072,6144]{1,0:T(8,128)} %refs_3_.12, f32[3072,6144]{1,0:T(8,128)} %refs_3_.12, f32[3072,6144]{1,0:T(8,128)} %refs_3_.12, f32[768,256]{1,0:T(8,128)} %collective-permute-done.26.refs_4_, ...), custom_call_target="tpu_custom_call" | custom-call | flops 14495514624 | bytes 47185920 | tf_op jit(solution)/shard_map/pallas_call | solution.py:58
  469.7 25.0 %collective-permute-start.32 = (f32[768,256]{1,0:T(8,128)}, f32[768,256]{1,0:T(8,128)}, u32[]{:S(2)}, u32[]{:S(2)}) collective-permute-start(f32[768,256]{1,0:T(8,128)} %collective-permute-done.22), channel_id=1, source_target_pairs={{0,16},{1,25},{2,2},{3,11},{4,20},{5,29},{6,6},{7,15},{8,24},{9,17... | collective-permute-start | bytes 2359304 | tf_op jit(solution)/shard_map/ppermute | solution.py:132
  501.5 10.9 %collective-permute-done.32 = f32[768,256]{1,0:T(8,128)} collective-permute-done((f32[768,256]{1,0:T(8,128)}, f32[768,256]{1,0:T(8,128)}, u32[]{:S(2)}, u32[]{:S(2)}) %collective-permute-start.32) | collective-permute-done | bytes 786464 | tf_op jit(solution)/shard_map/ppermute | solution.py:132
  518.6 13.7 %collective-permute-done.35 = f32[768,256]{1,0:T(8,128)} collective-permute-done((f32[768,256]{1,0:T(8,128)}, f32[768,256]{1,0:T(8,128)}, u32[]{:S(2)}, u32[]{:S(2)}) %collective-permute-start.35) | collective-permute-done | bytes 786464 | tf_op jit(solution)/shard_map/ppermute | solution.py:132
  544.4 7.8 %collective-permute-done.37 = f32[2,128,256]{2,1,0:T(8,128)} collective-permute-done((f32[2,128,256]{2,1,0:T(8,128)S(1)}, f32[2,128,256]{2,1,0:T(8,128)}, u32[]{:S(2)}, u32[]{:S(2)}) %collective-permute-start.37) | collective-permute-done | bytes 262176 | tf_op jit(solution)/shard_map/ppermute | solution.py:111
  569.5 6.9 %collective-permute-done.40 = f32[2,128,256]{2,1,0:T(8,128)S(1)} collective-permute-done((f32[2,128,256]{2,1,0:T(8,128)S(1)}, f32[2,128,256]{2,1,0:T(8,128)S(1)}, u32[]{:S(2)}, u32[]{:S(2)}) %collective-permute-start.40) | collective-permute-done | bytes 262176 | tf_op jit(solution)/shard_map/ppermute | solution.py:111
  593.7 7.6 %collective-permute-done.46 = f32[2,128,256]{2,1,0:T(8,128)S(1)} collective-permute-done((f32[2,128,256]{2,1,0:T(8,128)S(1)}, f32[2,128,256]{2,1,0:T(8,128)S(1)}, u32[]{:S(2)}, u32[]{:S(2)}) %collective-permute-start.46) | collective-permute-done | bytes 262176 | tf_op jit(solution)/shard_map/ppermute | solution.py:111
  618.8 5.9 collective-permute-done.49
  (196 shorter events, 129.5 us)
Async XLA Ops:
  7.2 511.5 %reduce-scatter.5.cloned.1.call-start = ((), (), s32[]{:S(2)}) async-start(), calls=%async_computation.4 | async-start | bytes 3932160 | tf_op jit(solution)/shard_map/reduce_scatter | solution.py:167
  36.6 31.0 %collective-permute-start.4 = (f32[768,256]{1,0:T(8,128)S(1)}, f32[768,256]{1,0:T(8,128)S(1)}, u32[]{:S(2)}, u32[]{:S(2)}) collective-permute-start(f32[768,256]{1,0:T(8,128)S(1)} %collective-permute-done.2.refs_4_), channel_id=1, source_target_pairs={{0,4},{4,0},{8,12},{12,8},{16,20},{20,16},{24,28},{28,24},{1,5},{5... | collective-permute-start | bytes 2359304 | tf_op jit(solution)/shard_map/ppermute | solution.py:99
  94.0 460.9 %reduce-scatter.7.cloned.1.call-start = ((), (), s32[]{:S(2)}) async-start(), calls=%async_computation.5 | async-start | bytes 3932160 | tf_op jit(solution)/shard_map/reduce_scatter | solution.py:167
  101.4 26.8 %collective-permute-start.10 = (f32[768,256]{1,0:T(8,128)}, f32[768,256]{1,0:T(8,128)S(1)}, u32[]{:S(2)}, u32[]{:S(2)}) collective-permute-start(f32[768,256]{1,0:T(8,128)} %collective-permute-done.7.refs_5_), channel_id=1, source_target_pairs={{0,16},{4,12},{8,24},{12,4},{16,0},{20,28},{24,8},{28,20},{1,17},{... | collective-permute-start | bytes 2359304 | tf_op jit(solution)/shard_map/ppermute | solution.py:99
  101.5 26.8 %collective-permute-start.14 = (f32[768,256]{1,0:T(8,128)S(1)}, f32[768,256]{1,0:T(8,128)S(1)}, u32[]{:S(2)}, u32[]{:S(2)}) collective-permute-start(f32[768,256]{1,0:T(8,128)S(1)} %get-tuple-element.41.refs_4_), channel_id=1, source_target_pairs={{0,4},{4,0},{8,12},{12,8},{16,20},{20,16},{24,28},{28,24},{1,5},{5... | collective-permute-start | bytes 2359304 | tf_op jit(solution)/shard_map/ppermute | solution.py:99
  101.5 97.5 %collective-permute-start.16 = (f32[768,256]{1,0:T(8,128)S(1)}, f32[768,256]{1,0:T(8,128)S(1)}, u32[]{:S(2)}, u32[]{:S(2)}) collective-permute-start(f32[768,256]{1,0:T(8,128)S(1)} %get-tuple-element.43.refs_4_), channel_id=1, source_target_pairs={{0,8},{4,20},{8,0},{12,28},{16,24},{20,4},{24,16},{28,12},{1,9},{5... | collective-permute-start | bytes 2359304 | tf_op jit(solution)/shard_map/ppermute | solution.py:99
  117.9 81.2 %collective-permute-start.11 = (f32[768,256]{1,0:T(8,128)S(1)}, f32[768,256]{1,0:T(8,128)S(1)}, u32[]{:S(2)}, u32[]{:S(2)}) collective-permute-start(f32[768,256]{1,0:T(8,128)S(1)} %collective-permute-done.9.refs_4_), channel_id=1, source_target_pairs={{0,4},{4,0},{8,12},{12,8},{16,20},{20,16},{24,28},{28,24},{1,5},{5... | collective-permute-start | bytes 2359304 | tf_op jit(solution)/shard_map/ppermute | solution.py:99
  128.2 71.3 %collective-permute-start.12 = (f32[768,256]{1,0:T(8,128)S(1)}, f32[768,256]{1,0:T(8,128)S(1)}, u32[]{:S(2)}, u32[]{:S(2)}) collective-permute-start(f32[768,256]{1,0:T(8,128)S(1)} %collective-permute-done.10.refs_5_), channel_id=1, source_target_pairs={{0,4},{4,0},{8,12},{12,8},{16,20},{20,16},{24,28},{28,24},{1,5},{5... | collective-permute-start | bytes 2359304 | tf_op jit(solution)/shard_map/ppermute | solution.py:99
  149.2 73.6 %collective-permute-start.18 = (f32[768,256]{1,0:T(8,128)S(1)}, f32[768,256]{1,0:T(8,128)S(1)}, u32[]{:S(2)}, u32[]{:S(2)}) collective-permute-start(f32[768,256]{1,0:T(8,128)S(1)} %get-tuple-element.43.refs_4_), channel_id=1, source_target_pairs={{0,16},{4,12},{8,24},{12,4},{16,0},{20,28},{24,8},{28,20},{1,17},{... | collective-permute-start | bytes 2359304 | tf_op jit(solution)/shard_map/ppermute | solution.py:99
  222.8 337.8 %reduce-scatter.9.cloned.1.call-start = ((), (), s32[]{:S(2)}) async-start(), calls=%async_computation.6 | async-start | bytes 3932160 | tf_op jit(solution)/shard_map/reduce_scatter | solution.py:167
  230.4 79.7 %collective-permute-start.22 = (f32[768,256]{1,0:T(8,128)S(1)}, f32[768,256]{1,0:T(8,128)}, u32[]{:S(2)}, u32[]{:S(2)}) collective-permute-start(f32[768,256]{1,0:T(8,128)S(1)} %select_select_fusion.2), channel_id=1, source_target_pairs={{0,2},{1,3},{2,0},{3,1},{4,6},{5,7},{6,4},{7,5},{8,11},{9,10},{10,... | collective-permute-start | bytes 2359304 | tf_op jit(solution)/shard_map/ppermute | solution.py:132
  232.7 100.7 %collective-permute-start.20 = (f32[768,256]{1,0:T(8,128)S(1)}, f32[768,256]{1,0:T(8,128)S(1)}, u32[]{:S(2)}, u32[]{:S(2)}) collective-permute-start(f32[768,256]{1,0:T(8,128)S(1)} %copy-done.2), channel_id=1, source_target_pairs={{0,4},{4,0},{8,12},{12,8},{16,20},{20,16},{24,28},{28,24},{1,5},{5... | collective-permute-start | bytes 2359304 | tf_op jit(solution)/shard_map/ppermute | solution.py:99
  232.8 100.6 %collective-permute-start.21 = (f32[768,256]{1,0:T(8,128)}, f32[768,256]{1,0:T(8,128)S(1)}, u32[]{:S(2)}, u32[]{:S(2)}) collective-permute-start(f32[768,256]{1,0:T(8,128)} %collective-permute-done.19.refs_5_), channel_id=1, source_target_pairs={{0,4},{4,0},{8,12},{12,8},{16,20},{20,16},{24,28},{28,24},{1,5},{5... | collective-permute-start | bytes 2359304 | tf_op jit(solution)/shard_map/ppermute | solution.py:99
  233.2 98.2 %collective-permute-start.24 = (f32[768,256]{1,0:T(8,128)S(1)}, f32[768,256]{1,0:T(8,128)}, u32[]{:S(2)}, u32[]{:S(2)}) collective-permute-start(f32[768,256]{1,0:T(8,128)S(1)} %copy-done), channel_id=1, source_target_pairs={{0,8},{4,20},{8,0},{12,28},{16,24},{20,4},{24,16},{28,12},{1,9},{5... | collective-permute-start | bytes 2359304 | tf_op jit(solution)/shard_map/ppermute | solution.py:99
  331.3 26.0 %collective-permute-start.26 = (f32[768,256]{1,0:T(8,128)S(1)}, f32[768,256]{1,0:T(8,128)}, u32[]{:S(2)}, u32[]{:S(2)}) collective-permute-start(f32[768,256]{1,0:T(8,128)S(1)} %copy-done), channel_id=1, source_target_pairs={{0,16},{4,12},{8,24},{12,4},{16,0},{20,28},{24,8},{28,20},{1,17},{... | collective-permute-start | bytes 2359304 | tf_op jit(solution)/shard_map/ppermute | solution.py:99
  331.4 25.9 %collective-permute-start.23 = (f32[768,256]{1,0:T(8,128)S(1)}, f32[768,256]{1,0:T(8,128)}, u32[]{:S(2)}, u32[]{:S(2)}) collective-permute-start(f32[768,256]{1,0:T(8,128)S(1)} %copy-done), channel_id=1, source_target_pairs={{0,4},{4,0},{8,12},{12,8},{16,20},{20,16},{24,28},{28,24},{1,5},{5... | collective-permute-start | bytes 2359304 | tf_op jit(solution)/shard_map/ppermute | solution.py:99
  331.5 25.8 %collective-permute-start.27 = (f32[768,256]{1,0:T(8,128)}, f32[768,256]{1,0:T(8,128)}, u32[]{:S(2)}, u32[]{:S(2)}) collective-permute-start(f32[768,256]{1,0:T(8,128)} %collective-permute-done.24.refs_5_), channel_id=1, source_target_pairs={{0,16},{4,12},{8,24},{12,4},{16,0},{20,28},{24,8},{28,20},{1,17},{... | collective-permute-start | bytes 2359304 | tf_op jit(solution)/shard_map/ppermute | solution.py:99
  333.4 23.9 %collective-permute-start.25 = (f32[768,256]{1,0:T(8,128)}, f32[768,256]{1,0:T(8,128)}, u32[]{:S(2)}, u32[]{:S(2)}) collective-permute-start(f32[768,256]{1,0:T(8,128)} %collective-permute-done.24.refs_5_), channel_id=1, source_target_pairs={{0,4},{4,0},{8,12},{12,8},{16,20},{20,16},{24,28},{28,24},{1,5},{5... | collective-permute-start | bytes 2359304 | tf_op jit(solution)/shard_map/ppermute | solution.py:99
  357.4 229.6 %reduce-scatter.11.cloned.1.call-start = ((), (), s32[]{:S(2)}) async-start(), calls=%async_computation.7 | async-start | bytes 3932160 | tf_op jit(solution)/shard_map/reduce_scatter | solution.py:167
  364.0 55.9 %collective-permute-start.30 = (f32[768,256]{1,0:T(8,128)S(1)}, f32[768,256]{1,0:T(8,128)}, u32[]{:S(2)}, u32[]{:S(2)}) collective-permute-start(f32[768,256]{1,0:T(8,128)S(1)} %select_select_fusion.1), channel_id=1, source_target_pairs={{0,1},{1,0},{2,3},{3,2},{4,5},{5,4},{6,7},{7,6},{8,8},{9,9},{10,10... | collective-permute-start | bytes 2359304 | tf_op jit(solution)/shard_map/ppermute | solution.py:132
  370.5 129.8 %collective-permute-start.31 = (f32[768,256]{1,0:T(8,128)}, f32[768,256]{1,0:T(8,128)}, u32[]{:S(2)}, u32[]{:S(2)}) collective-permute-start(f32[768,256]{1,0:T(8,128)} %collective-permute-done.13), channel_id=1, source_target_pairs={{0,0},{1,9},{2,18},{3,27},{4,4},{5,13},{6,22},{7,31},{8,8},{9,1},{... | collective-permute-start | bytes 2359304 | tf_op jit(solution)/shard_map/ppermute | solution.py:132
  443.8 53.2 %collective-permute-start.34 = (f32[768,256]{1,0:T(8,128)S(1)}, f32[768,256]{1,0:T(8,128)}, u32[]{:S(2)}, u32[]{:S(2)}) collective-permute-start(f32[768,256]{1,0:T(8,128)S(1)} %select_select_fusion), channel_id=1, source_target_pairs={{0,3},{1,2},{2,1},{3,0},{4,7},{5,6},{6,5},{7,4},{8,10},{9,11},{10,... | collective-permute-start | bytes 2359304 | tf_op jit(solution)/shard_map/ppermute | solution.py:132
  469.7 42.7 %collective-permute-start.32 = (f32[768,256]{1,0:T(8,128)}, f32[768,256]{1,0:T(8,128)}, u32[]{:S(2)}, u32[]{:S(2)}) collective-permute-start(f32[768,256]{1,0:T(8,128)} %collective-permute-done.22), channel_id=1, source_target_pairs={{0,16},{1,25},{2,2},{3,11},{4,20},{5,29},{6,6},{7,15},{8,24},{9,17... | collective-permute-start | bytes 2359304 | tf_op jit(solution)/shard_map/ppermute | solution.py:132
  497.0 35.3 %collective-permute-start.35 = (f32[768,256]{1,0:T(8,128)}, f32[768,256]{1,0:T(8,128)}, u32[]{:S(2)}, u32[]{:S(2)}) collective-permute-start(f32[768,256]{1,0:T(8,128)} %collective-permute-done.34), channel_id=1, source_target_pairs={{0,24},{1,17},{2,10},{3,3},{4,28},{5,21},{6,14},{7,7},{8,16},{9,25... | collective-permute-start | bytes 2359304 | tf_op jit(solution)/shard_map/ppermute | solution.py:132
  (58 other events, 813.9 us)
Sparse Core Ops, SparseCore 0:
  94.2 60.5 reduce-scatter.4
  223.0 89.1 reduce-scatter.6
  357.5 75.8 reduce-scatter.8
  469.8 80.9 reduce-scatter.10

commit v5 on v4

--- a/solution.py
+++ b/solution.py
@@ -8,7 +8,8 @@
 from jax.experimental.pallas import tpu as pltpu
 from jax.sharding import PartitionSpec as P
 
-CHUNKS = 4
+CHUNKS = 2
+SLICES = 4
 LANES = 128
 MIB = 1 << 20
 
@@ -65,7 +66,7 @@
             scratch_shapes=[pltpu.VMEM((count, depth, 2 * columns), jnp.bfloat16)],
         ),
         out_shape=jax.ShapeDtypeStruct((rows, columns), jnp.float32),
-        compiler_params=pltpu.CompilerParams(vmem_limit_bytes=32 * MIB, dimension_semantics=("arbitrary",)),
+        compiler_params=pltpu.CompilerParams(vmem_limit_bytes=44 * MIB, dimension_semantics=("arbitrary",)),
         cost_estimate=pl.CostEstimate(
             flops=6 * rows * depth * count * columns,
             bytes_accessed=4 * (rows * depth * count + depth * count * columns + 2 * rows * columns),
@@ -91,7 +92,7 @@
 
 
 def after(value, *others):
-    return lax.optimization_barrier((value, *others))[0]
+    return lax.optimization_barrier((value, *others))[0] if others else value
 
 
 def cross(pieces, masks, count):
@@ -122,27 +123,25 @@
     return total
 
 
-def move(value, target):
+def move(value, target, chosen):
     row_count, column_count = lax.axis_size("row"), lax.axis_size("col")
     pairs = []
     for r in range(row_count):
         for c in range(column_count):
-            to_row, to_column = target(r, c)
-            pairs.append((r * column_count + c, to_row * column_count + to_column))
+            if chosen(r, c):
+                to_row, to_column = target(r, c)
+                pairs.append((r * column_count + c, to_row * column_count + to_column))
     return lax.ppermute(value, ("row", "col"), pairs)
 
 
 def shards(parent_inverse, panel, saved_diag):
     row_count, column_count = lax.axis_size("row"), lax.axis_size("col")
-    row_index, column_index = lax.axis_index("row"), lax.axis_index("col")
+    row_index = lax.axis_index("row")
     group = row_count // column_count
-    block_rows = panel.shape[0]
     width = panel.shape[1] // CHUNKS
-    stepwise = block_rows % LANES == 0
+    stepwise = panel.shape[0] % LANES == 0
     orders = gather_orders(row_count)
-    places = gather_places(row_count)
-    place = jnp.asarray(places)[row_index]
-    slots = jnp.asarray(np.argsort(places, axis=1).astype(np.int32))[row_index]
+    place = jnp.asarray(gather_places(row_count))[row_index]
 
     def cut(chunk):
         return lax.slice_in_dim(panel, chunk * width, (chunk + 1) * width, axis=1)
@@ -153,65 +152,66 @@
     def all_after(pieces, *others):
         return [after(piece, *others) for piece in pieces]
 
-    def turn(chunk):
-        return chunk * 2 % column_count + chunk * 2 // column_count
-
-    def spread(chunk, select):
-        wanted = row_index % group * column_count + (column_index ^ (row_index // group) ^ turn(chunk))
-        return move(select(wanted), lambda r, c: (r, c ^ (r // group) ^ turn(chunk)))
-
-    def hop(value, chunk):
-        return move(value, lambda r, c: (((r // group) ^ c ^ turn(chunk)) * group + r % group, c))
+    def over_col(part, flip):
+        return [part] + [
+            move(part, lambda r, c: (r ^ flip, r % column_count), lambda r, c: r % column_count ^ c == shift)
+            for shift in range(1, column_count)
+        ]
+
+    def over_row(parts, flip):
+        def arrived(part, shift, flip):
+            return move(
+                part,
+                lambda r, c: ((c ^ shift) * group + (r ^ flip) // column_count, c),
+                lambda r, c: (r ^ flip) % column_count == c,
+            )
+
+        found = [arrived(part, shift, flip if shift else 0) for shift, part in enumerate(parts)]
+        return functools.reduce(jnp.add, found)
 
     def summed(partial_block, *others):
         return lax.psum_scatter(after(partial_block, *others), "col", scatter_dimension=0, tiled=True)
 
-    products, blocks, moved = [], [], []
+    breadth = panel.shape[1] // SLICES
+    flips = [i % 2 * group for i in range(SLICES)]
+    slices = [lax.slice_in_dim(panel, i * breadth, (i + 1) * breadth, axis=1) for i in range(SLICES)]
+    products, blocks = [], []
     if stepwise:
         half = row_count // 2
-
         def link(pieces, orders):
             for masks in orders:
                 pieces = pieces + cross(pieces, masks, row_count)
             return pieces
 
-        mine = [link([cut(0)], orders[:-1])] + [None] * (CHUNKS - 1)
-        theirs = [partner(all_after(mine[0], mine[0][-1]))] + [None] * (CHUNKS - 1)
-        late = [cross(all_after(mine[0], theirs[0][-1]), orders[-1], row_count)] + [None] * (CHUNKS - 1)
-        mine[1] = link(all_after([cut(1)], late[0][-1]), orders[:-1])
+        mine = link([cut(0)], orders[:-1])
+        pair = SLICES // 2
+        moving = [over_col(part, flip) for part, flip in zip(slices[:pair], flips)]
+        arrived = [part for parts in moving for part in parts[1:]]
+        moving += [over_col(after(part, *arrived), flip) for part, flip in zip(slices[pair:], flips[pair:])]
+        arrived = [arrived, [part for parts in moving[pair:] for part in parts[1:]]]
         last = None
         for chunk in range(CHUNKS):
-            if chunk == 1:
-                theirs[1] = partner(all_after(mine[1], last))
-                late[1] = cross(all_after(mine[1], theirs[1][-1]), orders[-1], row_count)
-            if 1 <= chunk < CHUNKS - 1:
-                mine[chunk + 1] = link(all_after([cut(chunk + 1)], last), orders[:-1])
-            first = mine[chunk] + theirs[chunk]
-            waits = moved[-1:]
-            last = negative_product(after(parent_inverse, *waits) if waits else parent_inverse, first, place[:half])
-            second = late[chunk] + partner(late[chunk])
-            if 1 <= chunk < CHUNKS - 1:
-                theirs[chunk + 1] = partner(all_after(mine[chunk + 1], last))
-                late[chunk + 1] = cross(all_after(mine[chunk + 1], last), orders[-1], row_count)
-            moved.append(spread(chunk, lambda wanted: lax.select_n(slots[wanted], *first, *second)))
-            last = negative_product(parent_inverse, second, place[half:], last)
+            theirs = partner(all_after(mine, mine[-1]) if last is None else all_after(mine, last))
+            late = cross(all_after(mine, theirs[-1]), orders[-1], row_count)
+            last = negative_product(parent_inverse, mine + theirs, place[:half])
+            waits = [last] if chunk else [last] + arrived[0]
+            late = late + partner(all_after(late, *waits))
+            if chunk + 1 < CHUNKS:
+                mine = link(all_after([cut(chunk + 1)], last), orders[:-1])
+            last = negative_product(parent_inverse, late, place[half:], last)
             products.append(last)
-            if chunk == 0:
-                waits = mine[1][-1:]
-            elif chunk < CHUNKS - 1:
-                waits = theirs[chunk + 1] + late[chunk + 1]
-            else:
-                waits = []
+            waits = [] if chunk else arrived[1] + mine[-1:]
             blocks.append(summed(last, *waits))
-        moved = [hop(after(value, products[-2]), chunk) for chunk, value in enumerate(moved)]
+        own_rows = [
+            over_row([after(part, products[0]) for part in parts], flip) for parts, flip in zip(moving, flips)
+        ]
     else:
+        own_rows = [over_row(over_col(part, flip), flip) for part, flip in zip(slices, flips)]
         for chunk in range(CHUNKS):
             whole = lax.all_gather(cut(chunk), "row", axis=0, tiled=True)
-            part = spread(chunk, lambda wanted: lax.dynamic_slice_in_dim(whole, wanted * block_rows, block_rows, 0))
-            moved.append(hop(part, chunk))
             products.append(negative_product(parent_inverse, [whole], jnp.zeros((1,), jnp.int32)))
             blocks.append(summed(products[-1]))
-    own_rows = jnp.concatenate(moved, axis=1)
+    own_rows = jnp.concatenate(own_rows, axis=1)
     grams = []
     for chunk, block in enumerate(blocks):
         waits = [products[-1]] if chunk < CHUNKS - 1 else grams

time: 639 us -> 491 us (0.77)
  starting transfers between devices: 133 us -> 88.2 us
  Pallas kernels: 172 us -> 147 us
  waiting for transfers between devices: 237 us -> 212 us
  between operations: 33.1 us -> 14.5 us
  local copies, waits for them, and re-layouts: 20.8 us -> 5.2 us
  other arithmetic: 20.8 us -> 13.3 us
    ppermute x8 -> x28, waiting for transfers between devices: 142 us -> 83.1 us  [move(): return lax.ppermute(value, ('row', 'col'), pairs)]
    ppermute x28 -> x14, starting transfers between devices: 71.5 us -> 15.6 us  [cross(): return [lax.ppermute(piece, 'row', pairs) for piece in pieces]]
    reduce_scatter x4 -> x2, waiting for transfers between devices: 0.03 us -> 52.4 us  [summed(): lax.psum_scatter(after(partial_block, *others), 'col', scatter_dimension=...]
    pallas_call x8 -> x4, Pallas kernels: 172 us -> 147 us  [negative_product(): pl.pallas_call(functools.partial(product_kernel, count), grid_spec=pltpu....]
    ppermute x28 -> x14, waiting for transfers between devices: 49.6 us -> 26.8 us  [cross(): return [lax.ppermute(piece, 'row', pairs) for piece in pieces]]
    unnamed x57 -> x28, local copies, waits for them, and re-layouts: 13.5 us -> 0.05 us
    ppermute x8 -> x28, starting transfers between devices: 47.3 us -> 59.8 us  [move(): return lax.ppermute(value, ('row', 'col'), pairs)]
    add x0 -> x4, other arithmetic: none -> 8.61 us  [over_row(): return functools.reduce(jnp.add, found)]
  transfers between devices with their start and end apart: 55 -> 53, of which waited for: 20 -> 20; matrix products, arithmetic and copies ran while one was open for 6% -> 4% of each run, Pallas kernels for 27% -> 30%
where the time goes in v5:
time: 491 us; the launch traced here: 490 us
  waiting for transfers between devices  212 us (43%)
  Pallas kernels  147 us (30%)
  starting transfers between devices  88.2 us (18%)
  between operations  14.5 us (3%)
  other arithmetic  13.3 us (3%)
  matrix products  9.54 us (2%)
  local copies, waits for them, and re-layouts  5.2 us (1%)
    pallas_call x4, Pallas kernels, negative_product(): pl.pallas_call(functools.partial(product_kernel, count), grid_spec=pltpu....  147 us
    ppermute x28, waiting for transfers between devices, move(): return lax.ppermute(value, ('row', 'col'), pairs)  83.1 us
    ppermute x28, starting transfers between devices, move(): return lax.ppermute(value, ('row', 'col'), pairs)  59.8 us
    reduce_scatter x2, waiting for transfers between devices, summed(): lax.psum_scatter(after(partial_block, *others), 'col', scatter_dimension=...  52.4 us
    ppermute x6, waiting for transfers between devices, sum_over_row(): lax.ppermute(send, 'row', [(i, i ^ 1 << bit) for i in range(count)])  45.6 us
    ppermute x14, waiting for transfers between devices, cross(): return [lax.ppermute(piece, 'row', pairs) for piece in pieces]  26.8 us
    ppermute x14, starting transfers between devices, cross(): return [lax.ppermute(piece, 'row', pairs) for piece in pieces]  15.6 us
  transfers between devices with their start and end apart: 53, of which 20 were waited for; matrix products, arithmetic and copies ran while one was open for 4% of the time, Pallas kernels for 30%

profile of v5, /device:TPU:0, one launch (start us, length us, event | category | flops | bytes accessed | tf_op | source)
XLA Modules:
  0.0 489.9 jit_solution(17421373820810114945)
XLA Ops:
  12.6 18.5 %collective-permute-done.refs_5_ = f32[768,512]{1,0:T(8,128)} collective-permute-done((f32[768,512]{1,0:T(8,128)S(1)}, f32[768,512]{1,0:T(8,128)}, u32[]{:S(2)}, u32[]{:S(2)}) %collective-permute-start) | collective-permute-done | bytes 1572896 | tf_op jit(solution)/shard_map/ppermute | solution.py:100
  41.1 15.8 %collective-permute-done.5 = f32[768,256]{1,0:T(8,128)} collective-permute-done((f32[768,256]{1,0:T(8,128)}, f32[768,256]{1,0:T(8,128)}, u32[]{:S(2)}, u32[]{:S(2)}) %collective-permute-start.5) | collective-permute-done | bytes 786464 | tf_op jit(solution)/shard_map/ppermute | solution.py:134
  58.4 26.2 %collective-permute-done.6 = f32[768,256]{1,0:T(8,128)} collective-permute-done((f32[768,256]{1,0:T(8,128)}, f32[768,256]{1,0:T(8,128)}, u32[]{:S(2)}, u32[]{:S(2)}) %collective-permute-start.6) | collective-permute-done | bytes 786464 | tf_op jit(solution)/shard_map/ppermute | solution.py:134
  86.7 37.9 %shard_map.59.refs_8_ = f32[3072,512]{1,0:T(8,128)} custom-call(s32[4]{0:T(128)S(1)} %get-tuple-element.79.place_ref, f32[3072,6144]{1,0:T(8,128)} %refs_3_.7, f32[3072,6144]{1,0:T(8,128)} %refs_3_.7, f32[3072,6144]{1,0:T(8,128)} %refs_3_.7, f32[3072,6144]{1,0:T(8,128)} %refs_3_.7, f32[768,512]{1,0:T(8,128)S(1)} %get-tuple-element.39.refs_4_, ...), custom_call_target="tpu_custom_call" | custom-call | flops 28991029248 | bytes 56623104 | tf_op jit(solution)/shard_map/pallas_call | solution.py:59
  125.6 3.4 collective-permute-start.11
  132.9 23.1 %collective-permute-done.13 = f32[768,256]{1,0:T(8,128)S(1)} collective-permute-done((f32[768,256]{1,0:T(8,128)}, f32[768,256]{1,0:T(8,128)S(1)}, u32[]{:S(2)}, u32[]{:S(2)}) %collective-permute-start.13) | collective-permute-done | bytes 786464 | tf_op jit(solution)/shard_map/ppermute | solution.py:134
  157.5 15.1 %collective-permute-done.14 = f32[768,256]{1,0:T(8,128)S(1)} collective-permute-done((f32[768,256]{1,0:T(8,128)}, f32[768,256]{1,0:T(8,128)S(1)}, u32[]{:S(2)}, u32[]{:S(2)}) %collective-permute-start.14) | collective-permute-done | bytes 786464 | tf_op jit(solution)/shard_map/ppermute | solution.py:134
  177.3 36.4 %shard_map.60 = f32[3072,512]{1,0:T(8,128)} custom-call(s32[4]{0:T(128)S(1)} %get-tuple-element.80.place_ref, f32[3072,6144]{1,0:T(8,128)} %refs_3_.7, f32[3072,6144]{1,0:T(8,128)} %refs_3_.7, f32[3072,6144]{1,0:T(8,128)} %refs_3_.7, f32[3072,6144]{1,0:T(8,128)} %refs_3_.7, f32[768,512]{1,0:T(8,128)S(1)} %collective-permute-done.2.refs_4_, ...), custom_call_target="tpu_custom_call" | custom-call | flops 28991029248 | bytes 56623104 | tf_op jit(solution)/shard_map/pallas_call | solution.py:59
  219.7 36.7 %shard_map.61.refs_8_ = f32[3072,512]{1,0:T(8,128)} custom-call(s32[4]{0:T(128)S(1)} %get-tuple-element.79.place_ref, f32[3072,6144]{1,0:T(8,128)} %refs_3_.7, f32[3072,6144]{1,0:T(8,128)} %refs_3_.7, f32[3072,6144]{1,0:T(8,128)} %refs_3_.7, f32[3072,6144]{1,0:T(8,128)} %refs_3_.7, f32[768,512]{1,0:T(8,128)S(1)} %get-tuple-element.49.refs_4_, ...), custom_call_target="tpu_custom_call" | custom-call | flops 28991029248 | bytes 56623104 | tf_op jit(solution)/shard_map/pallas_call | solution.py:59
  263.2 36.5 %shard_map.62 = f32[3072,512]{1,0:T(8,128)} custom-call(s32[4]{0:T(128)S(1)} %get-tuple-element.80.place_ref, f32[3072,6144]{1,0:T(8,128)} %refs_3_.7, f32[3072,6144]{1,0:T(8,128)} %refs_3_.7, f32[3072,6144]{1,0:T(8,128)} %refs_3_.7, f32[3072,6144]{1,0:T(8,128)} %refs_3_.7, f32[768,512]{1,0:T(8,128)S(1)} %collective-permute-done.21.refs_4_, ...), custom_call_target="tpu_custom_call" | custom-call | flops 28991029248 | bytes 56623104 | tf_op jit(solution)/shard_map/pallas_call | solution.py:59
  299.7 4.5 collective-permute-start.27
  304.3 3.3 collective-permute-start.28
  309.8 7.4 %collective-permute-start.26 = (f32[768,256]{1,0:T(8,128)}, f32[768,256]{1,0:T(8,128)}, u32[]{:S(2)}, u32[]{:S(2)}) collective-permute-start(f32[768,256]{1,0:T(8,128)} %get-tuple-element.52), channel_id=1, source_target_pairs={{0,0},{5,9},{10,18},{15,27},{16,4},{21,13},{26,22},{31,31}} | collective-permute-start | bytes 2359304 | tf_op jit(solution)/shard_map/ppermute | solution.py:134
  325.5 3.7 collective-permute-start.36
  331.7 7.5 %collective-permute-start.34 = (f32[768,256]{1,0:T(8,128)}, f32[768,256]{1,0:T(8,128)}, u32[]{:S(2)}, u32[]{:S(2)}) collective-permute-start(f32[768,256]{1,0:T(8,128)} %get-tuple-element.60), channel_id=1, source_target_pairs={{0,0},{5,9},{10,18},{15,27},{16,4},{21,13},{26,22},{31,31}} | collective-permute-start | bytes 2359304 | tf_op jit(solution)/shard_map/ppermute | solution.py:134
  354.2 4.8 fusion.1
  359.0 3.3 collective-permute-start.42
  366.3 14.1 %collective-permute-done.43 = f32[2,128,512]{2,1,0:T(8,128)S(1)} collective-permute-done((f32[2,128,512]{2,1,0:T(8,128)S(1)}, f32[2,128,512]{2,1,0:T(8,128)S(1)}, u32[]{:S(2)}, u32[]{:S(2)}) %collective-permute-start.43) | collective-permute-done | bytes 524320 | tf_op jit(solution)/shard_map/ppermute | solution.py:112
  380.7 7.8 %collective-permute-done.44 = f32[128,512]{1,0:T(8,128)S(1)} collective-permute-done((f32[128,512]{1,0:T(8,128)S(1)}, f32[128,512]{1,0:T(8,128)S(1)}, u32[]{:S(2)}, u32[]{:S(2)}) %collective-permute-start.44) | collective-permute-done | bytes 262176 | tf_op jit(solution)/shard_map/ppermute | solution.py:112
  388.5 52.4 %reduce-scatter.5.cloned.1.call-done = f32[768,512]{1,0:T(8,128)} async-done(((f32[3072,512]{1,0:T(8,128)}), f32[768,512]{1,0:T(8,128)}) %reduce-scatter.5.cloned.1.call-update) | async-done | bytes 1572880 | tf_op jit(solution)/shard_map/reduce_scatter | solution.py:173
  440.9 4.8 fusion
  450.3 12.5 %collective-permute-done.46 = f32[2,128,512]{2,1,0:T(8,128)S(1)} collective-permute-done((f32[2,128,512]{2,1,0:T(8,128)S(1)}, f32[2,128,512]{2,1,0:T(8,128)S(1)}, u32[]{:S(2)}, u32[]{:S(2)}) %collective-permute-start.46) | collective-permute-done | bytes 524320 | tf_op jit(solution)/shard_map/ppermute | solution.py:112
  464.5 6.1 %collective-permute-done.47 = f32[128,512]{1,0:T(8,128)S(1)} collective-permute-done((f32[128,512]{1,0:T(8,128)S(1)}, f32[128,512]{1,0:T(8,128)S(1)}, u32[]{:S(2)}, u32[]{:S(2)}) %collective-permute-start.47) | collective-permute-done | bytes 262176 | tf_op jit(solution)/shard_map/ppermute | solution.py:112
  479.0 3.3 collective-permute-done.49
  (141 shorter events, 90.4 us)
Async XLA Ops:
  7.2 347.0 %reduce-scatter.3.cloned.1.call-start = ((), (), s32[]{:S(2)}) async-start(), calls=%async_computation.2 | async-start | bytes 7864320 | tf_op jit(solution)/shard_map/reduce_scatter | solution.py:173
  9.6 21.5 %collective-permute-start = (f32[768,512]{1,0:T(8,128)S(1)}, f32[768,512]{1,0:T(8,128)}, u32[]{:S(2)}, u32[]{:S(2)}) collective-permute-start(f32[768,512]{1,0:T(8,128)S(1)} %get-tuple-element.39.refs_4_), channel_id=1, source_target_pairs={{0,8},{4,20},{8,0},{12,28},{16,24},{20,4},{24,16},{28,12},{1,9},{5... | collective-permute-start | bytes 4718600 | tf_op jit(solution)/shard_map/ppermute | solution.py:100
  31.1 55.1 %collective-permute-start.4 = (f32[768,512]{1,0:T(8,128)S(1)}, f32[768,512]{1,0:T(8,128)}, u32[]{:S(2)}, u32[]{:S(2)}) collective-permute-start(f32[768,512]{1,0:T(8,128)S(1)} %get-tuple-element.39.refs_4_), channel_id=1, source_target_pairs={{0,4},{4,0},{8,12},{12,8},{16,20},{20,16},{24,28},{28,24},{1,5},{5... | collective-permute-start | bytes 4718600 | tf_op jit(solution)/shard_map/ppermute | solution.py:100
  34.9 22.0 %collective-permute-start.5 = (f32[768,256]{1,0:T(8,128)}, f32[768,256]{1,0:T(8,128)}, u32[]{:S(2)}, u32[]{:S(2)}) collective-permute-start(f32[768,256]{1,0:T(8,128)} %get-tuple-element.52), channel_id=1, source_target_pairs={{1,0},{4,5},{11,10},{14,15},{17,16},{20,21},{27,26},{30,31}} | collective-permute-start | bytes 2359304 | tf_op jit(solution)/shard_map/ppermute | solution.py:134
  36.2 48.4 %collective-permute-start.6 = (f32[768,256]{1,0:T(8,128)}, f32[768,256]{1,0:T(8,128)}, u32[]{:S(2)}, u32[]{:S(2)}) collective-permute-start(f32[768,256]{1,0:T(8,128)} %get-tuple-element.52), channel_id=1, source_target_pairs={{2,0},{7,5},{8,10},{13,15},{18,16},{23,21},{24,26},{29,31}} | collective-permute-start | bytes 2359304 | tf_op jit(solution)/shard_map/ppermute | solution.py:134
  38.3 86.3 %collective-permute-start.7 = (f32[768,256]{1,0:T(8,128)}, f32[768,256]{1,0:T(8,128)S(1)}, u32[]{:S(2)}, u32[]{:S(2)}) collective-permute-start(f32[768,256]{1,0:T(8,128)} %get-tuple-element.52), channel_id=1, source_target_pairs={{3,0},{6,5},{9,10},{12,15},{19,16},{22,21},{25,26},{28,31}} | collective-permute-start | bytes 2359304 | tf_op jit(solution)/shard_map/ppermute | solution.py:134
  39.6 85.0 %collective-permute-start.8 = (f32[768,256]{1,0:T(8,128)}, f32[768,256]{1,0:T(8,128)}, u32[]{:S(2)}, u32[]{:S(2)}) collective-permute-start(f32[768,256]{1,0:T(8,128)} %get-tuple-element.56), channel_id=1, source_target_pairs={{1,8},{4,13},{11,2},{14,7},{17,24},{20,29},{27,18},{30,23}} | collective-permute-start | bytes 2359304 | tf_op jit(solution)/shard_map/ppermute | solution.py:134
  56.9 67.7 %collective-permute-start.9 = (f32[768,256]{1,0:T(8,128)}, f32[768,256]{1,0:T(8,128)}, u32[]{:S(2)}, u32[]{:S(2)}) collective-permute-start(f32[768,256]{1,0:T(8,128)} %get-tuple-element.56), channel_id=1, source_target_pairs={{2,8},{7,13},{8,2},{13,7},{18,24},{23,29},{24,18},{29,23}} | collective-permute-start | bytes 2359304 | tf_op jit(solution)/shard_map/ppermute | solution.py:134
  84.6 40.0 %collective-permute-start.3 = (f32[768,512]{1,0:T(8,128)}, f32[768,512]{1,0:T(8,128)S(1)}, u32[]{:S(2)}, u32[]{:S(2)}) collective-permute-start(f32[768,512]{1,0:T(8,128)} %collective-permute-done.refs_5_), channel_id=1, source_target_pairs={{0,16},{4,12},{8,24},{12,4},{16,0},{20,28},{24,8},{28,20},{1,17},{... | collective-permute-start | bytes 4718600 | tf_op jit(solution)/shard_map/ppermute | solution.py:100
  86.1 39.4 %collective-permute-start.2 = (f32[768,512]{1,0:T(8,128)S(1)}, f32[768,512]{1,0:T(8,128)S(1)}, u32[]{:S(2)}, u32[]{:S(2)}) collective-permute-start(f32[768,512]{1,0:T(8,128)S(1)} %get-tuple-element.39.refs_4_), channel_id=1, source_target_pairs={{0,16},{4,12},{8,24},{12,4},{16,0},{20,28},{24,8},{28,20},{1,17},{... | collective-permute-start | bytes 4718600 | tf_op jit(solution)/shard_map/ppermute | solution.py:100
  124.6 49.6 %collective-permute-start.12 = (f32[768,512]{1,0:T(8,128)S(1)}, f32[768,512]{1,0:T(8,128)S(1)}, u32[]{:S(2)}, u32[]{:S(2)}) collective-permute-start(f32[768,512]{1,0:T(8,128)S(1)} %collective-permute-done.3.refs_5_), channel_id=1, source_target_pairs={{0,4},{4,0},{8,12},{12,8},{16,20},{20,16},{24,28},{28,24},{1,5},{5... | collective-permute-start | bytes 4718600 | tf_op jit(solution)/shard_map/ppermute | solution.py:100
  125.6 50.2 %collective-permute-start.11 = (f32[768,512]{1,0:T(8,128)S(1)}, f32[768,512]{1,0:T(8,128)S(1)}, u32[]{:S(2)}, u32[]{:S(2)}) collective-permute-start(f32[768,512]{1,0:T(8,128)S(1)} %collective-permute-done.2.refs_4_), channel_id=1, source_target_pairs={{0,4},{4,0},{8,12},{12,8},{16,20},{20,16},{24,28},{28,24},{1,5},{5... | collective-permute-start | bytes 4718600 | tf_op jit(solution)/shard_map/ppermute | solution.py:100
  129.0 27.0 %collective-permute-start.13 = (f32[768,256]{1,0:T(8,128)}, f32[768,256]{1,0:T(8,128)S(1)}, u32[]{:S(2)}, u32[]{:S(2)}) collective-permute-start(f32[768,256]{1,0:T(8,128)} %get-tuple-element.60), channel_id=1, source_target_pairs={{1,0},{4,5},{11,10},{14,15},{17,16},{20,21},{27,26},{30,31}} | collective-permute-start | bytes 2359304 | tf_op jit(solution)/shard_map/ppermute | solution.py:134
  130.3 42.4 %collective-permute-start.14 = (f32[768,256]{1,0:T(8,128)}, f32[768,256]{1,0:T(8,128)S(1)}, u32[]{:S(2)}, u32[]{:S(2)}) collective-permute-start(f32[768,256]{1,0:T(8,128)} %get-tuple-element.60), channel_id=1, source_target_pairs={{2,0},{7,5},{8,10},{13,15},{18,16},{23,21},{24,26},{29,31}} | collective-permute-start | bytes 2359304 | tf_op jit(solution)/shard_map/ppermute | solution.py:134
  131.6 82.1 %collective-permute-start.15 = (f32[768,256]{1,0:T(8,128)}, f32[768,256]{1,0:T(8,128)}, u32[]{:S(2)}, u32[]{:S(2)}) collective-permute-start(f32[768,256]{1,0:T(8,128)} %get-tuple-element.60), channel_id=1, source_target_pairs={{3,0},{6,5},{9,10},{12,15},{19,16},{22,21},{25,26},{28,31}} | collective-permute-start | bytes 2359304 | tf_op jit(solution)/shard_map/ppermute | solution.py:134
  156.0 57.7 %collective-permute-start.16 = (f32[768,256]{1,0:T(8,128)}, f32[768,256]{1,0:T(8,128)}, u32[]{:S(2)}, u32[]{:S(2)}) collective-permute-start(f32[768,256]{1,0:T(8,128)} %get-tuple-element.64), channel_id=1, source_target_pairs={{1,8},{4,13},{11,2},{14,7},{17,24},{20,29},{27,18},{30,23}} | collective-permute-start | bytes 2359304 | tf_op jit(solution)/shard_map/ppermute | solution.py:134
  172.7 41.0 %collective-permute-start.17 = (f32[768,256]{1,0:T(8,128)}, f32[768,256]{1,0:T(8,128)}, u32[]{:S(2)}, u32[]{:S(2)}) collective-permute-start(f32[768,256]{1,0:T(8,128)} %get-tuple-element.64), channel_id=1, source_target_pairs={{2,8},{7,13},{8,2},{13,7},{18,24},{23,29},{24,18},{29,23}} | collective-permute-start | bytes 2359304 | tf_op jit(solution)/shard_map/ppermute | solution.py:134
  174.2 39.4 %collective-permute-start.18 = (f32[768,256]{1,0:T(8,128)}, f32[768,256]{1,0:T(8,128)}, u32[]{:S(2)}, u32[]{:S(2)}) collective-permute-start(f32[768,256]{1,0:T(8,128)} %get-tuple-element.64), channel_id=1, source_target_pairs={{3,8},{6,13},{9,2},{12,7},{19,24},{22,29},{25,18},{28,23}} | collective-permute-start | bytes 2359304 | tf_op jit(solution)/shard_map/ppermute | solution.py:134
  175.8 37.9 %collective-permute-start.19 = (f32[768,512]{1,0:T(8,128)S(1)}, f32[768,512]{1,0:T(8,128)S(1)}, u32[]{:S(2)}, u32[]{:S(2)}) collective-permute-start(f32[768,512]{1,0:T(8,128)S(1)} %get-tuple-element.49.refs_4_), channel_id=1, source_target_pairs={{0,8},{4,20},{8,0},{12,28},{16,24},{20,4},{24,16},{28,12},{1,9},{5... | collective-permute-start | bytes 4718600 | tf_op jit(solution)/shard_map/ppermute | solution.py:100
  213.7 227.2 %reduce-scatter.5.cloned.1.call-start = ((), (), s32[]{:S(2)}) async-start(), calls=%async_computation.3 | async-start | bytes 7864320 | tf_op jit(solution)/shard_map/reduce_scatter | solution.py:173
  217.4 38.9 %collective-permute-start.22 = (f32[768,512]{1,0:T(8,128)S(1)}, f32[768,512]{1,0:T(8,128)S(1)}, u32[]{:S(2)}, u32[]{:S(2)}) collective-permute-start(f32[768,512]{1,0:T(8,128)S(1)} %collective-permute-done.19.refs_5_), channel_id=1, source_target_pairs={{0,16},{4,12},{8,24},{12,4},{16,0},{20,28},{24,8},{28,20},{1,17},{... | collective-permute-start | bytes 4718600 | tf_op jit(solution)/shard_map/ppermute | solution.py:100
  219.0 38.9 %collective-permute-start.21 = (f32[768,512]{1,0:T(8,128)S(1)}, f32[768,512]{1,0:T(8,128)S(1)}, u32[]{:S(2)}, u32[]{:S(2)}) collective-permute-start(f32[768,512]{1,0:T(8,128)S(1)} %get-tuple-element.49.refs_4_), channel_id=1, source_target_pairs={{0,16},{4,12},{8,24},{12,4},{16,0},{20,28},{24,8},{28,20},{1,17},{... | collective-permute-start | bytes 4718600 | tf_op jit(solution)/shard_map/ppermute | solution.py:100
  299.7 19.0 %collective-permute-start.27 = (f32[768,256]{1,0:T(8,128)}, f32[768,256]{1,0:T(8,128)S(1)}, u32[]{:S(2)}, u32[]{:S(2)}) collective-permute-start(f32[768,256]{1,0:T(8,128)} %collective-permute-done.5), channel_id=1, source_target_pairs={{0,8},{5,1},{10,26},{15,19},{16,12},{21,5},{26,30},{31,23}} | collective-permute-start | bytes 2359304 | tf_op jit(solution)/shard_map/ppermute | solution.py:134
  331.7 18.6 %collective-permute-start.34 = (f32[768,256]{1,0:T(8,128)}, f32[768,256]{1,0:T(8,128)}, u32[]{:S(2)}, u32[]{:S(2)}) collective-permute-start(f32[768,256]{1,0:T(8,128)} %get-tuple-element.60), channel_id=1, source_target_pairs={{0,0},{5,9},{10,18},{15,27},{16,4},{21,13},{26,22},{31,31}} | collective-permute-start | bytes 2359304 | tf_op jit(solution)/shard_map/ppermute | solution.py:134
  (43 other events, 550.4 us)
Sparse Core Ops, SparseCore 0:
  213.8 113.4 reduce-scatter.2
  329.6 111.2 reduce-scatter.4

commit v6 on v5

--- a/solution.py
+++ b/solution.py
@@ -8,8 +8,7 @@
 from jax.experimental.pallas import tpu as pltpu
 from jax.sharding import PartitionSpec as P
 
-CHUNKS = 2
-SLICES = 4
+EIGHTHS = (3, 3, 2)
 LANES = 128
 MIB = 1 << 20
 
@@ -123,28 +122,29 @@
     return total
 
 
-def move(value, target, chosen):
+def move(value, target):
     row_count, column_count = lax.axis_size("row"), lax.axis_size("col")
     pairs = []
     for r in range(row_count):
         for c in range(column_count):
-            if chosen(r, c):
-                to_row, to_column = target(r, c)
-                pairs.append((r * column_count + c, to_row * column_count + to_column))
+            to = target(r, c)
+            if to is not None:
+                pairs.append((r * column_count + c, to[0] * column_count + to[1]))
     return lax.ppermute(value, ("row", "col"), pairs)
 
 
 def shards(parent_inverse, panel, saved_diag):
     row_count, column_count = lax.axis_size("row"), lax.axis_size("col")
-    row_index = lax.axis_index("row")
+    row_index, column_index = lax.axis_index("row"), lax.axis_index("col")
     group = row_count // column_count
-    width = panel.shape[1] // CHUNKS
     stepwise = panel.shape[0] % LANES == 0
     orders = gather_orders(row_count)
     place = jnp.asarray(gather_places(row_count))[row_index]
-
-    def cut(chunk):
-        return lax.slice_in_dim(panel, chunk * width, (chunk + 1) * width, axis=1)
+    unit = panel.shape[1] // 8
+    chunks, first = [], 0
+    for size in EIGHTHS:
+        chunks.append(lax.slice_in_dim(panel, first * unit, (first + size) * unit, axis=1))
+        first += size
 
     def partner(pieces):
         return cross(pieces, (1, 1), row_count)
@@ -152,69 +152,77 @@
     def all_after(pieces, *others):
         return [after(piece, *others) for piece in pieces]
 
-    def over_col(part, flip):
-        return [part] + [
-            move(part, lambda r, c: (r ^ flip, r % column_count), lambda r, c: r % column_count ^ c == shift)
-            for shift in range(1, column_count)
-        ]
-
-    def over_row(parts, flip):
-        def arrived(part, shift, flip):
-            return move(
-                part,
-                lambda r, c: ((c ^ shift) * group + (r ^ flip) // column_count, c),
-                lambda r, c: (r ^ flip) % column_count == c,
-            )
-
-        found = [arrived(part, shift, flip if shift else 0) for shift, part in enumerate(parts)]
-        return functools.reduce(jnp.add, found)
+    rounds = [(k, k % (column_count - 1) + 1) for k in range(1, column_count)]
+    panel_left, panel_right = jnp.split(panel, 2, axis=1)
+
+    def over_col(shifts, *others):
+        left, right = shifts
+
+        def target(r, c):
+            goal = r % column_count
+            return {left: (r, goal), right: (r ^ group, goal)}.get(goal ^ c)
+
+        sends_right = (row_index % column_count) ^ column_index == right
+        return move(after(jnp.where(sends_right, panel_right, panel_left), *others), target)
+
+    def over_row(arrived):
+        def target(left, right):
+            def of(r, c):
+                for source, shift in ((r, left), (r ^ group, right)):
+                    if source % column_count == c:
+                        return (c ^ shift) * group + source // column_count, c
+
+            return of
+
+        def still(r, c):
+            return (c * group + r // column_count, c) if r % column_count == c else None
+
+        halves = list(jnp.split(move(panel, still), 2, axis=1))
+        mine = (row_index // group) ^ column_index
+        for value, shifts in zip(arrived, rounds):
+            value = move(value, target(*shifts))
+            for side in range(2):
+                halves[side] = halves[side] + jnp.where(mine == shifts[side], value, jnp.zeros_like(value))
+        return jnp.concatenate(halves, axis=1)
 
     def summed(partial_block, *others):
         return lax.psum_scatter(after(partial_block, *others), "col", scatter_dimension=0, tiled=True)
 
-    breadth = panel.shape[1] // SLICES
-    flips = [i % 2 * group for i in range(SLICES)]
-    slices = [lax.slice_in_dim(panel, i * breadth, (i + 1) * breadth, axis=1) for i in range(SLICES)]
     products, blocks = [], []
     if stepwise:
         half = row_count // 2
+
         def link(pieces, orders):
             for masks in orders:
                 pieces = pieces + cross(pieces, masks, row_count)
             return pieces
 
-        mine = link([cut(0)], orders[:-1])
-        pair = SLICES // 2
-        moving = [over_col(part, flip) for part, flip in zip(slices[:pair], flips)]
-        arrived = [part for parts in moving for part in parts[1:]]
-        moving += [over_col(after(part, *arrived), flip) for part, flip in zip(slices[pair:], flips[pair:])]
-        arrived = [arrived, [part for parts in moving[pair:] for part in parts[1:]]]
+        mine = link(chunks[:1], orders[:-1])
+        arrived = [over_col(shifts, mine[-1]) for shifts in rounds[:2]]
+        arrived += [over_col(shifts, *arrived) for shifts in rounds[2:]]
         last = None
-        for chunk in range(CHUNKS):
+        for chunk in range(len(chunks)):
             theirs = partner(all_after(mine, mine[-1]) if last is None else all_after(mine, last))
             late = cross(all_after(mine, theirs[-1]), orders[-1], row_count)
             last = negative_product(parent_inverse, mine + theirs, place[:half])
-            waits = [last] if chunk else [last] + arrived[0]
+            waits = [last] if chunk else [last] + arrived[:2]
             late = late + partner(all_after(late, *waits))
-            if chunk + 1 < CHUNKS:
-                mine = link(all_after([cut(chunk + 1)], last), orders[:-1])
+            if chunk + 1 < len(chunks):
+                mine = link(all_after([chunks[chunk + 1]], last), orders[:-1])
             last = negative_product(parent_inverse, late, place[half:], last)
             products.append(last)
-            waits = [] if chunk else arrived[1] + mine[-1:]
-            blocks.append(summed(last, *waits))
-        own_rows = [
-            over_row([after(part, products[0]) for part in parts], flip) for parts, flip in zip(moving, flips)
-        ]
+            waits = mine[-1:] if chunk + 1 < len(chunks) else []
+            blocks.append(summed(last, *waits, *([] if chunk else arrived[2:])))
+        own_rows = over_row([after(value, products[0]) for value in arrived])
     else:
-        own_rows = [over_row(over_col(part, flip), flip) for part, flip in zip(slices, flips)]
-        for chunk in range(CHUNKS):
-            whole = lax.all_gather(cut(chunk), "row", axis=0, tiled=True)
+        own_rows = over_row([over_col(shifts) for shifts in rounds])
+        for own in chunks:
+            whole = lax.all_gather(own, "row", axis=0, tiled=True)
             products.append(negative_product(parent_inverse, [whole], jnp.zeros((1,), jnp.int32)))
             blocks.append(summed(products[-1]))
-    own_rows = jnp.concatenate(own_rows, axis=1)
     grams = []
     for chunk, block in enumerate(blocks):
-        waits = [products[-1]] if chunk < CHUNKS - 1 else grams
+        waits = [products[-1]] if chunk < len(blocks) - 1 else grams
         gram = lax.dot_general(
             own_rows,
             after(block, *waits),

time: 491 us -> 464 us (0.945); the launches traced: 490 us -> 457 us
  waiting for transfers between devices: 212 us -> 165 us
  starting transfers between devices: 88.2 us -> 63 us
  Pallas kernels: 147 us -> 165 us
  local copies, waits for them, and re-layouts: 5.2 us -> 19.5 us
  other arithmetic: 13.3 us -> 18.3 us
    reduce_scatter x2 -> x3, waiting for transfers between devices: 52.4 us -> 11 us  [summed(): lax.psum_scatter(after(partial_block, *others), 'col', scatter_dimension=...]
    ppermute x28 -> x7, starting transfers between devices: 59.8 us -> 28.5 us  [move(): return lax.ppermute(value, ('row', 'col'), pairs)]
    ppermute x28 -> x7, waiting for transfers between devices: 83.1 us -> 101 us  [move(): return lax.ppermute(value, ('row', 'col'), pairs)]
    ppermute x6 -> x9, waiting for transfers between devices: 45.6 us -> 28 us  [sum_over_row(): lax.ppermute(send, 'row', [(i, i ^ 1 << bit) for i in range(count)])]
    pallas_call x4 -> x6, Pallas kernels: 147 us -> 165 us  [negative_product(): pl.pallas_call(functools.partial(product_kernel, count), grid_spec=pltpu....]
    unnamed x28 -> x34, local copies, waits for them, and re-layouts: 0.05 us -> 11.3 us
    ppermute x14 -> x21, waiting for transfers between devices: 26.8 us -> 21.3 us  [cross(): return [lax.ppermute(piece, 'row', pairs) for piece in pieces]]
    ppermute x6 -> x9, starting transfers between devices: 6.54 us -> 10.4 us  [sum_over_row(): lax.ppermute(send, 'row', [(i, i ^ 1 << bit) for i in range(count)])]
  transfers between devices with their start and end apart: 53 -> 43, of which waited for: 20 -> 20; matrix products, arithmetic and copies ran while one was open for 4% -> 7% of each run, Pallas kernels for 30% -> 36%
where the time goes in v6:
time: 464 us; the launch traced here: 457 us
  waiting for transfers between devices  165 us (36%)
  Pallas kernels  165 us (36%)
  starting transfers between devices  63 us (14%)
  local copies, waits for them, and re-layouts  19.5 us (4%)
  other arithmetic  18.3 us (4%)
  between operations  14.4 us (3%)
  matrix products  11.8 us (3%)
    pallas_call x6, Pallas kernels, negative_product(): pl.pallas_call(functools.partial(product_kernel, count), grid_spec=pltpu....  165 us
    ppermute x7, waiting for transfers between devices, move(): return lax.ppermute(value, ('row', 'col'), pairs)  101 us
    ppermute x7, starting transfers between devices, move(): return lax.ppermute(value, ('row', 'col'), pairs)  28.5 us
    ppermute x9, waiting for transfers between devices, sum_over_row(): lax.ppermute(send, 'row', [(i, i ^ 1 << bit) for i in range(count)])  28 us
    ppermute x21, waiting for transfers between devices, cross(): return [lax.ppermute(piece, 'row', pairs) for piece in pieces]  21.3 us
    ppermute x21, starting transfers between devices, cross(): return [lax.ppermute(piece, 'row', pairs) for piece in pieces]  18.2 us
    dot_general x3, matrix products, shards(): lax.dot_general(own_rows, after(block, *waits), (((0,), (0,)), ((), ())),...  11.8 us
    unnamed x34, local copies, waits for them, and re-layouts  11.3 us
  transfers between devices with their start and end apart: 43, of which 20 were waited for; matrix products, arithmetic and copies ran while one was open for 7% of the time, Pallas kernels for 36%

profile of v6, /device:TPU:0, one launch (start us, length us, event | category | flops | bytes accessed | tf_op | source)
XLA Modules:
  0.0 457.1 jit_solution(9073831996305740808)
XLA Ops:
  12.0 14.2 %collective-permute-done.refs_5_ = f32[768,384]{1,0:T(8,128)S(1)} collective-permute-done((f32[768,384]{1,0:T(8,128)S(1)}, f32[768,384]{1,0:T(8,128)S(1)}, u32[]{:S(2)}, u32[]{:S(2)}) %collective-permute-start) | collective-permute-done | bytes 1179680 | tf_op jit(solution)/shard_map/ppermute | solution.py:99
  27.5 3.8 slice_select_fusion
  36.0 31.3 %shard_map.59.refs_8_ = f32[3072,384]{1,0:T(8,128)S(1)} custom-call(s32[4]{0:T(128)S(1)} %get-tuple-element.74.place_ref, f32[3072,6144]{1,0:T(8,128)} %refs_3_.11, f32[3072,6144]{1,0:T(8,128)} %refs_3_.11, f32[3072,6144]{1,0:T(8,128)} %refs_3_.11, f32[3072,6144]{1,0:T(8,128)} %refs_3_.11, f32[768,384]{1,0:T(8,128)S(1)} %get-tuple-element.36.refs_4_, ...), custom_call_target="tpu_custom_call" | custom-call | flops 21743271936 | bytes 51904512 | tf_op jit(solution)/shard_map/pallas_call | solution.py:58
  69.5 70.7 %collective-permute-done.6 = f32[768,512]{1,0:T(8,128)S(1)} collective-permute-done((f32[768,512]{1,0:T(8,128)S(1)}, f32[768,512]{1,0:T(8,128)S(1)}, u32[]{:S(2)}, u32[]{:S(2)}) %collective-permute-start.6) | collective-permute-done | bytes 1572896 | tf_op jit(solution)/shard_map/ppermute | solution.py:133
  144.8 30.4 %shard_map.60 = f32[3072,384]{1,0:T(8,128)S(1)} custom-call(s32[4]{0:T(128)S(1)} %get-tuple-element.75.place_ref, f32[3072,6144]{1,0:T(8,128)} %refs_3_.11, f32[3072,6144]{1,0:T(8,128)} %refs_3_.11, f32[3072,6144]{1,0:T(8,128)} %refs_3_.11, f32[3072,6144]{1,0:T(8,128)} %refs_3_.11, f32[768,384]{1,0:T(8,128)S(1)} %collective-permute-done.2.refs_4_, ...), custom_call_target="tpu_custom_call" | custom-call | flops 21743271936 | bytes 51904512 | tf_op jit(solution)/shard_map/pallas_call | solution.py:58
  182.6 30.2 %shard_map.61.refs_8_ = f32[3072,384]{1,0:T(8,128)S(1)} custom-call(s32[4]{0:T(128)S(1)} %get-tuple-element.74.place_ref, f32[3072,6144]{1,0:T(8,128)} %refs_3_.11, f32[3072,6144]{1,0:T(8,128)} %refs_3_.11, f32[3072,6144]{1,0:T(8,128)} %refs_3_.11, f32[3072,6144]{1,0:T(8,128)} %refs_3_.11, f32[768,384]{1,0:T(8,128)S(1)} %get-tuple-element.47.refs_4_, ...), custom_call_target="tpu_custom_call" | custom-call | flops 21743271936 | bytes 51904512 | tf_op jit(solution)/shard_map/pallas_call | solution.py:58
  215.0 3.6 collective-permute-start.16
  222.8 30.5 %shard_map.62 = f32[3072,384]{1,0:T(8,128)S(1)} custom-call(s32[4]{0:T(128)S(1)} %get-tuple-element.75.place_ref, f32[3072,6144]{1,0:T(8,128)} %refs_3_.11, f32[3072,6144]{1,0:T(8,128)} %refs_3_.11, f32[3072,6144]{1,0:T(8,128)} %refs_3_.11, f32[3072,6144]{1,0:T(8,128)} %refs_3_.11, f32[768,384]{1,0:T(8,128)S(1)} %collective-permute-done.12.refs_4_, ...), custom_call_target="tpu_custom_call" | custom-call | flops 21743271936 | bytes 51904512 | tf_op jit(solution)/shard_map/pallas_call | solution.py:58
  260.1 21.0 %shard_map.63.refs_8_ = f32[3072,256]{1,0:T(8,128)S(1)} custom-call(s32[4]{0:T(128)S(1)} %get-tuple-element.74.place_ref, f32[3072,6144]{1,0:T(8,128)} %refs_3_.11, f32[3072,6144]{1,0:T(8,128)} %refs_3_.11, f32[3072,6144]{1,0:T(8,128)} %refs_3_.11, f32[3072,6144]{1,0:T(8,128)} %refs_3_.11, f32[768,256]{1,0:T(8,128)S(1)} %slice.31.refs_4_, ...), custom_call_target="tpu_custom_call" | custom-call | flops 14495514624 | bytes 47185920 | tf_op jit(solution)/shard_map/pallas_call | solution.py:58
  284.6 21.4 %shard_map.64 = f32[3072,256]{1,0:T(8,128)} custom-call(s32[4]{0:T(128)S(1)} %get-tuple-element.75.place_ref, f32[3072,6144]{1,0:T(8,128)} %refs_3_.11, f32[3072,6144]{1,0:T(8,128)} %refs_3_.11, f32[3072,6144]{1,0:T(8,128)} %refs_3_.11, f32[3072,6144]{1,0:T(8,128)} %refs_3_.11, f32[768,256]{1,0:T(8,128)S(1)} %collective-permute-done.19.refs_4_, ...), custom_call_target="tpu_custom_call" | custom-call | flops 14495514624 | bytes 47185920 | tf_op jit(solution)/shard_map/pallas_call | solution.py:58
  306.0 6.5 %collective-permute-start.27 = (f32[768,512]{1,0:T(8,128)}, f32[768,512]{1,0:T(8,128)}, u32[]{:S(2)}, u32[]{:S(2)}) collective-permute-start(f32[768,512]{1,0:T(8,128)} %collective-permute-done.10), channel_id=1, source_target_pairs={{0,24},{2,26},{5,17},{7,19},{8,8},{10,10},{13,1},{15,3},{16,28},{1... | collective-permute-start | bytes 4718600 | tf_op jit(solution)/shard_map/ppermute | solution.py:133
  312.6 12.4 %collective-permute-start.25 = (f32[768,512]{1,0:T(8,128)}, f32[768,512]{1,0:T(8,128)}, u32[]{:S(2)}, u32[]{:S(2)}) collective-permute-start(f32[768,512]{1,0:T(8,128)} %copy-done.15), channel_id=1, source_target_pairs={{0,8},{2,2},{5,1},{7,11},{8,16},{10,26},{13,25},{15,19},{16,12},{1... | collective-permute-start | bytes 4718600 | tf_op jit(solution)/shard_map/ppermute | solution.py:133
  329.7 16.9 %collective-permute-done.25 = f32[768,512]{1,0:T(8,128)} collective-permute-done((f32[768,512]{1,0:T(8,128)}, f32[768,512]{1,0:T(8,128)}, u32[]{:S(2)}, u32[]{:S(2)}) %collective-permute-start.25) | collective-permute-done | bytes 1572896 | tf_op jit(solution)/shard_map/ppermute | solution.py:133
  346.5 11.8 %collective-permute-done.26 = f32[768,512]{1,0:T(8,128)} collective-permute-done((f32[768,512]{1,0:T(8,128)}, f32[768,512]{1,0:T(8,128)}, u32[]{:S(2)}, u32[]{:S(2)}) %collective-permute-start.26) | collective-permute-done | bytes 1572896 | tf_op jit(solution)/shard_map/ppermute | solution.py:133
  358.3 4.3 fusion.6
  362.6 4.1 fusion.2
  368.9 3.9 fusion.1
  382.3 7.8 %collective-permute-done.29 = f32[2,128,384]{2,1,0:T(8,128)S(1)} collective-permute-done((f32[2,128,384]{2,1,0:T(8,128)}, f32[2,128,384]{2,1,0:T(8,128)S(1)}, u32[]{:S(2)}, u32[]{:S(2)}) %collective-permute-start.29) | collective-permute-done | bytes 393248 | tf_op jit(solution)/shard_map/ppermute | solution.py:111
  393.5 4.2 collective-permute-done.32
  401.9 3.5 collective-permute-done.33
  406.1 11.0 %reduce-scatter.8.cloned.1.call-done = f32[768,256]{1,0:T(8,128)} async-done(((f32[3072,256]{1,0:T(8,128)}), f32[768,256]{1,0:T(8,128)}) %reduce-scatter.8.cloned.1.call-update) | async-done | bytes 786448 | tf_op jit(solution)/shard_map/reduce_scatter | solution.py:189
  417.1 3.8 fusion
  424.6 6.9 %collective-permute-done.35 = f32[2,128,256]{2,1,0:T(8,128)S(1)} collective-permute-done((f32[2,128,256]{2,1,0:T(8,128)S(1)}, f32[2,128,256]{2,1,0:T(8,128)S(1)}, u32[]{:S(2)}, u32[]{:S(2)}) %collective-permute-start.35) | collective-permute-done | bytes 262176 | tf_op jit(solution)/shard_map/ppermute | solution.py:111
  433.6 3.7 collective-permute-done.36
  (136 shorter events, 85.0 us)
Async XLA Ops:
  7.2 355.4 %reduce-scatter.4.cloned.1.call-start = ((), (), s32[]{:S(2)}) async-start(), calls=%async_computation.3 | async-start | bytes 5898240 | tf_op jit(solution)/shard_map/reduce_scatter | solution.py:189
  9.0 17.2 %collective-permute-start = (f32[768,384]{1,0:T(8,128)S(1)}, f32[768,384]{1,0:T(8,128)S(1)}, u32[]{:S(2)}, u32[]{:S(2)}) collective-permute-start(f32[768,384]{1,0:T(8,128)S(1)} %get-tuple-element.36.refs_4_), channel_id=1, source_target_pairs={{0,8},{4,20},{8,0},{12,28},{16,24},{20,4},{24,16},{28,12},{1,9},{5... | collective-permute-start | bytes 3538952 | tf_op jit(solution)/shard_map/ppermute | solution.py:99
  26.2 9.8 %collective-permute-start.4 = (f32[768,384]{1,0:T(8,128)S(1)}, f32[768,384]{1,0:T(8,128)}, u32[]{:S(2)}, u32[]{:S(2)}) collective-permute-start(f32[768,384]{1,0:T(8,128)S(1)} %get-tuple-element.36.refs_4_), channel_id=1, source_target_pairs={{0,4},{4,0},{8,12},{12,8},{16,20},{20,16},{24,28},{28,24},{1,5},{5... | collective-permute-start | bytes 3538952 | tf_op jit(solution)/shard_map/ppermute | solution.py:99
  31.2 38.2 %collective-permute-start.5 = (f32[768,512]{1,0:T(8,128)S(1)}, f32[768,512]{1,0:T(8,128)S(1)}, u32[]{:S(2)}, u32[]{:S(2)}) collective-permute-start(f32[768,512]{1,0:T(8,128)S(1)} %get-tuple-element.37), channel_id=1, source_target_pairs={{1,0},{2,8},{4,5},{7,13},{8,2},{11,10},{13,7},{14,15},{17,16},{18,... | collective-permute-start | bytes 4718600 | tf_op jit(solution)/shard_map/ppermute | solution.py:133
  32.5 107.7 %collective-permute-start.6 = (f32[768,512]{1,0:T(8,128)S(1)}, f32[768,512]{1,0:T(8,128)S(1)}, u32[]{:S(2)}, u32[]{:S(2)}) collective-permute-start(f32[768,512]{1,0:T(8,128)S(1)} %get-tuple-element.38), channel_id=1, source_target_pairs={{2,0},{3,8},{6,13},{7,5},{8,10},{9,2},{12,7},{13,15},{18,16},{19,2... | collective-permute-start | bytes 4718600 | tf_op jit(solution)/shard_map/ppermute | solution.py:133
  33.8 106.4 %collective-permute-start.3 = (f32[768,384]{1,0:T(8,128)S(1)}, f32[768,384]{1,0:T(8,128)S(1)}, u32[]{:S(2)}, u32[]{:S(2)}) collective-permute-start(f32[768,384]{1,0:T(8,128)S(1)} %collective-permute-done.refs_5_), channel_id=1, source_target_pairs={{0,16},{4,12},{8,24},{12,4},{16,0},{20,28},{24,8},{28,20},{1,17},{... | collective-permute-start | bytes 3538952 | tf_op jit(solution)/shard_map/ppermute | solution.py:99
  36.0 104.3 %collective-permute-start.2 = (f32[768,384]{1,0:T(8,128)S(1)}, f32[768,384]{1,0:T(8,128)S(1)}, u32[]{:S(2)}, u32[]{:S(2)}) collective-permute-start(f32[768,384]{1,0:T(8,128)S(1)} %get-tuple-element.36.refs_4_), channel_id=1, source_target_pairs={{0,16},{4,12},{8,24},{12,4},{16,0},{20,28},{24,8},{28,20},{1,17},{... | collective-permute-start | bytes 3538952 | tf_op jit(solution)/shard_map/ppermute | solution.py:99
  140.7 36.6 %collective-permute-start.9 = (f32[768,384]{1,0:T(8,128)S(1)}, f32[768,384]{1,0:T(8,128)S(1)}, u32[]{:S(2)}, u32[]{:S(2)}) collective-permute-start(f32[768,384]{1,0:T(8,128)S(1)} %get-tuple-element.47.refs_4_), channel_id=1, source_target_pairs={{0,8},{4,20},{8,0},{12,28},{16,24},{20,4},{24,16},{28,12},{1,9},{5... | collective-permute-start | bytes 3538952 | tf_op jit(solution)/shard_map/ppermute | solution.py:99
  140.7 36.6 %collective-permute-start.10 = (f32[768,512]{1,0:T(8,128)}, f32[768,512]{1,0:T(8,128)}, u32[]{:S(2)}, u32[]{:S(2)}) collective-permute-start(f32[768,512]{1,0:T(8,128)} %get-tuple-element.42), channel_id=1, source_target_pairs={{1,8},{3,0},{4,13},{6,5},{9,10},{11,2},{12,15},{14,7},{17,24},{19,... | collective-permute-start | bytes 4718600 | tf_op jit(solution)/shard_map/ppermute | solution.py:133
  177.4 191.6 %reduce-scatter.6.cloned.1.call-start = ((), (), s32[]{:S(2)}) async-start(), calls=%async_computation.4 | async-start | bytes 5898240 | tf_op jit(solution)/shard_map/reduce_scatter | solution.py:189
  180.6 34.4 %collective-permute-start.13 = (f32[768,384]{1,0:T(8,128)S(1)}, f32[768,384]{1,0:T(8,128)S(1)}, u32[]{:S(2)}, u32[]{:S(2)}) collective-permute-start(f32[768,384]{1,0:T(8,128)S(1)} %collective-permute-done.9.refs_5_), channel_id=1, source_target_pairs={{0,16},{4,12},{8,24},{12,4},{16,0},{20,28},{24,8},{28,20},{1,17},{... | collective-permute-start | bytes 3538952 | tf_op jit(solution)/shard_map/ppermute | solution.py:99
  182.0 36.6 %collective-permute-start.12 = (f32[768,384]{1,0:T(8,128)S(1)}, f32[768,384]{1,0:T(8,128)S(1)}, u32[]{:S(2)}, u32[]{:S(2)}) collective-permute-start(f32[768,384]{1,0:T(8,128)S(1)} %get-tuple-element.47.refs_4_), channel_id=1, source_target_pairs={{0,16},{4,12},{8,24},{12,4},{16,0},{20,28},{24,8},{28,20},{1,17},{... | collective-permute-start | bytes 3538952 | tf_op jit(solution)/shard_map/ppermute | solution.py:99
  219.9 35.6 %collective-permute-start.17 = (f32[768,256]{1,0:T(8,128)S(1)}, f32[768,256]{1,0:T(8,128)S(1)}, u32[]{:S(2)}, u32[]{:S(2)}) collective-permute-start(f32[768,256]{1,0:T(8,128)S(1)} %slice.31.refs_4_), channel_id=1, source_target_pairs={{0,8},{4,20},{8,0},{12,28},{16,24},{20,4},{24,16},{28,12},{1,9},{5... | collective-permute-start | bytes 2359304 | tf_op jit(solution)/shard_map/ppermute | solution.py:99
  255.5 161.6 %reduce-scatter.8.cloned.1.call-start = ((), (), s32[]{:S(2)}) async-start(), calls=%async_computation.5 | async-start | bytes 3932160 | tf_op jit(solution)/shard_map/reduce_scatter | solution.py:189
  258.1 23.0 %collective-permute-start.20 = (f32[768,256]{1,0:T(8,128)S(1)}, f32[768,256]{1,0:T(8,128)S(1)}, u32[]{:S(2)}, u32[]{:S(2)}) collective-permute-start(f32[768,256]{1,0:T(8,128)S(1)} %collective-permute-done.17.refs_5_), channel_id=1, source_target_pairs={{0,16},{4,12},{8,24},{12,4},{16,0},{20,28},{24,8},{28,20},{1,17},{... | collective-permute-start | bytes 2359304 | tf_op jit(solution)/shard_map/ppermute | solution.py:99
  259.7 21.7 %collective-permute-start.19 = (f32[768,256]{1,0:T(8,128)S(1)}, f32[768,256]{1,0:T(8,128)S(1)}, u32[]{:S(2)}, u32[]{:S(2)}) collective-permute-start(f32[768,256]{1,0:T(8,128)S(1)} %slice.31.refs_4_), channel_id=1, source_target_pairs={{0,16},{4,12},{8,24},{12,4},{16,0},{20,28},{24,8},{28,20},{1,17},{... | collective-permute-start | bytes 2359304 | tf_op jit(solution)/shard_map/ppermute | solution.py:99
  281.7 45.9 %collective-permute-start.24 = (f32[768,1024]{1,0:T(8,128)}, f32[768,1024]{1,0:T(8,128)S(1)}, u32[]{:S(2)}, u32[]{:S(2)}) collective-permute-start(f32[768,1024]{1,0:T(8,128)} %param.5), channel_id=1, source_target_pairs={{0,0},{5,9},{10,18},{15,27},{16,4},{21,13},{26,22},{31,31}} | collective-permute-start | bytes 9437192 | tf_op jit(solution)/shard_map/ppermute | solution.py:133
  306.0 23.6 %collective-permute-start.27 = (f32[768,512]{1,0:T(8,128)}, f32[768,512]{1,0:T(8,128)}, u32[]{:S(2)}, u32[]{:S(2)}) collective-permute-start(f32[768,512]{1,0:T(8,128)} %collective-permute-done.10), channel_id=1, source_target_pairs={{0,24},{2,26},{5,17},{7,19},{8,8},{10,10},{13,1},{15,3},{16,28},{1... | collective-permute-start | bytes 4718600 | tf_op jit(solution)/shard_map/ppermute | solution.py:133
  312.6 34.0 %collective-permute-start.25 = (f32[768,512]{1,0:T(8,128)}, f32[768,512]{1,0:T(8,128)}, u32[]{:S(2)}, u32[]{:S(2)}) collective-permute-start(f32[768,512]{1,0:T(8,128)} %copy-done.15), channel_id=1, source_target_pairs={{0,8},{2,2},{5,1},{7,11},{8,16},{10,26},{13,25},{15,19},{16,12},{1... | collective-permute-start | bytes 4718600 | tf_op jit(solution)/shard_map/ppermute | solution.py:133
  325.0 33.4 %collective-permute-start.26 = (f32[768,512]{1,0:T(8,128)}, f32[768,512]{1,0:T(8,128)}, u32[]{:S(2)}, u32[]{:S(2)}) collective-permute-start(f32[768,512]{1,0:T(8,128)} %copy-done.16), channel_id=1, source_target_pairs={{0,16},{2,10},{5,25},{7,3},{8,24},{10,2},{13,17},{15,11},{16,20},{... | collective-permute-start | bytes 4718600 | tf_op jit(solution)/shard_map/ppermute | solution.py:133
  377.9 12.2 %collective-permute-start.29 = (f32[2,128,384]{2,1,0:T(8,128)}, f32[2,128,384]{2,1,0:T(8,128)S(1)}, u32[]{:S(2)}, u32[]{:S(2)}) collective-permute-start(f32[2,128,384]{2,1,0:T(8,128)} %dynamic-slice_bitcast_fusion.4), channel_id=1, source_target_pairs={{0,8},{4,12},{8,0},{12,4},{16,24},{20,28},{24,16},{28,20},{1,9},{5... | collective-permute-start | bytes 1179656 | tf_op jit(solution)/shard_map/ppermute | solution.py:111
  380.2 17.5 %collective-permute-start.32 = (f32[2,128,384]{2,1,0:T(8,128)}, f32[2,128,384]{2,1,0:T(8,128)}, u32[]{:S(2)}, u32[]{:S(2)}) collective-permute-start(f32[2,128,384]{2,1,0:T(8,128)} %dynamic-slice_bitcast_fusion.3), channel_id=1, source_target_pairs={{0,8},{4,12},{8,0},{12,4},{16,24},{20,28},{24,16},{28,20},{1,9},{5... | collective-permute-start | bytes 1179656 | tf_op jit(solution)/shard_map/ppermute | solution.py:111
  391.2 10.0 %collective-permute-start.30 = (f32[128,384]{1,0:T(8,128)S(1)}, f32[128,384]{1,0:T(8,128)S(1)}, u32[]{:S(2)}, u32[]{:S(2)}) collective-permute-start(f32[128,384]{1,0:T(8,128)S(1)} %dynamic-slice_bitcast_fusion.7), channel_id=1, source_target_pairs={{0,16},{4,20},{8,24},{12,28},{16,0},{20,4},{24,8},{28,12},{1,17},{... | collective-permute-start | bytes 589832 | tf_op jit(solution)/shard_map/ppermute | solution.py:111
  439.5 10.1 %collective-permute-start.38 = (f32[128,256]{1,0:T(8,128)S(1)}, f32[128,256]{1,0:T(8,128)S(1)}, u32[]{:S(2)}, u32[]{:S(2)}) collective-permute-start(f32[128,256]{1,0:T(8,128)S(1)} %get-tuple-element.73), channel_id=1, source_target_pairs={{0,2},{1,3},{2,0},{3,1},{4,6},{5,7},{6,4},{7,5},{8,10},{9,11},{10,... | collective-permute-start | bytes 393224 | tf_op jit(solution)/shard_map/ppermute | solution.py:121
  (36 other events, 297.1 us)
Sparse Core Ops, SparseCore 0:
  177.5 87.7 reduce-scatter.3
  267.6 85.7 reduce-scatter.5
  356.3 60.7 reduce-scatter.7

commit v7 on v6

--- a/solution.py
+++ b/solution.py
@@ -152,37 +152,31 @@
     def all_after(pieces, *others):
         return [after(piece, *others) for piece in pieces]
 
-    rounds = [(k, k % (column_count - 1) + 1) for k in range(1, column_count)]
     panel_left, panel_right = jnp.split(panel, 2, axis=1)
-
-    def over_col(shifts, *others):
-        left, right = shifts
-
+    to_goal = (row_index % column_count) ^ column_index
+
+    def right_of_neighbour():
+        return move(panel_right, lambda r, c: (r ^ group, c))
+
+    def over_col(right, k, *others):
         def target(r, c):
-            goal = r % column_count
-            return {left: (r, goal), right: (r ^ group, goal)}.get(goal ^ c)
-
-        sends_right = (row_index % column_count) ^ column_index == right
-        return move(after(jnp.where(sends_right, panel_right, panel_left), *others), target)
-
-    def over_row(arrived):
-        def target(left, right):
-            def of(r, c):
-                for source, shift in ((r, left), (r ^ group, right)):
-                    if source % column_count == c:
-                        return (c ^ shift) * group + source // column_count, c
-
-            return of
-
-        def still(r, c):
-            return (c * group + r // column_count, c) if r % column_count == c else None
-
-        halves = list(jnp.split(move(panel, still), 2, axis=1))
+            return (r, c ^ k) if r % column_count ^ c in (k, k ^ group) else None
+
+        return move(after(jnp.where(to_goal == k, panel_left, right), *others), target)
+
+    def over_row(right, arrived):
+        left_parts, right_parts = [panel_left, *arrived], [right, *arrived]
         mine = (row_index // group) ^ column_index
-        for value, shifts in zip(arrived, rounds):
-            value = move(value, target(*shifts))
-            for side in range(2):
-                halves[side] = halves[side] + jnp.where(mine == shifts[side], value, jnp.zeros_like(value))
+        halves = [jnp.zeros_like(panel_left)] * 2
+        for k in range(column_count):
+            other = (k + 1) % column_count
+
+            def target(r, c):
+                shift = {c: k, c ^ group: other}.get(r % column_count)
+                return None if shift is None else ((c ^ shift) * group + r // column_count, c)
+
+            value = move(jnp.where(to_goal == 0, left_parts[k], right_parts[other]), target)
+            halves = [jnp.where(mine == shift, value, held) for shift, held in zip((k, other), halves)]
         return jnp.concatenate(halves, axis=1)
 
     def summed(partial_block, *others):
@@ -198,24 +192,27 @@
             return pieces
 
         mine = link(chunks[:1], orders[:-1])
-        arrived = [over_col(shifts, mine[-1]) for shifts in rounds[:2]]
-        arrived += [over_col(shifts, *arrived) for shifts in rounds[2:]]
+        right = right_of_neighbour()
+        arrived = [over_col(right, k) for k in range(1, min(3, column_count))]
+        early = len(arrived)
+        arrived += [over_col(right, k, *arrived) for k in range(3, column_count)]
         last = None
         for chunk in range(len(chunks)):
             theirs = partner(all_after(mine, mine[-1]) if last is None else all_after(mine, last))
             late = cross(all_after(mine, theirs[-1]), orders[-1], row_count)
             last = negative_product(parent_inverse, mine + theirs, place[:half])
-            waits = [last] if chunk else [last] + arrived[:2]
+            waits = [last] if chunk else [last] + arrived[:early]
             late = late + partner(all_after(late, *waits))
             if chunk + 1 < len(chunks):
                 mine = link(all_after([chunks[chunk + 1]], last), orders[:-1])
             last = negative_product(parent_inverse, late, place[half:], last)
             products.append(last)
             waits = mine[-1:] if chunk + 1 < len(chunks) else []
-            blocks.append(summed(last, *waits, *([] if chunk else arrived[2:])))
-        own_rows = over_row([after(value, products[0]) for value in arrived])
+            blocks.append(summed(last, *waits, *([] if chunk else arrived[early:])))
+        own_rows = over_row(right, [after(value, products[0]) for value in arrived])
     else:
-        own_rows = over_row([over_col(shifts) for shifts in rounds])
+        right = right_of_neighbour()
+        own_rows = over_row(right, [over_col(right, k) for k in range(1, column_count)])
         for own in chunks:
             whole = lax.all_gather(own, "row", axis=0, tiled=True)
             products.append(negative_product(parent_inverse, [whole], jnp.zeros((1,), jnp.int32)))

time: 464 us -> 430 us (0.927)
  waiting for transfers between devices: 165 us -> 119 us
  other arithmetic: 18.3 us -> 23.5 us
    ppermute x7 -> x8, waiting for transfers between devices: 101 us -> 39.2 us  [move(): return lax.ppermute(value, ('row', 'col'), pairs)]
    ppermute x21, waiting for transfers between devices: 21.3 us -> 31.7 us  [cross(): return [lax.ppermute(piece, 'row', pairs) for piece in pieces]]
    select_n x1 -> x3, other arithmetic: 3.78 us -> 13.3 us  [the longest x1 5.87 us: over_row(): jnp.where(to_goal == 0, left_parts[k], right_parts[other])]
    ppermute x7 -> x8, starting transfers between devices: 28.5 us -> 33 us  [move(): return lax.ppermute(value, ('row', 'col'), pairs)]
    unnamed x34 -> x40, local copies, waits for them, and re-layouts: 11.3 us -> 14.3 us
  transfers between devices with their start and end apart: 43 -> 44, of which waited for: 20 -> 18; matrix products, arithmetic and copies ran while one was open for 7% -> 9% of each run, Pallas kernels for 36% -> 39%
where the time goes in v7:
time: 430 us; the launch traced here: 423 us
  Pallas kernels  165 us (38%)
  waiting for transfers between devices  119 us (28%)
  starting transfers between devices  64.9 us (15%)
  local copies, waits for them, and re-layouts  24 us (6%)
  other arithmetic  23.5 us (5%)
  between operations  14.7 us (3%)
  matrix products  11.6 us (3%)
    pallas_call x6, Pallas kernels, negative_product(): pl.pallas_call(functools.partial(product_kernel, count), grid_spec=pltpu....  165 us
    ppermute x8, waiting for transfers between devices, move(): return lax.ppermute(value, ('row', 'col'), pairs)  39.2 us
    ppermute x8, starting transfers between devices, move(): return lax.ppermute(value, ('row', 'col'), pairs)  33 us
    ppermute x9, waiting for transfers between devices, sum_over_row(): lax.ppermute(send, 'row', [(i, i ^ 1 << bit) for i in range(count)])  32.5 us
    ppermute x21, waiting for transfers between devices, cross(): return [lax.ppermute(piece, 'row', pairs) for piece in pieces]  31.7 us
    ppermute x21, starting transfers between devices, cross(): return [lax.ppermute(piece, 'row', pairs) for piece in pieces]  17.6 us
    unnamed x40, local copies, waits for them, and re-layouts  14.3 us
    reduce_scatter x3, waiting for transfers between devices, summed(): lax.psum_scatter(after(partial_block, *others), 'col', scatter_dimension=...  12.3 us
  transfers between devices with their start and end apart: 44, of which 18 were waited for; matrix products, arithmetic and copies ran while one was open for 9% of the time, Pallas kernels for 39%

profile of v7, /device:TPU:0, one launch (start us, length us, event | category | flops | bytes accessed | tf_op | source)
XLA Modules:
  0.0 423.0 jit_solution(17433225752342696292)
XLA Ops:
  14.1 22.8 %collective-permute-done.refs_5_ = f32[768,384]{1,0:T(8,128)S(1)} collective-permute-done((f32[768,384]{1,0:T(8,128)S(1)}, f32[768,384]{1,0:T(8,128)S(1)}, u32[]{:S(2)}, u32[]{:S(2)}) %collective-permute-start) | collective-permute-done | bytes 1179680 | tf_op jit(solution)/shard_map/ppermute | solution.py:99
  38.1 22.0 %collective-permute-done.5 = f32[768,512]{1,0:T(8,128)} collective-permute-done((f32[768,512]{1,0:T(8,128)}, f32[768,512]{1,0:T(8,128)}, u32[]{:S(2)}, u32[]{:S(2)}) %collective-permute-start.5) | collective-permute-done | bytes 1572896 | tf_op jit(solution)/shard_map/ppermute | solution.py:133
  60.2 3.8 slice_select_fusion.1
  65.2 5.2 %collective-permute-start.7 = (f32[768,512]{1,0:T(8,128)S(1)}, f32[768,512]{1,0:T(8,128)S(1)}, u32[]{:S(2)}, u32[]{:S(2)}) collective-permute-start(f32[768,512]{1,0:T(8,128)S(1)} %get-tuple-element.63), channel_id=1, source_target_pairs={{0,2},{2,0},{5,7},{7,5},{8,10},{10,8},{13,15},{15,13},{16,18},{18,... | collective-permute-start | bytes 4718600 | tf_op jit(solution)/shard_map/ppermute | solution.py:133
  72.8 31.3 %shard_map.59.refs_8_ = f32[3072,384]{1,0:T(8,128)S(1)} custom-call(s32[4]{0:T(128)S(1)} %get-tuple-element.74.place_ref, f32[3072,6144]{1,0:T(8,128)} %refs_3_.11, f32[3072,6144]{1,0:T(8,128)} %refs_3_.11, f32[3072,6144]{1,0:T(8,128)} %refs_3_.11, f32[3072,6144]{1,0:T(8,128)} %refs_3_.11, f32[768,384]{1,0:T(8,128)S(1)} %get-tuple-element.34.refs_4_, ...), custom_call_target="tpu_custom_call" | custom-call | flops 21743271936 | bytes 51904512 | tf_op jit(solution)/shard_map/pallas_call | solution.py:58
  110.9 30.4 %shard_map.60 = f32[3072,384]{1,0:T(8,128)S(1)} custom-call(s32[4]{0:T(128)S(1)} %get-tuple-element.75.place_ref, f32[3072,6144]{1,0:T(8,128)} %refs_3_.11, f32[3072,6144]{1,0:T(8,128)} %refs_3_.11, f32[3072,6144]{1,0:T(8,128)} %refs_3_.11, f32[3072,6144]{1,0:T(8,128)} %refs_3_.11, f32[768,384]{1,0:T(8,128)S(1)} %collective-permute-done.2.refs_4_, ...), custom_call_target="tpu_custom_call" | custom-call | flops 21743271936 | bytes 51904512 | tf_op jit(solution)/shard_map/pallas_call | solution.py:58
  150.4 30.9 %shard_map.61.refs_8_ = f32[3072,384]{1,0:T(8,128)S(1)} custom-call(s32[4]{0:T(128)S(1)} %get-tuple-element.74.place_ref, f32[3072,6144]{1,0:T(8,128)} %refs_3_.11, f32[3072,6144]{1,0:T(8,128)} %refs_3_.11, f32[3072,6144]{1,0:T(8,128)} %refs_3_.11, f32[3072,6144]{1,0:T(8,128)} %refs_3_.11, f32[768,384]{1,0:T(8,128)S(1)} %get-tuple-element.43.refs_4_, ...), custom_call_target="tpu_custom_call" | custom-call | flops 21743271936 | bytes 51904512 | tf_op jit(solution)/shard_map/pallas_call | solution.py:58
  188.0 30.5 %shard_map.62 = f32[3072,384]{1,0:T(8,128)S(1)} custom-call(s32[4]{0:T(128)S(1)} %get-tuple-element.75.place_ref, f32[3072,6144]{1,0:T(8,128)} %refs_3_.11, f32[3072,6144]{1,0:T(8,128)} %refs_3_.11, f32[3072,6144]{1,0:T(8,128)} %refs_3_.11, f32[3072,6144]{1,0:T(8,128)} %refs_3_.11, f32[768,384]{1,0:T(8,128)S(1)} %collective-permute-done.13.refs_4_, ...), custom_call_target="tpu_custom_call" | custom-call | flops 21743271936 | bytes 51904512 | tf_op jit(solution)/shard_map/pallas_call | solution.py:58
  225.3 20.5 %shard_map.63.refs_8_ = f32[3072,256]{1,0:T(8,128)S(1)} custom-call(s32[4]{0:T(128)S(1)} %get-tuple-element.74.place_ref, f32[3072,6144]{1,0:T(8,128)} %refs_3_.11, f32[3072,6144]{1,0:T(8,128)} %refs_3_.11, f32[3072,6144]{1,0:T(8,128)} %refs_3_.11, f32[3072,6144]{1,0:T(8,128)} %refs_3_.11, f32[768,256]{1,0:T(8,128)S(1)} %slice.31.refs_4_, ...), custom_call_target="tpu_custom_call" | custom-call | flops 14495514624 | bytes 47185920 | tf_op jit(solution)/shard_map/pallas_call | solution.py:58
  249.3 21.4 %shard_map.64 = f32[3072,256]{1,0:T(8,128)} custom-call(s32[4]{0:T(128)S(1)} %get-tuple-element.75.place_ref, f32[3072,6144]{1,0:T(8,128)} %refs_3_.11, f32[3072,6144]{1,0:T(8,128)} %refs_3_.11, f32[3072,6144]{1,0:T(8,128)} %refs_3_.11, f32[3072,6144]{1,0:T(8,128)} %refs_3_.11, f32[768,256]{1,0:T(8,128)S(1)} %collective-permute-done.20.refs_4_, ...), custom_call_target="tpu_custom_call" | custom-call | flops 14495514624 | bytes 47185920 | tf_op jit(solution)/shard_map/pallas_call | solution.py:58
  272.7 5.9 %slice_select_fusion = (f32[768,512]{1,0:T(8,128)}, f32[768,512]{1,0:T(8,128)}, f32[768,512]{1,0:T(8,128)}, f32[768,512]{1,0:T(8,128)}) fusion(f32[768,512]{1,0:T(8,128)} %copy-done.17, f32[768,1024]{1,0:T(8,128)S(1)} %copy-done.5, pred[]{:T(512)S(6)} %eq.40, f32[768,512]{1,0:T(8,128)} %copy-done.18, f32[768,512]{1,0:T(8,128)} %collective-permute-done.11, ...), kind=kLoop, calls=%fused_computation.7 | loop fusion | flops 1572864 | bytes 14155777 | tf_op jit(solution)/shard_map/jit(_where)/select_n | solution.py:178
  278.6 4.1 collective-permute-start.25
  285.0 4.3 %collective-permute-start.27 = (f32[768,512]{1,0:T(8,128)}, f32[768,512]{1,0:T(8,128)}, u32[]{:S(2)}, u32[]{:S(2)}) collective-permute-start(f32[768,512]{1,0:T(8,128)} %get-tuple-element.68), channel_id=1, source_target_pairs={{0,8},{2,2},{5,1},{7,11},{8,16},{10,26},{13,25},{15,19},{16,12},{1... | collective-permute-start | bytes 4718600 | tf_op jit(solution)/shard_map/ppermute | solution.py:133
  289.3 13.5 %collective-permute-start.28 = (f32[768,512]{1,0:T(8,128)}, f32[768,512]{1,0:T(8,128)}, u32[]{:S(2)}, u32[]{:S(2)}) collective-permute-start(f32[768,512]{1,0:T(8,128)} %get-tuple-element.67), channel_id=1, source_target_pairs={{0,0},{2,26},{5,9},{7,19},{8,8},{10,18},{13,1},{15,27},{16,4},{18,... | collective-permute-start | bytes 4718600 | tf_op jit(solution)/shard_map/ppermute | solution.py:133
  302.8 17.2 %collective-permute-done.26 = f32[768,512]{1,0:T(8,128)S(1)} collective-permute-done((f32[768,512]{1,0:T(8,128)}, f32[768,512]{1,0:T(8,128)S(1)}, u32[]{:S(2)}, u32[]{:S(2)}) %collective-permute-start.26) | collective-permute-done | bytes 1572896 | tf_op jit(solution)/shard_map/ppermute | solution.py:133
  324.8 3.9 fusion.2
  330.9 3.9 fusion.1
  345.9 7.7 %collective-permute-done.30 = f32[2,128,384]{2,1,0:T(8,128)S(1)} collective-permute-done((f32[2,128,384]{2,1,0:T(8,128)}, f32[2,128,384]{2,1,0:T(8,128)S(1)}, u32[]{:S(2)}, u32[]{:S(2)}) %collective-permute-start.30) | collective-permute-done | bytes 393248 | tf_op jit(solution)/shard_map/ppermute | solution.py:111
  355.6 6.4 %collective-permute-done.33 = f32[2,128,384]{2,1,0:T(8,128)} collective-permute-done((f32[2,128,384]{2,1,0:T(8,128)}, f32[2,128,384]{2,1,0:T(8,128)}, u32[]{:S(2)}, u32[]{:S(2)}) %collective-permute-start.33) | collective-permute-done | bytes 393248 | tf_op jit(solution)/shard_map/ppermute | solution.py:111
  363.9 5.9 %collective-permute-done.34 = f32[128,384]{1,0:T(8,128)S(1)} collective-permute-done((f32[128,384]{1,0:T(8,128)S(1)}, f32[128,384]{1,0:T(8,128)S(1)}, u32[]{:S(2)}, u32[]{:S(2)}) %collective-permute-start.34) | collective-permute-done | bytes 196640 | tf_op jit(solution)/shard_map/ppermute | solution.py:111
  370.5 12.2 %reduce-scatter.8.cloned.1.call-done = f32[768,256]{1,0:T(8,128)} async-done(((f32[3072,256]{1,0:T(8,128)}), f32[768,256]{1,0:T(8,128)}) %reduce-scatter.8.cloned.1.call-update) | async-done | bytes 786448 | tf_op jit(solution)/shard_map/reduce_scatter | solution.py:183
  382.7 3.8 fusion
  390.2 6.9 %collective-permute-done.36 = f32[2,128,256]{2,1,0:T(8,128)S(1)} collective-permute-done((f32[2,128,256]{2,1,0:T(8,128)S(1)}, f32[2,128,256]{2,1,0:T(8,128)S(1)}, u32[]{:S(2)}, u32[]{:S(2)}) %collective-permute-start.36) | collective-permute-done | bytes 262176 | tf_op jit(solution)/shard_map/ppermute | solution.py:111
  399.3 3.7 collective-permute-done.37
  (146 shorter events, 90.2 us)
Async XLA Ops:
  7.2 317.6 %reduce-scatter.4.cloned.1.call-start = ((), (), s32[]{:S(2)}) async-start(), calls=%async_computation.3 | async-start | bytes 5898240 | tf_op jit(solution)/shard_map/reduce_scatter | solution.py:183
  9.2 27.7 %collective-permute-start = (f32[768,384]{1,0:T(8,128)S(1)}, f32[768,384]{1,0:T(8,128)S(1)}, u32[]{:S(2)}, u32[]{:S(2)}) collective-permute-start(f32[768,384]{1,0:T(8,128)S(1)} %get-tuple-element.34.refs_4_), channel_id=1, source_target_pairs={{0,8},{4,20},{8,0},{12,28},{16,24},{20,4},{24,16},{28,12},{1,9},{5... | collective-permute-start | bytes 3538952 | tf_op jit(solution)/shard_map/ppermute | solution.py:99
  13.5 46.7 %collective-permute-start.5 = (f32[768,512]{1,0:T(8,128)}, f32[768,512]{1,0:T(8,128)}, u32[]{:S(2)}, u32[]{:S(2)}) collective-permute-start(f32[768,512]{1,0:T(8,128)} %split.7), channel_id=1, source_target_pairs={{0,8},{1,9},{2,10},{3,11},{4,12},{5,13},{6,14},{7,15},{8,0},{9,1},... | collective-permute-start | bytes 4718600 | tf_op jit(solution)/shard_map/ppermute | solution.py:133
  36.8 33.6 %collective-permute-start.1 = (f32[768,384]{1,0:T(8,128)S(1)}, f32[768,384]{1,0:T(8,128)}, u32[]{:S(2)}, u32[]{:S(2)}) collective-permute-start(f32[768,384]{1,0:T(8,128)S(1)} %collective-permute-done.refs_5_), channel_id=1, source_target_pairs={{0,4},{4,0},{8,12},{12,8},{16,20},{20,16},{24,28},{28,24},{1,5},{5... | collective-permute-start | bytes 3538952 | tf_op jit(solution)/shard_map/ppermute | solution.py:99
  36.8 36.0 %collective-permute-start.4 = (f32[768,384]{1,0:T(8,128)S(1)}, f32[768,384]{1,0:T(8,128)}, u32[]{:S(2)}, u32[]{:S(2)}) collective-permute-start(f32[768,384]{1,0:T(8,128)S(1)} %get-tuple-element.34.refs_4_), channel_id=1, source_target_pairs={{0,4},{4,0},{8,12},{12,8},{16,20},{20,16},{24,28},{28,24},{1,5},{5... | collective-permute-start | bytes 3538952 | tf_op jit(solution)/shard_map/ppermute | solution.py:99
  63.9 42.3 %collective-permute-start.6 = (f32[768,512]{1,0:T(8,128)S(1)}, f32[768,512]{1,0:T(8,128)S(1)}, u32[]{:S(2)}, u32[]{:S(2)}) collective-permute-start(f32[768,512]{1,0:T(8,128)S(1)} %get-tuple-element.64), channel_id=1, source_target_pairs={{1,0},{3,2},{4,5},{6,7},{9,8},{11,10},{12,13},{14,15},{17,16},{19,... | collective-permute-start | bytes 4718600 | tf_op jit(solution)/shard_map/ppermute | solution.py:133
  65.2 41.0 %collective-permute-start.7 = (f32[768,512]{1,0:T(8,128)S(1)}, f32[768,512]{1,0:T(8,128)S(1)}, u32[]{:S(2)}, u32[]{:S(2)}) collective-permute-start(f32[768,512]{1,0:T(8,128)S(1)} %get-tuple-element.63), channel_id=1, source_target_pairs={{0,2},{2,0},{5,7},{7,5},{8,10},{10,8},{13,15},{15,13},{16,18},{18,... | collective-permute-start | bytes 4718600 | tf_op jit(solution)/shard_map/ppermute | solution.py:133
  70.4 35.9 %collective-permute-start.3 = (f32[768,384]{1,0:T(8,128)S(1)}, f32[768,384]{1,0:T(8,128)S(1)}, u32[]{:S(2)}, u32[]{:S(2)}) collective-permute-start(f32[768,384]{1,0:T(8,128)S(1)} %collective-permute-done.refs_5_), channel_id=1, source_target_pairs={{0,16},{4,12},{8,24},{12,4},{16,0},{20,28},{24,8},{28,20},{1,17},{... | collective-permute-start | bytes 3538952 | tf_op jit(solution)/shard_map/ppermute | solution.py:99
  72.7 33.6 %collective-permute-start.2 = (f32[768,384]{1,0:T(8,128)S(1)}, f32[768,384]{1,0:T(8,128)S(1)}, u32[]{:S(2)}, u32[]{:S(2)}) collective-permute-start(f32[768,384]{1,0:T(8,128)S(1)} %get-tuple-element.34.refs_4_), channel_id=1, source_target_pairs={{0,16},{4,12},{8,24},{12,4},{16,0},{20,28},{24,8},{28,20},{1,17},{... | collective-permute-start | bytes 3538952 | tf_op jit(solution)/shard_map/ppermute | solution.py:99
  106.9 36.6 %collective-permute-start.10 = (f32[768,384]{1,0:T(8,128)S(1)}, f32[768,384]{1,0:T(8,128)S(1)}, u32[]{:S(2)}, u32[]{:S(2)}) collective-permute-start(f32[768,384]{1,0:T(8,128)S(1)} %get-tuple-element.43.refs_4_), channel_id=1, source_target_pairs={{0,8},{4,20},{8,0},{12,28},{16,24},{20,4},{24,16},{28,12},{1,9},{5... | collective-permute-start | bytes 3538952 | tf_op jit(solution)/shard_map/ppermute | solution.py:99
  108.4 35.1 %collective-permute-start.11 = (f32[768,512]{1,0:T(8,128)}, f32[768,512]{1,0:T(8,128)}, u32[]{:S(2)}, u32[]{:S(2)}) collective-permute-start(f32[768,512]{1,0:T(8,128)} %get-tuple-element.38), channel_id=1, source_target_pairs={{1,2},{3,0},{4,7},{6,5},{9,10},{11,8},{12,15},{14,13},{17,18},{19,... | collective-permute-start | bytes 4718600 | tf_op jit(solution)/shard_map/ppermute | solution.py:133
  143.5 187.4 %reduce-scatter.6.cloned.1.call-start = ((), (), s32[]{:S(2)}) async-start(), calls=%async_computation.4 | async-start | bytes 5898240 | tf_op jit(solution)/shard_map/reduce_scatter | solution.py:183
  148.3 35.1 %collective-permute-start.14 = (f32[768,384]{1,0:T(8,128)S(1)}, f32[768,384]{1,0:T(8,128)S(1)}, u32[]{:S(2)}, u32[]{:S(2)}) collective-permute-start(f32[768,384]{1,0:T(8,128)S(1)} %collective-permute-done.10.refs_5_), channel_id=1, source_target_pairs={{0,16},{4,12},{8,24},{12,4},{16,0},{20,28},{24,8},{28,20},{1,17},{... | collective-permute-start | bytes 3538952 | tf_op jit(solution)/shard_map/ppermute | solution.py:99
  148.6 34.9 %collective-permute-start.13 = (f32[768,384]{1,0:T(8,128)S(1)}, f32[768,384]{1,0:T(8,128)S(1)}, u32[]{:S(2)}, u32[]{:S(2)}) collective-permute-start(f32[768,384]{1,0:T(8,128)S(1)} %get-tuple-element.43.refs_4_), channel_id=1, source_target_pairs={{0,16},{4,12},{8,24},{12,4},{16,0},{20,28},{24,8},{28,20},{1,17},{... | collective-permute-start | bytes 3538952 | tf_op jit(solution)/shard_map/ppermute | solution.py:99
  185.1 35.5 %collective-permute-start.18 = (f32[768,256]{1,0:T(8,128)S(1)}, f32[768,256]{1,0:T(8,128)S(1)}, u32[]{:S(2)}, u32[]{:S(2)}) collective-permute-start(f32[768,256]{1,0:T(8,128)S(1)} %slice.31.refs_4_), channel_id=1, source_target_pairs={{0,8},{4,20},{8,0},{12,28},{16,24},{20,4},{24,16},{28,12},{1,9},{5... | collective-permute-start | bytes 2359304 | tf_op jit(solution)/shard_map/ppermute | solution.py:99
  220.7 162.1 %reduce-scatter.8.cloned.1.call-start = ((), (), s32[]{:S(2)}) async-start(), calls=%async_computation.5 | async-start | bytes 3932160 | tf_op jit(solution)/shard_map/reduce_scatter | solution.py:183
  223.3 22.6 %collective-permute-start.21 = (f32[768,256]{1,0:T(8,128)S(1)}, f32[768,256]{1,0:T(8,128)S(1)}, u32[]{:S(2)}, u32[]{:S(2)}) collective-permute-start(f32[768,256]{1,0:T(8,128)S(1)} %collective-permute-done.18.refs_5_), channel_id=1, source_target_pairs={{0,16},{4,12},{8,24},{12,4},{16,0},{20,28},{24,8},{28,20},{1,17},{... | collective-permute-start | bytes 2359304 | tf_op jit(solution)/shard_map/ppermute | solution.py:99
  223.3 22.6 %collective-permute-start.20 = (f32[768,256]{1,0:T(8,128)S(1)}, f32[768,256]{1,0:T(8,128)S(1)}, u32[]{:S(2)}, u32[]{:S(2)}) collective-permute-start(f32[768,256]{1,0:T(8,128)S(1)} %slice.31.refs_4_), channel_id=1, source_target_pairs={{0,16},{4,12},{8,24},{12,4},{16,0},{20,28},{24,8},{28,20},{1,17},{... | collective-permute-start | bytes 2359304 | tf_op jit(solution)/shard_map/ppermute | solution.py:99
  278.6 24.2 %collective-permute-start.25 = (f32[768,512]{1,0:T(8,128)}, f32[768,512]{1,0:T(8,128)S(1)}, u32[]{:S(2)}, u32[]{:S(2)}) collective-permute-start(f32[768,512]{1,0:T(8,128)} %get-tuple-element.70), channel_id=1, source_target_pairs={{0,24},{2,18},{5,17},{7,27},{8,0},{10,10},{13,9},{15,3},{16,28},{1... | collective-permute-start | bytes 4718600 | tf_op jit(solution)/shard_map/ppermute | solution.py:133
  282.7 37.3 %collective-permute-start.26 = (f32[768,512]{1,0:T(8,128)}, f32[768,512]{1,0:T(8,128)S(1)}, u32[]{:S(2)}, u32[]{:S(2)}) collective-permute-start(f32[768,512]{1,0:T(8,128)} %get-tuple-element.69), channel_id=1, source_target_pairs={{0,16},{2,10},{5,25},{7,3},{8,24},{10,2},{13,17},{15,11},{16,20},{... | collective-permute-start | bytes 4718600 | tf_op jit(solution)/shard_map/ppermute | solution.py:133
  285.0 35.0 %collective-permute-start.27 = (f32[768,512]{1,0:T(8,128)}, f32[768,512]{1,0:T(8,128)}, u32[]{:S(2)}, u32[]{:S(2)}) collective-permute-start(f32[768,512]{1,0:T(8,128)} %get-tuple-element.68), channel_id=1, source_target_pairs={{0,8},{2,2},{5,1},{7,11},{8,16},{10,26},{13,25},{15,19},{16,12},{1... | collective-permute-start | bytes 4718600 | tf_op jit(solution)/shard_map/ppermute | solution.py:133
  289.3 31.9 %collective-permute-start.28 = (f32[768,512]{1,0:T(8,128)}, f32[768,512]{1,0:T(8,128)}, u32[]{:S(2)}, u32[]{:S(2)}) collective-permute-start(f32[768,512]{1,0:T(8,128)} %get-tuple-element.67), channel_id=1, source_target_pairs={{0,0},{2,26},{5,9},{7,19},{8,8},{10,18},{13,1},{15,27},{16,4},{18,... | collective-permute-start | bytes 4718600 | tf_op jit(solution)/shard_map/ppermute | solution.py:133
  339.9 13.8 %collective-permute-start.30 = (f32[2,128,384]{2,1,0:T(8,128)}, f32[2,128,384]{2,1,0:T(8,128)S(1)}, u32[]{:S(2)}, u32[]{:S(2)}) collective-permute-start(f32[2,128,384]{2,1,0:T(8,128)} %dynamic-slice_bitcast_fusion.4), channel_id=1, source_target_pairs={{0,8},{4,12},{8,0},{12,4},{16,24},{20,28},{24,16},{28,20},{1,9},{5... | collective-permute-start | bytes 1179656 | tf_op jit(solution)/shard_map/ppermute | solution.py:111
  345.8 16.2 %collective-permute-start.33 = (f32[2,128,384]{2,1,0:T(8,128)}, f32[2,128,384]{2,1,0:T(8,128)}, u32[]{:S(2)}, u32[]{:S(2)}) collective-permute-start(f32[2,128,384]{2,1,0:T(8,128)} %dynamic-slice_bitcast_fusion.3), channel_id=1, source_target_pairs={{0,8},{4,12},{8,0},{12,4},{16,24},{20,28},{24,16},{28,20},{1,9},{5... | collective-permute-start | bytes 1179656 | tf_op jit(solution)/shard_map/ppermute | solution.py:111
  (40 other events, 253.9 us)
Sparse Core Ops, SparseCore 0:
  143.6 87.3 reduce-scatter.3
  233.3 85.7 reduce-scatter.5
  322.0 60.7 reduce-scatter.7

commit v8 on v7

--- a/solution.py
+++ b/solution.py
@@ -8,7 +8,7 @@
 from jax.experimental.pallas import tpu as pltpu
 from jax.sharding import PartitionSpec as P
 
-EIGHTHS = (3, 3, 2)
+EIGHTHS = (2, 2, 3, 1)
 LANES = 128
 MIB = 1 << 20
 
@@ -101,15 +101,18 @@
 
 def sum_over_row(value, count):
     rows, columns = value.shape
+    chips = count // 2
     me = lax.axis_index("row")
-    value = value.reshape((2,) * (count.bit_length() - 1) + (rows // count, columns))
-    for bit in range(count.bit_length() - 1):
-        axis = value.ndim - 3
-        mine = (me >> bit) & 1
-        keep = lax.dynamic_index_in_dim(value, mine, axis, keepdims=False)
-        send = lax.dynamic_index_in_dim(value, 1 - mine, axis, keepdims=False)
-        value = keep + lax.ppermute(send, "row", [(i, i ^ (1 << bit)) for i in range(count)])
-    return value
+    core, chip = me % 2, me // 2
+    value = value.reshape(chips, 2, rows // count, columns)
+    keep = lax.dynamic_index_in_dim(value, core, 1, keepdims=False)
+    send = lax.dynamic_index_in_dim(value, 1 - core, 1, keepdims=False)
+    value = keep + lax.ppermute(send, "row", [(i, i ^ 1) for i in range(count)])
+    total = lax.dynamic_index_in_dim(value, chip, 0, keepdims=False)
+    for mask in range(1, chips):
+        send = lax.dynamic_index_in_dim(value, chip ^ mask, 0, keepdims=False)
+        total = total + lax.ppermute(send, "row", [(i, i ^ (2 * mask)) for i in range(count)])
+    return total
 
 
 def sum_over_col(value, count):
@@ -155,17 +158,17 @@
     panel_left, panel_right = jnp.split(panel, 2, axis=1)
     to_goal = (row_index % column_count) ^ column_index
 
-    def right_of_neighbour():
-        return move(panel_right, lambda r, c: (r ^ group, c))
-
-    def over_col(right, k, *others):
+    def to_neighbour(value):
+        return move(value, lambda r, c: (r ^ group, c))
+
+    def over_col(left, k, *others):
         def target(r, c):
             return (r, c ^ k) if r % column_count ^ c in (k, k ^ group) else None
 
-        return move(after(jnp.where(to_goal == k, panel_left, right), *others), target)
-
-    def over_row(right, arrived):
-        left_parts, right_parts = [panel_left, *arrived], [right, *arrived]
+        return move(after(jnp.where(to_goal == k, panel_right, left), *others), target)
+
+    def over_row(left, arrived):
+        right_parts, left_parts = [panel_right, *arrived], [left, *arrived]
         mine = (row_index // group) ^ column_index
         halves = [jnp.zeros_like(panel_left)] * 2
         for k in range(column_count):
@@ -175,8 +178,8 @@
                 shift = {c: k, c ^ group: other}.get(r % column_count)
                 return None if shift is None else ((c ^ shift) * group + r // column_count, c)
 
-            value = move(jnp.where(to_goal == 0, left_parts[k], right_parts[other]), target)
-            halves = [jnp.where(mine == shift, value, held) for shift, held in zip((k, other), halves)]
+            value = move(jnp.where(to_goal == 0, right_parts[k], left_parts[other]), target)
+            halves = [jnp.where(mine == shift, value, held) for shift, held in zip((other, k), halves)]
         return jnp.concatenate(halves, axis=1)
 
     def summed(partial_block, *others):
@@ -192,27 +195,28 @@
             return pieces
 
         mine = link(chunks[:1], orders[:-1])
-        right = right_of_neighbour()
-        arrived = [over_col(right, k) for k in range(1, min(3, column_count))]
-        early = len(arrived)
-        arrived += [over_col(right, k, *arrived) for k in range(3, column_count)]
+        hopped = to_neighbour(panel_left[:, chunks[0].shape[1] :])
         last = None
         for chunk in range(len(chunks)):
             theirs = partner(all_after(mine, mine[-1]) if last is None else all_after(mine, last))
-            late = cross(all_after(mine, theirs[-1]), orders[-1], row_count)
+            late = cross(all_after(mine, theirs[-1], *([] if chunk else [hopped])), orders[-1], row_count)
             last = negative_product(parent_inverse, mine + theirs, place[:half])
-            waits = [last] if chunk else [last] + arrived[:early]
-            late = late + partner(all_after(late, *waits))
+            if chunk == 0:
+                left = jnp.concatenate([jnp.where(row_index % 2 == 0, mine[1], late[0]), hopped], axis=1)
+                arrived = [over_col(left, k) for k in range(1, min(3, column_count))]
+                early = len(arrived)
+                arrived += [over_col(left, k, *arrived) for k in range(3, column_count)]
+            late = late + partner(all_after(late, last, *(arrived[early:] if chunk == 1 else [])))
             if chunk + 1 < len(chunks):
                 mine = link(all_after([chunks[chunk + 1]], last), orders[:-1])
             last = negative_product(parent_inverse, late, place[half:], last)
             products.append(last)
             waits = mine[-1:] if chunk + 1 < len(chunks) else []
-            blocks.append(summed(last, *waits, *([] if chunk else arrived[early:])))
-        own_rows = over_row(right, [after(value, products[0]) for value in arrived])
+            blocks.append(summed(last, *waits, *([] if chunk else arrived[:early])))
+        own_rows = over_row(left, [after(value, products[1]) for value in arrived])
     else:
-        right = right_of_neighbour()
-        own_rows = over_row(right, [over_col(right, k) for k in range(1, column_count)])
+        left = to_neighbour(panel_left)
+        own_rows = over_row(left, [over_col(left, k) for k in range(1, column_count)])
         for own in chunks:
             whole = lax.all_gather(own, "row", axis=0, tiled=True)
             products.append(negative_product(parent_inverse, [whole], jnp.zeros((1,), jnp.int32)))

time: 430 us -> 497 us (1.16)
  waiting for transfers between devices: 119 us -> 153 us
  starting transfers between devices: 64.9 us -> 81.9 us
  Pallas kernels: 165 us -> 181 us
  local copies, waits for them, and re-layouts: 24 us -> 18.3 us
    ppermute x21 -> x28, waiting for transfers between devices: 31.7 us -> 55.9 us  [cross(): return [lax.ppermute(piece, 'row', pairs) for piece in pieces]]
    ppermute x8, waiting for transfers between devices: 39.2 us -> 57.9 us  [move(): return lax.ppermute(value, ('row', 'col'), pairs)]
    pallas_call x6 -> x8, Pallas kernels: 165 us -> 181 us  [negative_product(): pl.pallas_call(functools.partial(product_kernel, count), grid_spec=pltpu....]
    ppermute x3, starting transfers between devices: 5.44 us -> 17 us  [sum_over_col(): lax.ppermute(send, 'col', [(i, (i + shift) % count) for i in range(count)])]
    ppermute x9 -> x16, waiting for transfers between devices: 32.5 us -> 22.9 us  [the longest x12 19.2 us: sum_over_row(): lax.ppermute(send, 'row', [(i, i ^ 2 * mask) for i in range(count)])]
    ppermute x9 -> x16, starting transfers between devices: 8.36 us -> 14.7 us  [the longest x12 14.1 us: sum_over_row(): lax.ppermute(send, 'row', [(i, i ^ 2 * mask) for i in range(count)])]
    unnamed x40 -> x36, local copies, waits for them, and re-layouts: 14.3 us -> 9.52 us
    dot_general x3 -> x4, matrix products: 11.6 us -> 15.3 us  [shards(): lax.dot_general(own_rows, after(block, *waits), (((0,), (0,)), ((), ())),...]
  transfers between devices with their start and end apart: 44 -> 59, of which waited for: 18 -> 26; matrix products, arithmetic and copies ran while one was open for 9% -> 8% of each run, Pallas kernels for 39% -> 37%
where the time goes in v8:
time: 497 us; the launch traced here: 490 us
  Pallas kernels  181 us (36%)
  waiting for transfers between devices  153 us (31%)
  starting transfers between devices  81.9 us (16%)
  other arithmetic  25.4 us (5%)
  local copies, waits for them, and re-layouts  18.3 us (4%)
  matrix products  15.3 us (3%)
  between operations  14.4 us (3%)
    pallas_call x8, Pallas kernels, negative_product(): pl.pallas_call(functools.partial(product_kernel, count), grid_spec=pltpu....  181 us
    ppermute x8, waiting for transfers between devices, move(): return lax.ppermute(value, ('row', 'col'), pairs)  57.9 us
    ppermute x28, waiting for transfers between devices, cross(): return [lax.ppermute(piece, 'row', pairs) for piece in pieces]  55.9 us
    ppermute x8, starting transfers between devices, move(): return lax.ppermute(value, ('row', 'col'), pairs)  29.7 us
    ppermute x28, starting transfers between devices, cross(): return [lax.ppermute(piece, 'row', pairs) for piece in pieces]  19.8 us
    ppermute x12, waiting for transfers between devices, sum_over_row(): lax.ppermute(send, 'row', [(i, i ^ 2 * mask) for i in range(count)])  19.2 us
    ppermute x3, starting transfers between devices, sum_over_col(): lax.ppermute(send, 'col', [(i, (i + shift) % count) for i in range(count)])  17 us
    dot_general x4, matrix products, shards(): lax.dot_general(own_rows, after(block, *waits), (((0,), (0,)), ((), ())),...  15.3 us
  transfers between devices with their start and end apart: 59, of which 26 were waited for; matrix products, arithmetic and copies ran while one was open for 8% of the time, Pallas kernels for 37%

profile of v8, /device:TPU:0, one launch (start us, length us, event | category | flops | bytes accessed | tf_op | source)
XLA Modules:
  0.0 489.8 jit_solution(9345215150329765506)
XLA Ops:
  11.8 17.7 %collective-permute-done.refs_5_ = f32[768,256]{1,0:T(8,128)S(1)} collective-permute-done((f32[768,256]{1,0:T(8,128)S(1)}, f32[768,256]{1,0:T(8,128)S(1)}, u32[]{:S(2)}, u32[]{:S(2)}) %collective-permute-start) | collective-permute-done | bytes 786464 | tf_op jit(solution)/shard_map/ppermute | solution.py:99
  30.8 9.9 %collective-permute-done.2 = f32[768,256]{1,0:T(8,128)} collective-permute-done((f32[768,256]{1,0:T(8,128)S(1)}, f32[768,256]{1,0:T(8,128)}, u32[]{:S(2)}, u32[]{:S(2)}) %collective-permute-start.2) | collective-permute-done | bytes 786464 | tf_op jit(solution)/shard_map/ppermute | solution.py:136
  42.7 21.1 %shard_map.59.refs_8_ = f32[3072,256]{1,0:T(8,128)S(1)} custom-call(s32[4]{0:T(128)S(1)} %get-tuple-element.104.place_ref, f32[3072,6144]{1,0:T(8,128)} %refs_3_.15, f32[3072,6144]{1,0:T(8,128)} %refs_3_.15, f32[3072,6144]{1,0:T(8,128)} %refs_3_.15, f32[3072,6144]{1,0:T(8,128)} %refs_3_.15, f32[768,256]{1,0:T(8,128)S(1)} %get-tuple-element.43.refs_4_, ...), custom_call_target="tpu_custom_call" | custom-call | flops 14495514624 | bytes 47185920 | tf_op jit(solution)/shard_map/pallas_call | solution.py:58
  68.2 5.3 %collective-permute-start.10 = (f32[768,512]{1,0:T(8,128)}, f32[768,512]{1,0:T(8,128)}, u32[]{:S(2)}, u32[]{:S(2)}) collective-permute-start(f32[768,512]{1,0:T(8,128)} %get-tuple-element.80), channel_id=1, source_target_pairs={{0,2},{2,0},{5,7},{7,5},{8,10},{10,8},{13,15},{15,13},{16,18},{18,... | collective-permute-start | bytes 4718600 | tf_op jit(solution)/shard_map/ppermute | solution.py:136
  76.3 21.5 %shard_map.60 = f32[3072,256]{1,0:T(8,128)} custom-call(s32[4]{0:T(128)S(1)} %get-tuple-element.105.place_ref, f32[3072,6144]{1,0:T(8,128)} %refs_3_.15, f32[3072,6144]{1,0:T(8,128)} %refs_3_.15, f32[3072,6144]{1,0:T(8,128)} %refs_3_.15, f32[3072,6144]{1,0:T(8,128)} %refs_3_.15, f32[768,256]{1,0:T(8,128)S(1)} %collective-permute-done.3.refs_4_, ...), custom_call_target="tpu_custom_call" | custom-call | flops 14495514624 | bytes 47185920 | tf_op jit(solution)/shard_map/pallas_call | solution.py:58
  97.8 11.3 %collective-permute-done.10 = f32[768,512]{1,0:T(8,128)} collective-permute-done((f32[768,512]{1,0:T(8,128)}, f32[768,512]{1,0:T(8,128)}, u32[]{:S(2)}, u32[]{:S(2)}) %collective-permute-start.10) | collective-permute-done | bytes 1572896 | tf_op jit(solution)/shard_map/ppermute | solution.py:136
  116.7 20.2 %shard_map.61.refs_8_ = f32[3072,256]{1,0:T(8,128)S(1)} custom-call(s32[4]{0:T(128)S(1)} %get-tuple-element.104.place_ref, f32[3072,6144]{1,0:T(8,128)} %refs_3_.15, f32[3072,6144]{1,0:T(8,128)} %refs_3_.15, f32[3072,6144]{1,0:T(8,128)} %refs_3_.15, f32[3072,6144]{1,0:T(8,128)} %refs_3_.15, f32[768,256]{1,0:T(8,128)S(1)} %get-tuple-element.51.refs_4_, ...), custom_call_target="tpu_custom_call" | custom-call | flops 14495514624 | bytes 47185920 | tf_op jit(solution)/shard_map/pallas_call | solution.py:58
  136.9 33.6 %collective-permute-done.15 = f32[768,512]{1,0:T(8,128)S(1)} collective-permute-done((f32[768,512]{1,0:T(8,128)S(1)}, f32[768,512]{1,0:T(8,128)S(1)}, u32[]{:S(2)}, u32[]{:S(2)}) %collective-permute-start.15) | collective-permute-done | bytes 1572896 | tf_op jit(solution)/shard_map/ppermute | solution.py:136
  174.2 21.5 %shard_map.62 = f32[3072,256]{1,0:T(8,128)} custom-call(s32[4]{0:T(128)S(1)} %get-tuple-element.105.place_ref, f32[3072,6144]{1,0:T(8,128)} %refs_3_.15, f32[3072,6144]{1,0:T(8,128)} %refs_3_.15, f32[3072,6144]{1,0:T(8,128)} %refs_3_.15, f32[3072,6144]{1,0:T(8,128)} %refs_3_.15, f32[768,256]{1,0:T(8,128)S(1)} %collective-permute-done.12.refs_4_, ...), custom_call_target="tpu_custom_call" | custom-call | flops 14495514624 | bytes 47185920 | tf_op jit(solution)/shard_map/pallas_call | solution.py:58
  201.6 30.9 %shard_map.63.refs_8_ = f32[3072,384]{1,0:T(8,128)S(1)} custom-call(s32[4]{0:T(128)S(1)} %get-tuple-element.104.place_ref, f32[3072,6144]{1,0:T(8,128)} %refs_3_.15, f32[3072,6144]{1,0:T(8,128)} %refs_3_.15, f32[3072,6144]{1,0:T(8,128)} %refs_3_.15, f32[3072,6144]{1,0:T(8,128)} %refs_3_.15, f32[768,384]{1,0:T(8,128)S(1)} %slice.38.refs_4_, ...), custom_call_target="tpu_custom_call" | custom-call | flops 21743271936 | bytes 51904512 | tf_op jit(solution)/shard_map/pallas_call | solution.py:58
  239.3 30.5 %shard_map.64 = f32[3072,384]{1,0:T(8,128)S(1)} custom-call(s32[4]{0:T(128)S(1)} %get-tuple-element.105.place_ref, f32[3072,6144]{1,0:T(8,128)} %refs_3_.15, f32[3072,6144]{1,0:T(8,128)} %refs_3_.15, f32[3072,6144]{1,0:T(8,128)} %refs_3_.15, f32[3072,6144]{1,0:T(8,128)} %refs_3_.15, f32[768,384]{1,0:T(8,128)S(1)} %collective-permute-done.20.refs_4_, ...), custom_call_target="tpu_custom_call" | custom-call | flops 21743271936 | bytes 51904512 | tf_op jit(solution)/shard_map/pallas_call | solution.py:58
  273.6 6.1 %slice_select_fusion = (f32[768,512]{1,0:T(8,128)}, f32[768,512]{1,0:T(8,128)}, f32[768,512]{1,0:T(8,128)}, f32[768,512]{1,0:T(8,128)}) fusion(f32[768,512]{1,0:T(8,128)} %collective-permute-done.9, f32[768,1024]{1,0:T(8,128)} %param.5, pred[]{:T(512)S(6)} %eq.49, f32[768,512]{1,0:T(8,128)} %collective-permute-done.10, f32[768,512]{1,0:T(8,128)S(1)} %copy-done.14, ...), kind=kLoop, calls=%fused_computation.9 | loop fusion | flops 1966080 | bytes 14155777 | tf_op jit(solution)/shard_map/jit(_where)/select_n | solution.py:181
  279.7 13.3 %collective-permute-start.35 = (f32[768,512]{1,0:T(8,128)}, f32[768,512]{1,0:T(8,128)}, u32[]{:S(2)}, u32[]{:S(2)}) collective-permute-start(f32[768,512]{1,0:T(8,128)} %get-tuple-element.85), channel_id=1, source_target_pairs={{0,0},{2,26},{5,9},{7,19},{8,8},{10,18},{13,1},{15,27},{16,4},{18,... | collective-permute-start | bytes 4718600 | tf_op jit(solution)/shard_map/ppermute | solution.py:136
  293.0 3.7 collective-permute-start.34
  303.0 31.2 %collective-permute-done.28.refs_5_ = f32[768,128]{1,0:T(8,128)S(1)} collective-permute-done((f32[768,128]{1,0:T(8,128)S(1)}, f32[768,128]{1,0:T(8,128)S(1)}, u32[]{:S(2)}, u32[]{:S(2)}) %collective-permute-start.28) | collective-permute-done | bytes 393248 | tf_op jit(solution)/shard_map/ppermute | solution.py:99
  336.7 17.3 %shard_map.65.refs_8_ = f32[3072,128]{1,0:T(8,128)S(1)} custom-call(s32[4]{0:T(128)S(1)} %get-tuple-element.104.place_ref, f32[3072,6144]{1,0:T(8,128)} %refs_3_.15, f32[3072,6144]{1,0:T(8,128)} %refs_3_.15, f32[3072,6144]{1,0:T(8,128)} %refs_3_.15, f32[3072,6144]{1,0:T(8,128)} %refs_3_.15, f32[768,128]{1,0:T(8,128)S(1)} %slice.39.refs_4_, ...), custom_call_target="tpu_custom_call" | custom-call | flops 7247757312 | bytes 42467328 | tf_op jit(solution)/shard_map/pallas_call | solution.py:58
  358.4 18.2 %shard_map.66 = f32[3072,128]{1,0:T(8,128)} custom-call(s32[4]{0:T(128)S(1)} %get-tuple-element.105.place_ref, f32[3072,6144]{1,0:T(8,128)} %refs_3_.15, f32[3072,6144]{1,0:T(8,128)} %refs_3_.15, f32[3072,6144]{1,0:T(8,128)} %refs_3_.15, f32[3072,6144]{1,0:T(8,128)} %refs_3_.15, f32[768,128]{1,0:T(8,128)S(1)} %collective-permute-done.27.refs_4_, ...), custom_call_target="tpu_custom_call" | custom-call | flops 7247757312 | bytes 42467328 | tf_op jit(solution)/shard_map/pallas_call | solution.py:58
  376.6 3.8 fusion.3
  386.6 3.8 fusion.2
  392.4 4.0 fusion.1
  430.6 10.3 %reduce-scatter.11.cloned.1.call-done = f32[768,128]{1,0:T(8,128)} async-done(((f32[3072,128]{1,0:T(8,128)}), f32[768,128]{1,0:T(8,128)}) %reduce-scatter.11.cloned.1.call-update) | async-done | bytes 393232 | tf_op jit(solution)/shard_map/reduce_scatter | solution.py:186
  457.0 10.2 %collective-permute-start.52 = (f32[128,256]{1,0:T(8,128)S(1)}, f32[128,256]{1,0:T(8,128)S(1)}, u32[]{:S(2)}, u32[]{:S(2)}) collective-permute-start(f32[128,256]{1,0:T(8,128)S(1)} %get-tuple-element.92), channel_id=1, source_target_pairs={{0,1},{1,2},{2,3},{3,0},{4,5},{5,6},{6,7},{7,4},{8,9},{9,10},{10,1... | collective-permute-start | bytes 393224 | tf_op jit(solution)/shard_map/ppermute | solution.py:124
  467.2 6.8 %collective-permute-start.53 = (f32[128,256]{1,0:T(8,128)S(1)}, f32[128,256]{1,0:T(8,128)S(1)}, u32[]{:S(2)}, u32[]{:S(2)}) collective-permute-start(f32[128,256]{1,0:T(8,128)S(1)} %get-tuple-element.94), channel_id=1, source_target_pairs={{0,2},{1,3},{2,0},{3,1},{4,6},{5,7},{6,4},{7,5},{8,10},{9,11},{10,... | collective-permute-start | bytes 393224 | tf_op jit(solution)/shard_map/ppermute | solution.py:124
  476.1 6.2 %collective-permute-done.53 = f32[128,256]{1,0:T(8,128)S(1)} collective-permute-done((f32[128,256]{1,0:T(8,128)S(1)}, f32[128,256]{1,0:T(8,128)S(1)}, u32[]{:S(2)}, u32[]{:S(2)}) %collective-permute-start.53) | collective-permute-done | bytes 131104 | tf_op jit(solution)/shard_map/ppermute | solution.py:124
  (175 shorter events, 116.7 us)
Async XLA Ops:
  7.2 369.4 %reduce-scatter.5.cloned.1.call-start = ((), (), s32[]{:S(2)}) async-start(), calls=%async_computation.4 | async-start | bytes 3932160 | tf_op jit(solution)/shard_map/reduce_scatter | solution.py:186
  8.7 20.8 %collective-permute-start = (f32[768,256]{1,0:T(8,128)S(1)}, f32[768,256]{1,0:T(8,128)S(1)}, u32[]{:S(2)}, u32[]{:S(2)}) collective-permute-start(f32[768,256]{1,0:T(8,128)S(1)} %get-tuple-element.43.refs_4_), channel_id=1, source_target_pairs={{0,8},{4,20},{8,0},{12,28},{16,24},{20,4},{24,16},{28,12},{1,9},{5... | collective-permute-start | bytes 2359304 | tf_op jit(solution)/shard_map/ppermute | solution.py:99
  11.7 29.0 %collective-permute-start.2 = (f32[768,256]{1,0:T(8,128)S(1)}, f32[768,256]{1,0:T(8,128)}, u32[]{:S(2)}, u32[]{:S(2)}) collective-permute-start(f32[768,256]{1,0:T(8,128)S(1)} %get-tuple-element.51.refs_4_), channel_id=1, source_target_pairs={{0,8},{1,9},{2,10},{3,11},{4,12},{5,13},{6,14},{7,15},{8,0},{9,1},... | collective-permute-start | bytes 2359304 | tf_op jit(solution)/shard_map/ppermute | solution.py:136
  40.7 23.1 %collective-permute-start.3 = (f32[768,256]{1,0:T(8,128)S(1)}, f32[768,256]{1,0:T(8,128)S(1)}, u32[]{:S(2)}, u32[]{:S(2)}) collective-permute-start(f32[768,256]{1,0:T(8,128)S(1)} %get-tuple-element.43.refs_4_), channel_id=1, source_target_pairs={{0,16},{4,12},{8,24},{12,4},{16,0},{20,28},{24,8},{28,20},{1,17},{... | collective-permute-start | bytes 2359304 | tf_op jit(solution)/shard_map/ppermute | solution.py:99
  41.9 22.0 %collective-permute-start.4 = (f32[768,256]{1,0:T(8,128)S(1)}, f32[768,256]{1,0:T(8,128)S(1)}, u32[]{:S(2)}, u32[]{:S(2)}) collective-permute-start(f32[768,256]{1,0:T(8,128)S(1)} %collective-permute-done.refs_5_), channel_id=1, source_target_pairs={{0,16},{4,12},{8,24},{12,4},{16,0},{20,28},{24,8},{28,20},{1,17},{... | collective-permute-start | bytes 2359304 | tf_op jit(solution)/shard_map/ppermute | solution.py:99
  68.2 41.0 %collective-permute-start.10 = (f32[768,512]{1,0:T(8,128)}, f32[768,512]{1,0:T(8,128)}, u32[]{:S(2)}, u32[]{:S(2)}) collective-permute-start(f32[768,512]{1,0:T(8,128)} %get-tuple-element.80), channel_id=1, source_target_pairs={{0,2},{2,0},{5,7},{7,5},{8,10},{10,8},{13,15},{15,13},{16,18},{18,... | collective-permute-start | bytes 4718600 | tf_op jit(solution)/shard_map/ppermute | solution.py:136
  73.5 38.7 %collective-permute-start.9 = (f32[768,512]{1,0:T(8,128)}, f32[768,512]{1,0:T(8,128)}, u32[]{:S(2)}, u32[]{:S(2)}) collective-permute-start(f32[768,512]{1,0:T(8,128)} %get-tuple-element.82), channel_id=1, source_target_pairs={{1,0},{3,2},{4,5},{6,7},{9,8},{11,10},{12,13},{14,15},{17,16},{19,... | collective-permute-start | bytes 4718600 | tf_op jit(solution)/shard_map/ppermute | solution.py:136
  74.8 23.0 %collective-permute-start.8 = (f32[768,256]{1,0:T(8,128)S(1)}, f32[768,256]{1,0:T(8,128)S(1)}, u32[]{:S(2)}, u32[]{:S(2)}) collective-permute-start(f32[768,256]{1,0:T(8,128)S(1)} %get-tuple-element.51.refs_4_), channel_id=1, source_target_pairs={{0,8},{4,20},{8,0},{12,28},{16,24},{20,4},{24,16},{28,12},{1,9},{5... | collective-permute-start | bytes 2359304 | tf_op jit(solution)/shard_map/ppermute | solution.py:99
  112.2 274.4 %reduce-scatter.7.cloned.1.call-start = ((), (), s32[]{:S(2)}) async-start(), calls=%async_computation.5 | async-start | bytes 3932160 | tf_op jit(solution)/shard_map/reduce_scatter | solution.py:186
  112.9 57.7 %collective-permute-start.15 = (f32[768,512]{1,0:T(8,128)S(1)}, f32[768,512]{1,0:T(8,128)S(1)}, u32[]{:S(2)}, u32[]{:S(2)}) collective-permute-start(f32[768,512]{1,0:T(8,128)S(1)} %get-tuple-element.52), channel_id=1, source_target_pairs={{1,2},{3,0},{4,7},{6,5},{9,10},{11,8},{12,15},{14,13},{17,18},{19,... | collective-permute-start | bytes 4718600 | tf_op jit(solution)/shard_map/ppermute | solution.py:136
  114.6 55.9 %collective-permute-start.12 = (f32[768,256]{1,0:T(8,128)S(1)}, f32[768,256]{1,0:T(8,128)S(1)}, u32[]{:S(2)}, u32[]{:S(2)}) collective-permute-start(f32[768,256]{1,0:T(8,128)S(1)} %get-tuple-element.51.refs_4_), channel_id=1, source_target_pairs={{0,16},{4,12},{8,24},{12,4},{16,0},{20,28},{24,8},{28,20},{1,17},{... | collective-permute-start | bytes 2359304 | tf_op jit(solution)/shard_map/ppermute | solution.py:99
  115.4 21.5 %collective-permute-start.13 = (f32[768,256]{1,0:T(8,128)S(1)}, f32[768,256]{1,0:T(8,128)S(1)}, u32[]{:S(2)}, u32[]{:S(2)}) collective-permute-start(f32[768,256]{1,0:T(8,128)S(1)} %collective-permute-done.8.refs_5_), channel_id=1, source_target_pairs={{0,16},{4,12},{8,24},{12,4},{16,0},{20,28},{24,8},{28,20},{1,17},{... | collective-permute-start | bytes 2359304 | tf_op jit(solution)/shard_map/ppermute | solution.py:99
  172.4 23.3 %collective-permute-start.18 = (f32[768,384]{1,0:T(8,128)S(1)}, f32[768,384]{1,0:T(8,128)S(1)}, u32[]{:S(2)}, u32[]{:S(2)}) collective-permute-start(f32[768,384]{1,0:T(8,128)S(1)} %slice.38.refs_4_), channel_id=1, source_target_pairs={{0,8},{4,20},{8,0},{12,28},{16,24},{20,4},{24,16},{28,12},{1,9},{5... | collective-permute-start | bytes 3538952 | tf_op jit(solution)/shard_map/ppermute | solution.py:99
  196.3 196.1 %reduce-scatter.9.cloned.1.call-start = ((), (), s32[]{:S(2)}) async-start(), calls=%async_computation.6 | async-start | bytes 5898240 | tf_op jit(solution)/shard_map/reduce_scatter | solution.py:186
  199.6 35.2 %collective-permute-start.20 = (f32[768,384]{1,0:T(8,128)S(1)}, f32[768,384]{1,0:T(8,128)S(1)}, u32[]{:S(2)}, u32[]{:S(2)}) collective-permute-start(f32[768,384]{1,0:T(8,128)S(1)} %slice.38.refs_4_), channel_id=1, source_target_pairs={{0,16},{4,12},{8,24},{12,4},{16,0},{20,28},{24,8},{28,20},{1,17},{... | collective-permute-start | bytes 3538952 | tf_op jit(solution)/shard_map/ppermute | solution.py:99
  199.8 34.9 %collective-permute-start.21 = (f32[768,384]{1,0:T(8,128)S(1)}, f32[768,384]{1,0:T(8,128)S(1)}, u32[]{:S(2)}, u32[]{:S(2)}) collective-permute-start(f32[768,384]{1,0:T(8,128)S(1)} %collective-permute-done.18.refs_5_), channel_id=1, source_target_pairs={{0,16},{4,12},{8,24},{12,4},{16,0},{20,28},{24,8},{28,20},{1,17},{... | collective-permute-start | bytes 3538952 | tf_op jit(solution)/shard_map/ppermute | solution.py:99
  236.3 35.7 %collective-permute-start.25 = (f32[768,128]{1,0:T(8,128)S(1)}, f32[768,128]{1,0:T(8,128)S(1)}, u32[]{:S(2)}, u32[]{:S(2)}) collective-permute-start(f32[768,128]{1,0:T(8,128)S(1)} %slice.39.refs_4_), channel_id=1, source_target_pairs={{0,8},{4,20},{8,0},{12,28},{16,24},{20,4},{24,16},{28,12},{1,9},{5... | collective-permute-start | bytes 1179656 | tf_op jit(solution)/shard_map/ppermute | solution.py:99
  271.9 168.9 %reduce-scatter.11.cloned.1.call-start = ((), (), s32[]{:S(2)}) async-start(), calls=%async_computation.7 | async-start | bytes 1966080 | tf_op jit(solution)/shard_map/reduce_scatter | solution.py:186
  272.0 29.2 %collective-permute-start.26 = (f32[768,128]{1,0:T(8,128)S(1)}, f32[768,128]{1,0:T(8,128)S(1)}, u32[]{:S(2)}, u32[]{:S(2)}) collective-permute-start(f32[768,128]{1,0:T(8,128)S(1)} %collective-permute-done.25.refs_5_), channel_id=1, source_target_pairs={{0,4},{4,0},{8,12},{12,8},{16,20},{20,16},{24,28},{28,24},{1,5},{5... | collective-permute-start | bytes 1179656 | tf_op jit(solution)/shard_map/ppermute | solution.py:99
  279.7 74.5 %collective-permute-start.35 = (f32[768,512]{1,0:T(8,128)}, f32[768,512]{1,0:T(8,128)}, u32[]{:S(2)}, u32[]{:S(2)}) collective-permute-start(f32[768,512]{1,0:T(8,128)} %get-tuple-element.85), channel_id=1, source_target_pairs={{0,0},{2,26},{5,9},{7,19},{8,8},{10,18},{13,1},{15,27},{16,4},{18,... | collective-permute-start | bytes 4718600 | tf_op jit(solution)/shard_map/ppermute | solution.py:136
  293.0 61.7 %collective-permute-start.34 = (f32[768,512]{1,0:T(8,128)}, f32[768,512]{1,0:T(8,128)}, u32[]{:S(2)}, u32[]{:S(2)}) collective-permute-start(f32[768,512]{1,0:T(8,128)} %get-tuple-element.86), channel_id=1, source_target_pairs={{0,8},{2,2},{5,1},{7,11},{8,16},{10,26},{13,25},{15,19},{16,12},{1... | collective-permute-start | bytes 4718600 | tf_op jit(solution)/shard_map/ppermute | solution.py:136
  296.7 57.9 %collective-permute-start.33 = (f32[768,512]{1,0:T(8,128)}, f32[768,512]{1,0:T(8,128)}, u32[]{:S(2)}, u32[]{:S(2)}) collective-permute-start(f32[768,512]{1,0:T(8,128)} %get-tuple-element.87), channel_id=1, source_target_pairs={{0,16},{2,10},{5,25},{7,3},{8,24},{10,2},{13,17},{15,11},{16,20},{... | collective-permute-start | bytes 4718600 | tf_op jit(solution)/shard_map/ppermute | solution.py:136
  299.1 55.5 %collective-permute-start.32 = (f32[768,512]{1,0:T(8,128)}, f32[768,512]{1,0:T(8,128)}, u32[]{:S(2)}, u32[]{:S(2)}) collective-permute-start(f32[768,512]{1,0:T(8,128)} %get-tuple-element.88), channel_id=1, source_target_pairs={{0,24},{2,18},{5,17},{7,27},{8,0},{10,10},{13,9},{15,3},{16,28},{1... | collective-permute-start | bytes 4718600 | tf_op jit(solution)/shard_map/ppermute | solution.py:136
  303.0 31.2 %collective-permute-start.28 = (f32[768,128]{1,0:T(8,128)S(1)}, f32[768,128]{1,0:T(8,128)S(1)}, u32[]{:S(2)}, u32[]{:S(2)}) collective-permute-start(f32[768,128]{1,0:T(8,128)S(1)} %collective-permute-done.25.refs_5_), channel_id=1, source_target_pairs={{0,16},{4,12},{8,24},{12,4},{16,0},{20,28},{24,8},{28,20},{1,17},{... | collective-permute-start | bytes 1179656 | tf_op jit(solution)/shard_map/ppermute | solution.py:99
  (53 other events, 472.9 us)
Sparse Core Ops, SparseCore 0:
  112.4 79.2 reduce-scatter.4
  196.4 87.4 reduce-scatter.6
  286.2 98.1 reduce-scatter.8
  386.6 54.2 reduce-scatter.10

commit v9 on v7

--- a/solution.py
+++ b/solution.py
@@ -8,7 +8,7 @@
 from jax.experimental.pallas import tpu as pltpu
 from jax.sharding import PartitionSpec as P
 
-EIGHTHS = (3, 3, 2)
+EIGHTHS = (2, 3, 3)
 LANES = 128
 MIB = 1 << 20
 
@@ -101,15 +101,18 @@
 
 def sum_over_row(value, count):
     rows, columns = value.shape
+    chips = count // 2
     me = lax.axis_index("row")
-    value = value.reshape((2,) * (count.bit_length() - 1) + (rows // count, columns))
-    for bit in range(count.bit_length() - 1):
-        axis = value.ndim - 3
-        mine = (me >> bit) & 1
-        keep = lax.dynamic_index_in_dim(value, mine, axis, keepdims=False)
-        send = lax.dynamic_index_in_dim(value, 1 - mine, axis, keepdims=False)
-        value = keep + lax.ppermute(send, "row", [(i, i ^ (1 << bit)) for i in range(count)])
-    return value
+    core, chip = me % 2, me // 2
+    value = value.reshape(chips, 2, rows // count, columns)
+    keep = lax.dynamic_index_in_dim(value, core, 1, keepdims=False)
+    send = lax.dynamic_index_in_dim(value, 1 - core, 1, keepdims=False)
+    value = keep + lax.ppermute(send, "row", [(i, i ^ 1) for i in range(count)])
+    total = lax.dynamic_index_in_dim(value, chip, 0, keepdims=False)
+    for mask in range(1, chips):
+        send = lax.dynamic_index_in_dim(value, chip ^ mask, 0, keepdims=False)
+        total = total + lax.ppermute(send, "row", [(i, i ^ (2 * mask)) for i in range(count)])
+    return total
 
 
 def sum_over_col(value, count):
@@ -191,8 +194,8 @@
                 pieces = pieces + cross(pieces, masks, row_count)
             return pieces
 
-        mine = link(chunks[:1], orders[:-1])
         right = right_of_neighbour()
+        mine = link(all_after(chunks[:1], right), orders[:-1])
         arrived = [over_col(right, k) for k in range(1, min(3, column_count))]
         early = len(arrived)
         arrived += [over_col(right, k, *arrived) for k in range(3, column_count)]
@@ -209,7 +212,7 @@
             products.append(last)
             waits = mine[-1:] if chunk + 1 < len(chunks) else []
             blocks.append(summed(last, *waits, *([] if chunk else arrived[early:])))
-        own_rows = over_row(right, [after(value, products[0]) for value in arrived])
+        own_rows = over_row(right, [after(value, products[-1]) for value in arrived])
     else:
         right = right_of_neighbour()
         own_rows = over_row(right, [over_col(right, k) for k in range(1, column_count)])

time: 430 us -> 439 us (1.021)
  waiting for transfers between devices: 119 us -> 127 us
  starting transfers between devices: 64.9 us -> 72.6 us
    ppermute x8, waiting for transfers between devices: 39.2 us -> 62.3 us  [move(): return lax.ppermute(value, ('row', 'col'), pairs)]
    ppermute x9 -> x12, waiting for transfers between devices: 32.5 us -> 21.9 us  [the longest x9 19.6 us: sum_over_row(): lax.ppermute(send, 'row', [(i, i ^ 2 * mask) for i in range(count)])]
    ppermute x21, waiting for transfers between devices: 31.7 us -> 21.4 us  [cross(): return [lax.ppermute(piece, 'row', pairs) for piece in pieces]]
    ppermute x9 -> x12, starting transfers between devices: 8.36 us -> 13.8 us  [the longest x9 13.2 us: sum_over_row(): lax.ppermute(send, 'row', [(i, i ^ 2 * mask) for i in range(count)])]
    reduce_scatter x3, waiting for transfers between devices: 12.3 us -> 17.5 us  [summed(): lax.psum_scatter(after(partial_block, *others), 'col', scatter_dimension=...]
    unnamed x40 -> x42, local copies, waits for them, and re-layouts: 14.3 us -> 14.7 us
  transfers between devices with their start and end apart: 44 -> 47, of which waited for: 18 -> 20; matrix products, arithmetic and copies ran while one was open for 9% -> 7% of each run, Pallas kernels for 39% -> 38%
where the time goes in v9:
time: 439 us; the launch traced here: 432 us
  Pallas kernels  164 us (37%)
  waiting for transfers between devices  127 us (29%)
  starting transfers between devices  72.6 us (17%)
  local copies, waits for them, and re-layouts  22.2 us (5%)
  other arithmetic  20.2 us (5%)
  between operations  14.5 us (3%)
  matrix products  10.5 us (2%)
    pallas_call x6, Pallas kernels, negative_product(): pl.pallas_call(functools.partial(product_kernel, count), grid_spec=pltpu....  164 us
    ppermute x8, waiting for transfers between devices, move(): return lax.ppermute(value, ('row', 'col'), pairs)  62.3 us
    ppermute x8, starting transfers between devices, move(): return lax.ppermute(value, ('row', 'col'), pairs)  34.7 us
    ppermute x21, waiting for transfers between devices, cross(): return [lax.ppermute(piece, 'row', pairs) for piece in pieces]  21.4 us
    ppermute x9, waiting for transfers between devices, sum_over_row(): lax.ppermute(send, 'row', [(i, i ^ 2 * mask) for i in range(count)])  19.6 us
    ppermute x21, starting transfers between devices, cross(): return [lax.ppermute(piece, 'row', pairs) for piece in pieces]  17.7 us
    reduce_scatter x3, waiting for transfers between devices, summed(): lax.psum_scatter(after(partial_block, *others), 'col', scatter_dimension=...  17.5 us
    unnamed x42, local copies, waits for them, and re-layouts  14.7 us
  transfers between devices with their start and end apart: 47, of which 20 were waited for; matrix products, arithmetic and copies ran while one was open for 7% of the time, Pallas kernels for 38%

profile of v9, /device:TPU:0, one launch (start us, length us, event | category | flops | bytes accessed | tf_op | source)
XLA Modules:
  0.0 431.7 jit_solution(16400048989820094306)
XLA Ops:
  12.9 33.2 %collective-permute-done = f32[768,512]{1,0:T(8,128)S(1)} collective-permute-done((f32[768,512]{1,0:T(8,128)S(1)}, f32[768,512]{1,0:T(8,128)S(1)}, u32[]{:S(2)}, u32[]{:S(2)}) %collective-permute-start) | collective-permute-done | bytes 1572896 | tf_op jit(solution)/shard_map/ppermute | solution.py:136
  47.9 10.2 %collective-permute-done.1.refs_5_ = f32[768,256]{1,0:T(8,128)S(1)} collective-permute-done((f32[768,256]{1,0:T(8,128)S(1)}, f32[768,256]{1,0:T(8,128)S(1)}, u32[]{:S(2)}, u32[]{:S(2)}) %collective-permute-start.1) | collective-permute-done | bytes 786464 | tf_op jit(solution)/shard_map/ppermute | solution.py:99
  59.3 3.8 slice_select_fusion.1
  64.5 4.7 %collective-permute-start.7 = (f32[768,512]{1,0:T(8,128)S(1)}, f32[768,512]{1,0:T(8,128)S(1)}, u32[]{:S(2)}, u32[]{:S(2)}) collective-permute-start(f32[768,512]{1,0:T(8,128)S(1)} %get-tuple-element.65), channel_id=1, source_target_pairs={{0,2},{2,0},{5,7},{7,5},{8,10},{10,8},{13,15},{15,13},{16,18},{18,... | collective-permute-start | bytes 4718600 | tf_op jit(solution)/shard_map/ppermute | solution.py:136
  71.3 20.4 %shard_map.59.refs_8_ = f32[3072,256]{1,0:T(8,128)S(1)} custom-call(s32[4]{0:T(128)S(1)} %get-tuple-element.85.place_ref, f32[3072,6144]{1,0:T(8,128)} %refs_3_.11, f32[3072,6144]{1,0:T(8,128)} %refs_3_.11, f32[3072,6144]{1,0:T(8,128)} %refs_3_.11, f32[3072,6144]{1,0:T(8,128)} %refs_3_.11, f32[768,256]{1,0:T(8,128)S(1)} %slice.27.refs_4_, ...), custom_call_target="tpu_custom_call" | custom-call | flops 14495514624 | bytes 47185920 | tf_op jit(solution)/shard_map/pallas_call | solution.py:58
  91.8 8.6 %collective-permute-done.6 = f32[768,512]{1,0:T(8,128)S(1)} collective-permute-done((f32[768,512]{1,0:T(8,128)S(1)}, f32[768,512]{1,0:T(8,128)S(1)}, u32[]{:S(2)}, u32[]{:S(2)}) %collective-permute-start.6) | collective-permute-done | bytes 1572896 | tf_op jit(solution)/shard_map/ppermute | solution.py:136
  100.4 3.8 collective-permute-done.7
  109.3 21.4 %shard_map.60 = f32[3072,256]{1,0:T(8,128)} custom-call(s32[4]{0:T(128)S(1)} %get-tuple-element.86.place_ref, f32[3072,6144]{1,0:T(8,128)} %refs_3_.11, f32[3072,6144]{1,0:T(8,128)} %refs_3_.11, f32[3072,6144]{1,0:T(8,128)} %refs_3_.11, f32[3072,6144]{1,0:T(8,128)} %refs_3_.11, f32[768,256]{1,0:T(8,128)S(1)} %collective-permute-done.3.refs_4_, ...), custom_call_target="tpu_custom_call" | custom-call | flops 14495514624 | bytes 47185920 | tf_op jit(solution)/shard_map/pallas_call | solution.py:58
  139.1 31.3 %shard_map.61.refs_8_ = f32[3072,384]{1,0:T(8,128)S(1)} custom-call(s32[4]{0:T(128)S(1)} %get-tuple-element.85.place_ref, f32[3072,6144]{1,0:T(8,128)} %refs_3_.11, f32[3072,6144]{1,0:T(8,128)} %refs_3_.11, f32[3072,6144]{1,0:T(8,128)} %refs_3_.11, f32[3072,6144]{1,0:T(8,128)} %refs_3_.11, f32[768,384]{1,0:T(8,128)S(1)} %get-tuple-element.45.refs_4_, ...), custom_call_target="tpu_custom_call" | custom-call | flops 21743271936 | bytes 51904512 | tf_op jit(solution)/shard_map/pallas_call | solution.py:58
  177.0 30.5 %shard_map.62 = f32[3072,384]{1,0:T(8,128)S(1)} custom-call(s32[4]{0:T(128)S(1)} %get-tuple-element.86.place_ref, f32[3072,6144]{1,0:T(8,128)} %refs_3_.11, f32[3072,6144]{1,0:T(8,128)} %refs_3_.11, f32[3072,6144]{1,0:T(8,128)} %refs_3_.11, f32[3072,6144]{1,0:T(8,128)} %refs_3_.11, f32[768,384]{1,0:T(8,128)S(1)} %collective-permute-done.13.refs_4_, ...), custom_call_target="tpu_custom_call" | custom-call | flops 21743271936 | bytes 51904512 | tf_op jit(solution)/shard_map/pallas_call | solution.py:58
  214.9 30.1 %shard_map.63.refs_8_ = f32[3072,384]{1,0:T(8,128)S(1)} custom-call(s32[4]{0:T(128)S(1)} %get-tuple-element.85.place_ref, f32[3072,6144]{1,0:T(8,128)} %refs_3_.11, f32[3072,6144]{1,0:T(8,128)} %refs_3_.11, f32[3072,6144]{1,0:T(8,128)} %refs_3_.11, f32[3072,6144]{1,0:T(8,128)} %refs_3_.11, f32[768,384]{1,0:T(8,128)S(1)} %copy-done.4, ...), custom_call_target="tpu_custom_call" | custom-call | flops 21743271936 | bytes 51904512 | tf_op jit(solution)/shard_map/pallas_call | solution.py:58
  251.7 30.5 %shard_map.64 = f32[3072,384]{1,0:T(8,128)S(1)} custom-call(s32[4]{0:T(128)S(1)} %get-tuple-element.86.place_ref, f32[3072,6144]{1,0:T(8,128)} %refs_3_.11, f32[3072,6144]{1,0:T(8,128)} %refs_3_.11, f32[3072,6144]{1,0:T(8,128)} %refs_3_.11, f32[3072,6144]{1,0:T(8,128)} %refs_3_.11, f32[768,384]{1,0:T(8,128)S(1)} %collective-permute-done.20.refs_4_, ...), custom_call_target="tpu_custom_call" | custom-call | flops 21743271936 | bytes 51904512 | tf_op jit(solution)/shard_map/pallas_call | solution.py:58
  286.3 5.9 %slice_select_fusion = (f32[768,512]{1,0:T(8,128)}, f32[768,512]{1,0:T(8,128)}, f32[768,512]{1,0:T(8,128)}, f32[768,512]{1,0:T(8,128)}) fusion(f32[768,512]{1,0:T(8,128)} %copy-done.18, f32[768,1024]{1,0:T(8,128)S(1)} %copy-done.6, pred[]{:T(512)S(6)} %eq.43, f32[768,512]{1,0:T(8,128)} %copy-done.19, f32[768,512]{1,0:T(8,128)} %collective-permute-done.11, ...), kind=kLoop, calls=%fused_computation.7 | loop fusion | flops 1572864 | bytes 14155777 | tf_op jit(solution)/shard_map/jit(_where)/select_n | solution.py:181
  298.2 5.0 %collective-permute-start.27 = (f32[768,512]{1,0:T(8,128)}, f32[768,512]{1,0:T(8,128)}, u32[]{:S(2)}, u32[]{:S(2)}) collective-permute-start(f32[768,512]{1,0:T(8,128)} %get-tuple-element.70), channel_id=1, source_target_pairs={{0,8},{2,2},{5,1},{7,11},{8,16},{10,26},{13,25},{15,19},{16,12},{1... | collective-permute-start | bytes 4718600 | tf_op jit(solution)/shard_map/ppermute | solution.py:136
  303.1 13.4 %collective-permute-start.28 = (f32[768,512]{1,0:T(8,128)}, f32[768,512]{1,0:T(8,128)}, u32[]{:S(2)}, u32[]{:S(2)}) collective-permute-start(f32[768,512]{1,0:T(8,128)} %get-tuple-element.69), channel_id=1, source_target_pairs={{0,0},{2,26},{5,9},{7,19},{8,8},{10,18},{13,1},{15,27},{16,4},{18,... | collective-permute-start | bytes 4718600 | tf_op jit(solution)/shard_map/ppermute | solution.py:136
  316.6 16.6 %collective-permute-done.26 = f32[768,512]{1,0:T(8,128)S(1)} collective-permute-done((f32[768,512]{1,0:T(8,128)}, f32[768,512]{1,0:T(8,128)S(1)}, u32[]{:S(2)}, u32[]{:S(2)}) %collective-permute-start.26) | collective-permute-done | bytes 1572896 | tf_op jit(solution)/shard_map/ppermute | solution.py:136
  342.4 3.9 fusion.1
  350.4 4.6 %collective-permute-start.30 = (f32[128,256]{1,0:T(8,128)S(1)}, f32[128,256]{1,0:T(8,128)S(1)}, u32[]{:S(2)}, u32[]{:S(2)}) collective-permute-start(f32[128,256]{1,0:T(8,128)S(1)} %get-tuple-element.82), channel_id=1, source_target_pairs={{0,8},{4,12},{8,0},{12,4},{16,24},{20,28},{24,16},{28,20},{1,9},{5... | collective-permute-start | bytes 393224 | tf_op jit(solution)/shard_map/ppermute | solution.py:114
  367.2 4.8 %collective-permute-done.35 = f32[128,384]{1,0:T(8,128)S(1)} collective-permute-done((f32[128,384]{1,0:T(8,128)S(1)}, f32[128,384]{1,0:T(8,128)S(1)}, u32[]{:S(2)}, u32[]{:S(2)}) %collective-permute-start.35) | collective-permute-done | bytes 196640 | tf_op jit(solution)/shard_map/ppermute | solution.py:114
  372.0 17.5 %reduce-scatter.8.cloned.1.call-done = f32[768,384]{1,0:T(8,128)} async-done(((f32[3072,384]{1,0:T(8,128)}), f32[768,384]{1,0:T(8,128)}) %reduce-scatter.8.cloned.1.call-update) | async-done | bytes 1179664 | tf_op jit(solution)/shard_map/reduce_scatter | solution.py:186
  389.5 3.9 fusion
  401.2 4.6 %collective-permute-done.38 = f32[128,384]{1,0:T(8,128)} collective-permute-done((f32[128,384]{1,0:T(8,128)}, f32[128,384]{1,0:T(8,128)}, u32[]{:S(2)}, u32[]{:S(2)}) %collective-permute-start.38) | collective-permute-done | bytes 196640 | tf_op jit(solution)/shard_map/ppermute | solution.py:114
  405.7 4.6 %collective-permute-done.39 = f32[128,384]{1,0:T(8,128)} collective-permute-done((f32[128,384]{1,0:T(8,128)}, f32[128,384]{1,0:T(8,128)}, u32[]{:S(2)}, u32[]{:S(2)}) %collective-permute-start.39) | collective-permute-done | bytes 196640 | tf_op jit(solution)/shard_map/ppermute | solution.py:114
  420.0 4.0 collective-permute-done.42
  (148 shorter events, 99.7 us)
Async XLA Ops:
  7.2 309.4 %reduce-scatter.4.cloned.1.call-start = ((), (), s32[]{:S(2)}) async-start(), calls=%async_computation.3 | async-start | bytes 3932160 | tf_op jit(solution)/shard_map/reduce_scatter | solution.py:186
  8.7 37.4 %collective-permute-start = (f32[768,512]{1,0:T(8,128)S(1)}, f32[768,512]{1,0:T(8,128)S(1)}, u32[]{:S(2)}, u32[]{:S(2)}) collective-permute-start(f32[768,512]{1,0:T(8,128)S(1)} %split.6), channel_id=1, source_target_pairs={{0,8},{1,9},{2,10},{3,11},{4,12},{5,13},{6,14},{7,15},{8,0},{9,1},... | collective-permute-start | bytes 4718600 | tf_op jit(solution)/shard_map/ppermute | solution.py:136
  46.1 12.0 %collective-permute-start.1 = (f32[768,256]{1,0:T(8,128)S(1)}, f32[768,256]{1,0:T(8,128)S(1)}, u32[]{:S(2)}, u32[]{:S(2)}) collective-permute-start(f32[768,256]{1,0:T(8,128)S(1)} %slice.27.refs_4_), channel_id=1, source_target_pairs={{0,8},{4,20},{8,0},{12,28},{16,24},{20,4},{24,16},{28,12},{1,9},{5... | collective-permute-start | bytes 2359304 | tf_op jit(solution)/shard_map/ppermute | solution.py:99
  58.1 13.2 %collective-permute-start.5 = (f32[768,256]{1,0:T(8,128)S(1)}, f32[768,256]{1,0:T(8,128)S(1)}, u32[]{:S(2)}, u32[]{:S(2)}) collective-permute-start(f32[768,256]{1,0:T(8,128)S(1)} %slice.27.refs_4_), channel_id=1, source_target_pairs={{0,4},{4,0},{8,12},{12,8},{16,20},{20,16},{24,28},{28,24},{1,5},{5... | collective-permute-start | bytes 2359304 | tf_op jit(solution)/shard_map/ppermute | solution.py:99
  63.2 37.2 %collective-permute-start.6 = (f32[768,512]{1,0:T(8,128)S(1)}, f32[768,512]{1,0:T(8,128)S(1)}, u32[]{:S(2)}, u32[]{:S(2)}) collective-permute-start(f32[768,512]{1,0:T(8,128)S(1)} %get-tuple-element.66), channel_id=1, source_target_pairs={{1,0},{3,2},{4,5},{6,7},{9,8},{11,10},{12,13},{14,15},{17,16},{19,... | collective-permute-start | bytes 4718600 | tf_op jit(solution)/shard_map/ppermute | solution.py:136
  64.5 39.8 %collective-permute-start.7 = (f32[768,512]{1,0:T(8,128)S(1)}, f32[768,512]{1,0:T(8,128)S(1)}, u32[]{:S(2)}, u32[]{:S(2)}) collective-permute-start(f32[768,512]{1,0:T(8,128)S(1)} %get-tuple-element.65), channel_id=1, source_target_pairs={{0,2},{2,0},{5,7},{7,5},{8,10},{10,8},{13,15},{15,13},{16,18},{18,... | collective-permute-start | bytes 4718600 | tf_op jit(solution)/shard_map/ppermute | solution.py:136
  69.3 34.9 %collective-permute-start.4 = (f32[768,256]{1,0:T(8,128)S(1)}, f32[768,256]{1,0:T(8,128)S(1)}, u32[]{:S(2)}, u32[]{:S(2)}) collective-permute-start(f32[768,256]{1,0:T(8,128)S(1)} %collective-permute-done.1.refs_5_), channel_id=1, source_target_pairs={{0,16},{4,12},{8,24},{12,4},{16,0},{20,28},{24,8},{28,20},{1,17},{... | collective-permute-start | bytes 2359304 | tf_op jit(solution)/shard_map/ppermute | solution.py:99
  70.8 33.4 %collective-permute-start.3 = (f32[768,256]{1,0:T(8,128)S(1)}, f32[768,256]{1,0:T(8,128)S(1)}, u32[]{:S(2)}, u32[]{:S(2)}) collective-permute-start(f32[768,256]{1,0:T(8,128)S(1)} %slice.27.refs_4_), channel_id=1, source_target_pairs={{0,16},{4,12},{8,24},{12,4},{16,0},{20,28},{24,8},{28,20},{1,17},{... | collective-permute-start | bytes 2359304 | tf_op jit(solution)/shard_map/ppermute | solution.py:99
  104.7 29.8 %collective-permute-start.11 = (f32[768,512]{1,0:T(8,128)}, f32[768,512]{1,0:T(8,128)}, u32[]{:S(2)}, u32[]{:S(2)}) collective-permute-start(f32[768,512]{1,0:T(8,128)} %get-tuple-element.40), channel_id=1, source_target_pairs={{1,2},{3,0},{4,7},{6,5},{9,10},{11,8},{12,15},{14,13},{17,18},{19,... | collective-permute-start | bytes 4718600 | tf_op jit(solution)/shard_map/ppermute | solution.py:136
  107.3 23.5 %collective-permute-start.10 = (f32[768,384]{1,0:T(8,128)S(1)}, f32[768,384]{1,0:T(8,128)S(1)}, u32[]{:S(2)}, u32[]{:S(2)}) collective-permute-start(f32[768,384]{1,0:T(8,128)S(1)} %get-tuple-element.45.refs_4_), channel_id=1, source_target_pairs={{0,8},{4,20},{8,0},{12,28},{16,24},{20,4},{24,16},{28,12},{1,9},{5... | collective-permute-start | bytes 3538952 | tf_op jit(solution)/shard_map/ppermute | solution.py:99
  134.5 207.9 %reduce-scatter.6.cloned.1.call-start = ((), (), s32[]{:S(2)}) async-start(), calls=%async_computation.4 | async-start | bytes 5898240 | tf_op jit(solution)/shard_map/reduce_scatter | solution.py:186
  137.0 35.5 %collective-permute-start.14 = (f32[768,384]{1,0:T(8,128)S(1)}, f32[768,384]{1,0:T(8,128)S(1)}, u32[]{:S(2)}, u32[]{:S(2)}) collective-permute-start(f32[768,384]{1,0:T(8,128)S(1)} %collective-permute-done.10.refs_5_), channel_id=1, source_target_pairs={{0,16},{4,12},{8,24},{12,4},{16,0},{20,28},{24,8},{28,20},{1,17},{... | collective-permute-start | bytes 3538952 | tf_op jit(solution)/shard_map/ppermute | solution.py:99
  137.5 35.0 %collective-permute-start.13 = (f32[768,384]{1,0:T(8,128)S(1)}, f32[768,384]{1,0:T(8,128)S(1)}, u32[]{:S(2)}, u32[]{:S(2)}) collective-permute-start(f32[768,384]{1,0:T(8,128)S(1)} %get-tuple-element.45.refs_4_), channel_id=1, source_target_pairs={{0,16},{4,12},{8,24},{12,4},{16,0},{20,28},{24,8},{28,20},{1,17},{... | collective-permute-start | bytes 3538952 | tf_op jit(solution)/shard_map/ppermute | solution.py:99
  173.0 36.7 %collective-permute-start.18 = (f32[768,384]{1,0:T(8,128)S(1)}, f32[768,384]{1,0:T(8,128)S(1)}, u32[]{:S(2)}, u32[]{:S(2)}) collective-permute-start(f32[768,384]{1,0:T(8,128)S(1)} %copy-done.4), channel_id=1, source_target_pairs={{0,8},{4,20},{8,0},{12,28},{16,24},{20,4},{24,16},{28,12},{1,9},{5... | collective-permute-start | bytes 3538952 | tf_op jit(solution)/shard_map/ppermute | solution.py:99
  209.7 179.8 %reduce-scatter.8.cloned.1.call-start = ((), (), s32[]{:S(2)}) async-start(), calls=%async_computation.5 | async-start | bytes 5898240 | tf_op jit(solution)/shard_map/reduce_scatter | solution.py:186
  212.9 34.3 %collective-permute-start.21 = (f32[768,384]{1,0:T(8,128)S(1)}, f32[768,384]{1,0:T(8,128)S(1)}, u32[]{:S(2)}, u32[]{:S(2)}) collective-permute-start(f32[768,384]{1,0:T(8,128)S(1)} %collective-permute-done.18.refs_5_), channel_id=1, source_target_pairs={{0,16},{4,12},{8,24},{12,4},{16,0},{20,28},{24,8},{28,20},{1,17},{... | collective-permute-start | bytes 3538952 | tf_op jit(solution)/shard_map/ppermute | solution.py:99
  213.3 33.9 %collective-permute-start.20 = (f32[768,384]{1,0:T(8,128)S(1)}, f32[768,384]{1,0:T(8,128)S(1)}, u32[]{:S(2)}, u32[]{:S(2)}) collective-permute-start(f32[768,384]{1,0:T(8,128)S(1)} %copy-done.4), channel_id=1, source_target_pairs={{0,16},{4,12},{8,24},{12,4},{16,0},{20,28},{24,8},{28,20},{1,17},{... | collective-permute-start | bytes 3538952 | tf_op jit(solution)/shard_map/ppermute | solution.py:99
  292.1 24.4 %collective-permute-start.25 = (f32[768,512]{1,0:T(8,128)}, f32[768,512]{1,0:T(8,128)S(1)}, u32[]{:S(2)}, u32[]{:S(2)}) collective-permute-start(f32[768,512]{1,0:T(8,128)} %get-tuple-element.72), channel_id=1, source_target_pairs={{0,24},{2,18},{5,17},{7,27},{8,0},{10,10},{13,9},{15,3},{16,28},{1... | collective-permute-start | bytes 4718600 | tf_op jit(solution)/shard_map/ppermute | solution.py:136
  295.8 37.4 %collective-permute-start.26 = (f32[768,512]{1,0:T(8,128)}, f32[768,512]{1,0:T(8,128)S(1)}, u32[]{:S(2)}, u32[]{:S(2)}) collective-permute-start(f32[768,512]{1,0:T(8,128)} %get-tuple-element.71), channel_id=1, source_target_pairs={{0,16},{2,10},{5,25},{7,3},{8,24},{10,2},{13,17},{15,11},{16,20},{... | collective-permute-start | bytes 4718600 | tf_op jit(solution)/shard_map/ppermute | solution.py:136
  298.2 35.0 %collective-permute-start.27 = (f32[768,512]{1,0:T(8,128)}, f32[768,512]{1,0:T(8,128)}, u32[]{:S(2)}, u32[]{:S(2)}) collective-permute-start(f32[768,512]{1,0:T(8,128)} %get-tuple-element.70), channel_id=1, source_target_pairs={{0,8},{2,2},{5,1},{7,11},{8,16},{10,26},{13,25},{15,19},{16,12},{1... | collective-permute-start | bytes 4718600 | tf_op jit(solution)/shard_map/ppermute | solution.py:136
  303.1 31.2 %collective-permute-start.28 = (f32[768,512]{1,0:T(8,128)}, f32[768,512]{1,0:T(8,128)}, u32[]{:S(2)}, u32[]{:S(2)}) collective-permute-start(f32[768,512]{1,0:T(8,128)} %get-tuple-element.69), channel_id=1, source_target_pairs={{0,0},{2,26},{5,9},{7,19},{8,8},{10,18},{13,1},{15,27},{16,4},{18,... | collective-permute-start | bytes 4718600 | tf_op jit(solution)/shard_map/ppermute | solution.py:136
  359.9 12.0 %collective-permute-start.35 = (f32[128,384]{1,0:T(8,128)S(1)}, f32[128,384]{1,0:T(8,128)S(1)}, u32[]{:S(2)}, u32[]{:S(2)}) collective-permute-start(f32[128,384]{1,0:T(8,128)S(1)} %get-tuple-element.78), channel_id=1, source_target_pairs={{0,16},{4,20},{8,24},{12,28},{16,0},{20,4},{24,8},{28,12},{1,17},{... | collective-permute-start | bytes 589832 | tf_op jit(solution)/shard_map/ppermute | solution.py:114
  359.9 12.0 %collective-permute-start.36 = (f32[128,384]{1,0:T(8,128)S(1)}, f32[128,384]{1,0:T(8,128)S(1)}, u32[]{:S(2)}, u32[]{:S(2)}) collective-permute-start(f32[128,384]{1,0:T(8,128)S(1)} %get-tuple-element.77), channel_id=1, source_target_pairs={{0,24},{4,28},{8,16},{12,20},{16,8},{20,12},{24,0},{28,4},{1,25},{... | collective-permute-start | bytes 589832 | tf_op jit(solution)/shard_map/ppermute | solution.py:114
  399.2 11.2 %collective-permute-start.39 = (f32[128,384]{1,0:T(8,128)}, f32[128,384]{1,0:T(8,128)}, u32[]{:S(2)}, u32[]{:S(2)}) collective-permute-start(f32[128,384]{1,0:T(8,128)} %get-tuple-element.75), channel_id=1, source_target_pairs={{0,16},{4,20},{8,24},{12,28},{16,0},{20,4},{24,8},{28,12},{1,17},{... | collective-permute-start | bytes 589832 | tf_op jit(solution)/shard_map/ppermute | solution.py:114
  (44 other events, 379.3 us)
Sparse Core Ops, SparseCore 0:
  134.6 68.3 reduce-scatter.3
  209.8 91.5 reduce-scatter.5
  303.7 85.7 reduce-scatter.7

commit v10 on v9

--- a/solution.py
+++ b/solution.py
@@ -8,7 +8,7 @@
 from jax.experimental.pallas import tpu as pltpu
 from jax.sharding import PartitionSpec as P
 
-EIGHTHS = (2, 3, 3)
+EIGHTHS = (3, 3, 2)
 LANES = 128
 MIB = 1 << 20
 
@@ -76,12 +76,12 @@
 
 def gather_orders(count):
     masks = [1 << b for b in range(1, count.bit_length() - 1)]
-    return list(zip(masks, masks[::-1]))
-
-
-def gather_places(count):
+    return list(zip(masks[::-1], masks[::-1])), list(zip(masks, masks[::-1]))
+
+
+def gather_places(count, orders):
     held = [[i] for i in range(count)]
-    for masks in gather_orders(count):
+    for masks in orders:
         held = [held[i] + held[i ^ masks[i & 1]] for i in range(count)]
     half = count // 4
     both = [
@@ -141,8 +141,8 @@
     row_index, column_index = lax.axis_index("row"), lax.axis_index("col")
     group = row_count // column_count
     stepwise = panel.shape[0] % LANES == 0
-    orders = gather_orders(row_count)
-    place = jnp.asarray(gather_places(row_count))[row_index]
+    first_orders, later_orders = gather_orders(row_count)
+    places = [jnp.asarray(gather_places(row_count, orders))[row_index] for orders in (first_orders, later_orders)]
     unit = panel.shape[1] // 8
     chunks, first = [], 0
     for size in EIGHTHS:
@@ -194,25 +194,26 @@
                 pieces = pieces + cross(pieces, masks, row_count)
             return pieces
 
+        mine = link(chunks[:1], first_orders[:-1])
         right = right_of_neighbour()
-        mine = link(all_after(chunks[:1], right), orders[:-1])
         arrived = [over_col(right, k) for k in range(1, min(3, column_count))]
         early = len(arrived)
         arrived += [over_col(right, k, *arrived) for k in range(3, column_count)]
         last = None
         for chunk in range(len(chunks)):
+            place, orders = (places[1], later_orders) if chunk else (places[0], first_orders)
             theirs = partner(all_after(mine, mine[-1]) if last is None else all_after(mine, last))
             late = cross(all_after(mine, theirs[-1]), orders[-1], row_count)
             last = negative_product(parent_inverse, mine + theirs, place[:half])
             waits = [last] if chunk else [last] + arrived[:early]
             late = late + partner(all_after(late, *waits))
             if chunk + 1 < len(chunks):
-                mine = link(all_after([chunks[chunk + 1]], last), orders[:-1])
+                mine = link(all_after([chunks[chunk + 1]], last), later_orders[:-1])
             last = negative_product(parent_inverse, late, place[half:], last)
             products.append(last)
             waits = mine[-1:] if chunk + 1 < len(chunks) else []
             blocks.append(summed(last, *waits, *([] if chunk else arrived[early:])))
-        own_rows = over_row(right, [after(value, products[-1]) for value in arrived])
+        own_rows = over_row(right, [after(value, products[0]) for value in arrived])
     else:
         right = right_of_neighbour()
         own_rows = over_row(right, [over_col(right, k) for k in range(1, column_count)])

time: 439 us -> 431 us (0.982)
  waiting for transfers between devices: 127 us -> 119 us
    ppermute x8, waiting for transfers between devices: 62.3 us -> 27.3 us  [move(): return lax.ppermute(value, ('row', 'col'), pairs)]
    ppermute x21, waiting for transfers between devices: 21.4 us -> 45.8 us  [cross(): return [lax.ppermute(piece, 'row', pairs) for piece in pieces]]
    unnamed x42 -> x38, local copies, waits for them, and re-layouts: 14.7 us -> 14.9 us
  transfers between devices with their start and end apart: 47 -> 47, of which waited for: 20 -> 19; matrix products, arithmetic and copies ran while one was open for 7% -> 7% of each run, Pallas kernels for 38% -> 39%
where the time goes in v10:
time: 431 us; the launch traced here: 424 us
  Pallas kernels  165 us (38%)
  waiting for transfers between devices  119 us (28%)
  starting transfers between devices  70.8 us (16%)
  local copies, waits for them, and re-layouts  23.6 us (5%)
  other arithmetic  19.9 us (5%)
  between operations  14.6 us (3%)
  matrix products  11.6 us (3%)
    pallas_call x6, Pallas kernels, negative_product(): pl.pallas_call(functools.partial(product_kernel, count), grid_spec=pltpu....  165 us
    ppermute x21, waiting for transfers between devices, cross(): return [lax.ppermute(piece, 'row', pairs) for piece in pieces]  45.8 us
    ppermute x8, starting transfers between devices, move(): return lax.ppermute(value, ('row', 'col'), pairs)  33.3 us
    ppermute x8, waiting for transfers between devices, move(): return lax.ppermute(value, ('row', 'col'), pairs)  27.3 us
    reduce_scatter x3, waiting for transfers between devices, summed(): lax.psum_scatter(after(partial_block, *others), 'col', scatter_dimension=...  20.3 us
    ppermute x9, waiting for transfers between devices, sum_over_row(): lax.ppermute(send, 'row', [(i, i ^ 2 * mask) for i in range(count)])  19.3 us
    ppermute x21, starting transfers between devices, cross(): return [lax.ppermute(piece, 'row', pairs) for piece in pieces]  18.9 us
    unnamed x38, local copies, waits for them, and re-layouts  14.9 us
  transfers between devices with their start and end apart: 47, of which 19 were waited for; matrix products, arithmetic and copies ran while one was open for 7% of the time, Pallas kernels for 39%

profile of v10, /device:TPU:0, one launch (start us, length us, event | category | flops | bytes accessed | tf_op | source)
XLA Modules:
  0.0 424.3 jit_solution(10906019606651257384)
XLA Ops:
  15.0 23.2 %collective-permute-done.refs_5_ = f32[768,384]{1,0:T(8,128)S(1)} collective-permute-done((f32[768,384]{1,0:T(8,128)S(1)}, f32[768,384]{1,0:T(8,128)S(1)}, u32[]{:S(2)}, u32[]{:S(2)}) %collective-permute-start) | collective-permute-done | bytes 1179680 | tf_op jit(solution)/shard_map/ppermute | solution.py:99
  40.0 9.7 %collective-permute-done.5 = f32[768,512]{1,0:T(8,128)} collective-permute-done((f32[768,512]{1,0:T(8,128)}, f32[768,512]{1,0:T(8,128)}, u32[]{:S(2)}, u32[]{:S(2)}) %collective-permute-start.5) | collective-permute-done | bytes 1572896 | tf_op jit(solution)/shard_map/ppermute | solution.py:136
  54.4 4.5 %collective-permute-start.7 = (f32[768,512]{1,0:T(8,128)S(1)}, f32[768,512]{1,0:T(8,128)S(1)}, u32[]{:S(2)}, u32[]{:S(2)}) collective-permute-start(f32[768,512]{1,0:T(8,128)S(1)} %get-tuple-element.63), channel_id=1, source_target_pairs={{0,2},{2,0},{5,7},{7,5},{8,10},{10,8},{13,15},{15,13},{16,18},{18,... | collective-permute-start | bytes 4718600 | tf_op jit(solution)/shard_map/ppermute | solution.py:136
  61.0 31.3 %shard_map.68.refs_8_ = f32[3072,384]{1,0:T(8,128)S(1)} custom-call(s32[4]{0:T(128)S(1)} %get-tuple-element.84.place_ref, f32[3072,6144]{1,0:T(8,128)} %refs_3_.11, f32[3072,6144]{1,0:T(8,128)} %refs_3_.11, f32[3072,6144]{1,0:T(8,128)} %refs_3_.11, f32[3072,6144]{1,0:T(8,128)} %refs_3_.11, f32[768,384]{1,0:T(8,128)S(1)} %get-tuple-element.34.refs_4_, ...), custom_call_target="tpu_custom_call" | custom-call | flops 21743271936 | bytes 51904512 | tf_op jit(solution)/shard_map/pallas_call | solution.py:58
  94.5 14.5 %collective-permute-done.2.refs_4_ = f32[768,384]{1,0:T(8,128)S(1)} collective-permute-done((f32[768,384]{1,0:T(8,128)S(1)}, f32[768,384]{1,0:T(8,128)S(1)}, u32[]{:S(2)}, u32[]{:S(2)}) %collective-permute-start.2) | collective-permute-done | bytes 1179680 | tf_op jit(solution)/shard_map/ppermute | solution.py:99
  112.4 30.4 %shard_map.69 = f32[3072,384]{1,0:T(8,128)S(1)} custom-call(s32[4]{0:T(128)S(1)} %get-tuple-element.83.place_ref, f32[3072,6144]{1,0:T(8,128)} %refs_3_.11, f32[3072,6144]{1,0:T(8,128)} %refs_3_.11, f32[3072,6144]{1,0:T(8,128)} %refs_3_.11, f32[3072,6144]{1,0:T(8,128)} %refs_3_.11, f32[768,384]{1,0:T(8,128)S(1)} %collective-permute-done.2.refs_4_, ...), custom_call_target="tpu_custom_call" | custom-call | flops 21743271936 | bytes 51904512 | tf_op jit(solution)/shard_map/pallas_call | solution.py:58
  145.2 4.3 %collective-permute-start.12 = (f32[768,384]{1,0:T(8,128)S(1)}, f32[768,384]{1,0:T(8,128)S(1)}, u32[]{:S(2)}, u32[]{:S(2)}) collective-permute-start(f32[768,384]{1,0:T(8,128)S(1)} %collective-permute-done.10.refs_5_), channel_id=1, source_target_pairs={{0,4},{4,0},{8,12},{12,8},{16,20},{20,16},{24,28},{28,24},{1,5},{5... | collective-permute-start | bytes 3538952 | tf_op jit(solution)/shard_map/ppermute | solution.py:99
  154.0 30.8 %shard_map.70.refs_8_ = f32[3072,384]{1,0:T(8,128)S(1)} custom-call(s32[4]{0:T(128)S(1)} %get-tuple-element.85.place_ref, f32[3072,6144]{1,0:T(8,128)} %refs_3_.11, f32[3072,6144]{1,0:T(8,128)} %refs_3_.11, f32[3072,6144]{1,0:T(8,128)} %refs_3_.11, f32[3072,6144]{1,0:T(8,128)} %refs_3_.11, f32[768,384]{1,0:T(8,128)S(1)} %get-tuple-element.43.refs_4_, ...), custom_call_target="tpu_custom_call" | custom-call | flops 21743271936 | bytes 51904512 | tf_op jit(solution)/shard_map/pallas_call | solution.py:58
  191.5 30.5 %shard_map.71 = f32[3072,384]{1,0:T(8,128)S(1)} custom-call(s32[4]{0:T(128)S(1)} %get-tuple-element.86.place_ref, f32[3072,6144]{1,0:T(8,128)} %refs_3_.11, f32[3072,6144]{1,0:T(8,128)} %refs_3_.11, f32[3072,6144]{1,0:T(8,128)} %refs_3_.11, f32[3072,6144]{1,0:T(8,128)} %refs_3_.11, f32[768,384]{1,0:T(8,128)S(1)} %collective-permute-done.13.refs_4_, ...), custom_call_target="tpu_custom_call" | custom-call | flops 21743271936 | bytes 51904512 | tf_op jit(solution)/shard_map/pallas_call | solution.py:58
  228.8 20.6 %shard_map.72.refs_8_ = f32[3072,256]{1,0:T(8,128)S(1)} custom-call(s32[4]{0:T(128)S(1)} %get-tuple-element.85.place_ref, f32[3072,6144]{1,0:T(8,128)} %refs_3_.11, f32[3072,6144]{1,0:T(8,128)} %refs_3_.11, f32[3072,6144]{1,0:T(8,128)} %refs_3_.11, f32[3072,6144]{1,0:T(8,128)} %refs_3_.11, f32[768,256]{1,0:T(8,128)S(1)} %slice.45.refs_4_, ...), custom_call_target="tpu_custom_call" | custom-call | flops 14495514624 | bytes 47185920 | tf_op jit(solution)/shard_map/pallas_call | solution.py:58
  252.9 21.4 %shard_map.73 = f32[3072,256]{1,0:T(8,128)} custom-call(s32[4]{0:T(128)S(1)} %get-tuple-element.86.place_ref, f32[3072,6144]{1,0:T(8,128)} %refs_3_.11, f32[3072,6144]{1,0:T(8,128)} %refs_3_.11, f32[3072,6144]{1,0:T(8,128)} %refs_3_.11, f32[3072,6144]{1,0:T(8,128)} %refs_3_.11, f32[768,256]{1,0:T(8,128)S(1)} %collective-permute-done.20.refs_4_, ...), custom_call_target="tpu_custom_call" | custom-call | flops 14495514624 | bytes 47185920 | tf_op jit(solution)/shard_map/pallas_call | solution.py:58
  276.2 5.9 %slice_select_fusion = (f32[768,512]{1,0:T(8,128)}, f32[768,512]{1,0:T(8,128)}, f32[768,512]{1,0:T(8,128)}, f32[768,512]{1,0:T(8,128)}) fusion(f32[768,512]{1,0:T(8,128)} %copy-done.15, f32[768,1024]{1,0:T(8,128)S(1)} %copy-done.5, pred[]{:T(512)S(6)} %eq.43, f32[768,512]{1,0:T(8,128)} %copy-done.16, f32[768,512]{1,0:T(8,128)} %collective-permute-done.11, ...), kind=kLoop, calls=%fused_computation.7 | loop fusion | flops 1572864 | bytes 14155777 | tf_op jit(solution)/shard_map/jit(_where)/select_n | solution.py:181
  282.1 4.5 %collective-permute-start.25 = (f32[768,512]{1,0:T(8,128)}, f32[768,512]{1,0:T(8,128)S(1)}, u32[]{:S(2)}, u32[]{:S(2)}) collective-permute-start(f32[768,512]{1,0:T(8,128)} %get-tuple-element.70), channel_id=1, source_target_pairs={{0,24},{2,18},{5,17},{7,27},{8,0},{10,10},{13,9},{15,3},{16,28},{1... | collective-permute-start | bytes 4718600 | tf_op jit(solution)/shard_map/ppermute | solution.py:136
  289.0 3.7 collective-permute-start.27
  292.8 13.6 %collective-permute-start.28 = (f32[768,512]{1,0:T(8,128)}, f32[768,512]{1,0:T(8,128)}, u32[]{:S(2)}, u32[]{:S(2)}) collective-permute-start(f32[768,512]{1,0:T(8,128)} %get-tuple-element.67), channel_id=1, source_target_pairs={{0,0},{2,26},{5,9},{7,19},{8,8},{10,18},{13,1},{15,27},{16,4},{18,... | collective-permute-start | bytes 4718600 | tf_op jit(solution)/shard_map/ppermute | solution.py:136
  306.4 17.6 %collective-permute-done.26 = f32[768,512]{1,0:T(8,128)S(1)} collective-permute-done((f32[768,512]{1,0:T(8,128)}, f32[768,512]{1,0:T(8,128)S(1)}, u32[]{:S(2)}, u32[]{:S(2)}) %collective-permute-start.26) | collective-permute-done | bytes 1572896 | tf_op jit(solution)/shard_map/ppermute | solution.py:136
  325.2 3.6 select_select_fusion.1
  328.8 3.9 fusion.2
  334.9 3.9 fusion.1
  353.7 4.6 %collective-permute-done.31 = f32[128,384]{1,0:T(8,128)S(1)} collective-permute-done((f32[128,384]{1,0:T(8,128)S(1)}, f32[128,384]{1,0:T(8,128)S(1)}, u32[]{:S(2)}, u32[]{:S(2)}) %collective-permute-start.31) | collective-permute-done | bytes 196640 | tf_op jit(solution)/shard_map/ppermute | solution.py:114
  360.5 5.4 %collective-permute-done.35 = f32[128,384]{1,0:T(8,128)S(1)} collective-permute-done((f32[128,384]{1,0:T(8,128)S(1)}, f32[128,384]{1,0:T(8,128)S(1)}, u32[]{:S(2)}, u32[]{:S(2)}) %collective-permute-start.35) | collective-permute-done | bytes 196640 | tf_op jit(solution)/shard_map/ppermute | solution.py:114
  366.0 20.3 %reduce-scatter.8.cloned.1.call-done = f32[768,256]{1,0:T(8,128)} async-done(((f32[3072,256]{1,0:T(8,128)}), f32[768,256]{1,0:T(8,128)}) %reduce-scatter.8.cloned.1.call-update) | async-done | bytes 786448 | tf_op jit(solution)/shard_map/reduce_scatter | solution.py:186
  386.2 3.8 fusion
  399.9 3.6 collective-permute-done.39
  (145 shorter events, 94.2 us)
Async XLA Ops:
  7.2 321.7 %reduce-scatter.4.cloned.1.call-start = ((), (), s32[]{:S(2)}) async-start(), calls=%async_computation.3 | async-start | bytes 5898240 | tf_op jit(solution)/shard_map/reduce_scatter | solution.py:186
  9.2 29.0 %collective-permute-start = (f32[768,384]{1,0:T(8,128)S(1)}, f32[768,384]{1,0:T(8,128)S(1)}, u32[]{:S(2)}, u32[]{:S(2)}) collective-permute-start(f32[768,384]{1,0:T(8,128)S(1)} %get-tuple-element.34.refs_4_), channel_id=1, source_target_pairs={{0,16},{4,20},{8,24},{12,28},{16,0},{20,4},{24,8},{28,12},{1,17},{... | collective-permute-start | bytes 3538952 | tf_op jit(solution)/shard_map/ppermute | solution.py:99
  13.5 36.2 %collective-permute-start.5 = (f32[768,512]{1,0:T(8,128)}, f32[768,512]{1,0:T(8,128)}, u32[]{:S(2)}, u32[]{:S(2)}) collective-permute-start(f32[768,512]{1,0:T(8,128)} %split.7), channel_id=1, source_target_pairs={{0,8},{1,9},{2,10},{3,11},{4,12},{5,13},{6,14},{7,15},{8,0},{9,1},... | collective-permute-start | bytes 4718600 | tf_op jit(solution)/shard_map/ppermute | solution.py:136
  38.2 20.7 %collective-permute-start.1 = (f32[768,384]{1,0:T(8,128)S(1)}, f32[768,384]{1,0:T(8,128)}, u32[]{:S(2)}, u32[]{:S(2)}) collective-permute-start(f32[768,384]{1,0:T(8,128)S(1)} %collective-permute-done.refs_5_), channel_id=1, source_target_pairs={{0,4},{4,0},{8,12},{12,8},{16,20},{20,16},{24,28},{28,24},{1,5},{5... | collective-permute-start | bytes 3538952 | tf_op jit(solution)/shard_map/ppermute | solution.py:99
  38.2 22.8 %collective-permute-start.4 = (f32[768,384]{1,0:T(8,128)S(1)}, f32[768,384]{1,0:T(8,128)}, u32[]{:S(2)}, u32[]{:S(2)}) collective-permute-start(f32[768,384]{1,0:T(8,128)S(1)} %get-tuple-element.34.refs_4_), channel_id=1, source_target_pairs={{0,4},{4,0},{8,12},{12,8},{16,20},{20,16},{24,28},{28,24},{1,5},{5... | collective-permute-start | bytes 3538952 | tf_op jit(solution)/shard_map/ppermute | solution.py:99
  53.1 41.3 %collective-permute-start.6 = (f32[768,512]{1,0:T(8,128)S(1)}, f32[768,512]{1,0:T(8,128)S(1)}, u32[]{:S(2)}, u32[]{:S(2)}) collective-permute-start(f32[768,512]{1,0:T(8,128)S(1)} %get-tuple-element.64), channel_id=1, source_target_pairs={{1,0},{3,2},{4,5},{6,7},{9,8},{11,10},{12,13},{14,15},{17,16},{19,... | collective-permute-start | bytes 4718600 | tf_op jit(solution)/shard_map/ppermute | solution.py:136
  54.4 40.1 %collective-permute-start.7 = (f32[768,512]{1,0:T(8,128)S(1)}, f32[768,512]{1,0:T(8,128)S(1)}, u32[]{:S(2)}, u32[]{:S(2)}) collective-permute-start(f32[768,512]{1,0:T(8,128)S(1)} %get-tuple-element.63), channel_id=1, source_target_pairs={{0,2},{2,0},{5,7},{7,5},{8,10},{10,8},{13,15},{15,13},{16,18},{18,... | collective-permute-start | bytes 4718600 | tf_op jit(solution)/shard_map/ppermute | solution.py:136
  58.9 35.6 %collective-permute-start.3 = (f32[768,384]{1,0:T(8,128)S(1)}, f32[768,384]{1,0:T(8,128)S(1)}, u32[]{:S(2)}, u32[]{:S(2)}) collective-permute-start(f32[768,384]{1,0:T(8,128)S(1)} %collective-permute-done.refs_5_), channel_id=1, source_target_pairs={{0,8},{4,12},{8,0},{12,4},{16,24},{20,28},{24,16},{28,20},{1,9},{5... | collective-permute-start | bytes 3538952 | tf_op jit(solution)/shard_map/ppermute | solution.py:99
  60.5 48.6 %collective-permute-start.2 = (f32[768,384]{1,0:T(8,128)S(1)}, f32[768,384]{1,0:T(8,128)S(1)}, u32[]{:S(2)}, u32[]{:S(2)}) collective-permute-start(f32[768,384]{1,0:T(8,128)S(1)} %get-tuple-element.34.refs_4_), channel_id=1, source_target_pairs={{0,8},{4,12},{8,0},{12,4},{16,24},{20,28},{24,16},{28,20},{1,9},{5... | collective-permute-start | bytes 3538952 | tf_op jit(solution)/shard_map/ppermute | solution.py:99
  94.5 17.9 %collective-permute-start.9 = (f32[768,384]{1,0:T(8,128)S(1)}, f32[768,384]{1,0:T(8,128)S(1)}, u32[]{:S(2)}, u32[]{:S(2)}) collective-permute-start(f32[768,384]{1,0:T(8,128)S(1)} %collective-permute-done.3.refs_5_), channel_id=1, source_target_pairs={{0,4},{4,0},{8,12},{12,8},{16,20},{20,16},{24,28},{28,24},{1,5},{5... | collective-permute-start | bytes 3538952 | tf_op jit(solution)/shard_map/ppermute | solution.py:99
  109.0 35.9 %collective-permute-start.10 = (f32[768,384]{1,0:T(8,128)S(1)}, f32[768,384]{1,0:T(8,128)S(1)}, u32[]{:S(2)}, u32[]{:S(2)}) collective-permute-start(f32[768,384]{1,0:T(8,128)S(1)} %get-tuple-element.43.refs_4_), channel_id=1, source_target_pairs={{0,8},{4,20},{8,0},{12,28},{16,24},{20,4},{24,16},{28,12},{1,9},{5... | collective-permute-start | bytes 3538952 | tf_op jit(solution)/shard_map/ppermute | solution.py:99
  110.5 34.4 %collective-permute-start.11 = (f32[768,512]{1,0:T(8,128)}, f32[768,512]{1,0:T(8,128)}, u32[]{:S(2)}, u32[]{:S(2)}) collective-permute-start(f32[768,512]{1,0:T(8,128)} %get-tuple-element.38), channel_id=1, source_target_pairs={{1,2},{3,0},{4,7},{6,5},{9,10},{11,8},{12,15},{14,13},{17,18},{19,... | collective-permute-start | bytes 4718600 | tf_op jit(solution)/shard_map/ppermute | solution.py:136
  145.0 189.9 %reduce-scatter.6.cloned.1.call-start = ((), (), s32[]{:S(2)}) async-start(), calls=%async_computation.4 | async-start | bytes 5898240 | tf_op jit(solution)/shard_map/reduce_scatter | solution.py:186
  151.9 35.0 %collective-permute-start.14 = (f32[768,384]{1,0:T(8,128)S(1)}, f32[768,384]{1,0:T(8,128)S(1)}, u32[]{:S(2)}, u32[]{:S(2)}) collective-permute-start(f32[768,384]{1,0:T(8,128)S(1)} %collective-permute-done.10.refs_5_), channel_id=1, source_target_pairs={{0,16},{4,12},{8,24},{12,4},{16,0},{20,28},{24,8},{28,20},{1,17},{... | collective-permute-start | bytes 3538952 | tf_op jit(solution)/shard_map/ppermute | solution.py:99
  152.8 34.3 %collective-permute-start.13 = (f32[768,384]{1,0:T(8,128)S(1)}, f32[768,384]{1,0:T(8,128)S(1)}, u32[]{:S(2)}, u32[]{:S(2)}) collective-permute-start(f32[768,384]{1,0:T(8,128)S(1)} %get-tuple-element.43.refs_4_), channel_id=1, source_target_pairs={{0,16},{4,12},{8,24},{12,4},{16,0},{20,28},{24,8},{28,20},{1,17},{... | collective-permute-start | bytes 3538952 | tf_op jit(solution)/shard_map/ppermute | solution.py:99
  188.7 35.5 %collective-permute-start.18 = (f32[768,256]{1,0:T(8,128)S(1)}, f32[768,256]{1,0:T(8,128)S(1)}, u32[]{:S(2)}, u32[]{:S(2)}) collective-permute-start(f32[768,256]{1,0:T(8,128)S(1)} %slice.45.refs_4_), channel_id=1, source_target_pairs={{0,8},{4,20},{8,0},{12,28},{16,24},{20,4},{24,16},{28,12},{1,9},{5... | collective-permute-start | bytes 2359304 | tf_op jit(solution)/shard_map/ppermute | solution.py:99
  224.2 162.1 %reduce-scatter.8.cloned.1.call-start = ((), (), s32[]{:S(2)}) async-start(), calls=%async_computation.5 | async-start | bytes 3932160 | tf_op jit(solution)/shard_map/reduce_scatter | solution.py:186
  226.8 22.6 %collective-permute-start.21 = (f32[768,256]{1,0:T(8,128)S(1)}, f32[768,256]{1,0:T(8,128)S(1)}, u32[]{:S(2)}, u32[]{:S(2)}) collective-permute-start(f32[768,256]{1,0:T(8,128)S(1)} %collective-permute-done.18.refs_5_), channel_id=1, source_target_pairs={{0,16},{4,12},{8,24},{12,4},{16,0},{20,28},{24,8},{28,20},{1,17},{... | collective-permute-start | bytes 2359304 | tf_op jit(solution)/shard_map/ppermute | solution.py:99
  227.7 21.7 %collective-permute-start.20 = (f32[768,256]{1,0:T(8,128)S(1)}, f32[768,256]{1,0:T(8,128)S(1)}, u32[]{:S(2)}, u32[]{:S(2)}) collective-permute-start(f32[768,256]{1,0:T(8,128)S(1)} %slice.45.refs_4_), channel_id=1, source_target_pairs={{0,16},{4,12},{8,24},{12,4},{16,0},{20,28},{24,8},{28,20},{1,17},{... | collective-permute-start | bytes 2359304 | tf_op jit(solution)/shard_map/ppermute | solution.py:99
  282.1 24.3 %collective-permute-start.25 = (f32[768,512]{1,0:T(8,128)}, f32[768,512]{1,0:T(8,128)S(1)}, u32[]{:S(2)}, u32[]{:S(2)}) collective-permute-start(f32[768,512]{1,0:T(8,128)} %get-tuple-element.70), channel_id=1, source_target_pairs={{0,24},{2,18},{5,17},{7,27},{8,0},{10,10},{13,9},{15,3},{16,28},{1... | collective-permute-start | bytes 4718600 | tf_op jit(solution)/shard_map/ppermute | solution.py:136
  286.7 37.4 %collective-permute-start.26 = (f32[768,512]{1,0:T(8,128)}, f32[768,512]{1,0:T(8,128)S(1)}, u32[]{:S(2)}, u32[]{:S(2)}) collective-permute-start(f32[768,512]{1,0:T(8,128)} %get-tuple-element.69), channel_id=1, source_target_pairs={{0,16},{2,10},{5,25},{7,3},{8,24},{10,2},{13,17},{15,11},{16,20},{... | collective-permute-start | bytes 4718600 | tf_op jit(solution)/shard_map/ppermute | solution.py:136
  289.0 35.0 %collective-permute-start.27 = (f32[768,512]{1,0:T(8,128)}, f32[768,512]{1,0:T(8,128)}, u32[]{:S(2)}, u32[]{:S(2)}) collective-permute-start(f32[768,512]{1,0:T(8,128)} %get-tuple-element.68), channel_id=1, source_target_pairs={{0,8},{2,2},{5,1},{7,11},{8,16},{10,26},{13,25},{15,19},{16,12},{1... | collective-permute-start | bytes 4718600 | tf_op jit(solution)/shard_map/ppermute | solution.py:136
  292.8 32.4 %collective-permute-start.28 = (f32[768,512]{1,0:T(8,128)}, f32[768,512]{1,0:T(8,128)}, u32[]{:S(2)}, u32[]{:S(2)}) collective-permute-start(f32[768,512]{1,0:T(8,128)} %get-tuple-element.67), channel_id=1, source_target_pairs={{0,0},{2,26},{5,9},{7,19},{8,8},{10,18},{13,1},{15,27},{16,4},{18,... | collective-permute-start | bytes 4718600 | tf_op jit(solution)/shard_map/ppermute | solution.py:136
  351.1 14.8 %collective-permute-start.35 = (f32[128,384]{1,0:T(8,128)S(1)}, f32[128,384]{1,0:T(8,128)S(1)}, u32[]{:S(2)}, u32[]{:S(2)}) collective-permute-start(f32[128,384]{1,0:T(8,128)S(1)} %get-tuple-element.73), channel_id=1, source_target_pairs={{0,16},{4,20},{8,24},{12,28},{16,0},{20,4},{24,8},{28,12},{1,17},{... | collective-permute-start | bytes 589832 | tf_op jit(solution)/shard_map/ppermute | solution.py:114
  (42 other events, 302.6 us)
Sparse Core Ops, SparseCore 0:
  145.1 89.2 reduce-scatter.3
  236.7 85.7 reduce-scatter.5
  325.4 60.7 reduce-scatter.7
